TPU v7x, 128 devices: a whole 4x4x4 slice. The times are simulated.
128 devices in a mesh: row: 16 (over x, z), col: 8 (over y, core).
Axes of the slice: x: 4, y: 4, z: 4, core: 2. Of those that a mesh axis runs over, the one named last changes fastest.
Arguments:
- amplitudes: bfloat16 [64, 32, 512, 512], P('row', None, None, 'col'), may hold values from -6 to 6
- vvvv_ints: bfloat16 [512, 512, 8, 512], P('row', 'col'), may hold values from -0.015625 to 0.015625
- ovov_ints: bfloat16 [32, 8, 64, 512], P(None, None, 'row'), may hold values from -0.046875 to 0.046875
- occ_energy: float32 [64], replicated, may hold values from -2 to -0.5
- vir_energy: float32 [512], replicated, may hold values from 0.5 to 3
- occ_irrep: int32 [64], replicated, may hold values from 0 to 7, as said below
- vir_irrep: int32 [512], replicated, may hold values from 0 to 7, as said below
- i_orbitals: int32 [32], replicated, may hold values from 0 to 63, as said below
- j_orbitals: int32 [32], replicated, may hold values from 0 to 63, as said below
- a_orbitals: int32 [8], replicated, may hold values from 0 to 511, as said below
Outputs:
- update: float32 [32, 32, 8, 512], P('row', None, None, 'col')
Inputs may be any that keep to these rules, and one draw needn't show every extreme that they name: `occ_irrep`: the orbitals form 8 contiguous runs of 8 each, one run for each label. `vir_irrep`: the orbitals form 8 contiguous runs of 64 each, one run for each label. `i_orbitals`: distinct occupied orbital numbers. `j_orbitals`: distinct occupied orbital numbers. `a_orbitals`: distinct virtual orbital numbers.
All inputs are finite; a program needn't handle non-finite values.
Results may differ from a plain program's by a relative error of at most 0.0003.
Values may be sent and summed in bfloat16 or wider, within the bound.
No kernel may reach another device: no remote copies, remote signals or barrier semaphores. Data moves between devices by JAX's collectives and lax.ppermute only.
A program may use at most 192 MiB of HBM per device.

v0:
```python
import jax
import jax.numpy as jnp
from jax import lax
from jax.sharding import PartitionSpec as P


def shards(
    amplitudes,
    vvvv_ints,
    ovov_ints,
    occ_energy,
    vir_energy,
    occ_irrep,
    vir_irrep,
    i_orbitals,
    j_orbitals,
    a_orbitals,
):
    n_rows = lax.axis_size("row")
    n_cols = lax.axis_size("col")
    row_index = lax.axis_index("row")
    col_index = lax.axis_index("col")
    occ_slab = i_orbitals.shape[0]
    occ_pair = amplitudes.shape[1]
    virtuals = amplitudes.shape[2]
    vir_slab = vvvv_ints.shape[2]
    c_local = vvvv_ints.shape[0]
    d_local = vvvv_ints.shape[1]
    i_local = occ_slab // n_rows
    by_first = lax.all_to_all(amplitudes, "row", split_axis=2, concat_axis=0, tiled=True)
    slab_rows = jnp.take(by_first, i_orbitals, axis=0).reshape(
        occ_slab * occ_pair, c_local * d_local
    )
    ints_flat = vvvv_ints.reshape(c_local * d_local, vir_slab * virtuals)
    ladder = jnp.dot(slab_rows, ints_flat, preferred_element_type=jnp.float32)
    ladder = ladder.reshape(occ_slab, occ_pair, vir_slab, virtuals)
    cycle_part = jnp.einsum(
        "iakc,kjcb->ijab", ovov_ints, amplitudes, preferred_element_type=jnp.float32
    )
    b_first = col_index * d_local
    current = lax.dynamic_slice_in_dim(ladder, b_first, d_local, 3)
    ladder = lax.dynamic_update_slice_in_dim(ladder, current + cycle_part, b_first, 3)
    arranged = ladder.reshape(n_rows, i_local, occ_pair, vir_slab, n_cols, d_local)
    arranged = arranged.transpose(0, 4, 1, 5, 2, 3).reshape(
        n_rows * n_cols * i_local * d_local, occ_pair * vir_slab
    )
    summed = lax.psum_scatter(arranged, ("row", "col"), scatter_dimension=0, tiled=True)
    block_sum = summed.reshape(i_local, d_local, occ_pair, vir_slab).transpose(0, 2, 3, 1)
    mine_i = lax.dynamic_slice_in_dim(i_orbitals, row_index * i_local, i_local)
    occ_i_energy = jnp.take(occ_energy, mine_i)
    occ_j_energy = jnp.take(occ_energy, j_orbitals)
    vir_a_energy = jnp.take(vir_energy, a_orbitals)
    vir_b_energy = lax.dynamic_slice_in_dim(vir_energy, col_index * d_local, d_local)
    denominator = (
        occ_i_energy[:, None, None, None]
        + occ_j_energy[None, :, None, None]
        - vir_a_energy[None, None, :, None]
        - vir_b_energy[None, None, None, :]
    )
    sym_i = jnp.take(occ_irrep, mine_i)
    sym_j = jnp.take(occ_irrep, j_orbitals)
    sym_a = jnp.take(vir_irrep, a_orbitals)
    sym_b = lax.dynamic_slice_in_dim(vir_irrep, col_index * d_local, d_local)
    product_irrep = jnp.bitwise_xor(
        jnp.bitwise_xor(sym_i[:, None, None, None], sym_j[None, :, None, None]),
        jnp.bitwise_xor(sym_a[None, None, :, None], sym_b[None, None, None, :]),
    )
    allowed = product_irrep == 0
    return jnp.where(allowed, block_sum / denominator, jnp.zeros_like(block_sum))


def solution(mesh):
    return jax.shard_map(
        shards,
        mesh=mesh,
        in_specs=(
            P("row", None, None, "col"),
            P("row", "col", None, None),
            P(None, None, "row", None),
            P(),
            P(),
            P(),
            P(),
            P(),
            P(),
            P(),
        ),
        out_specs=P("row", None, None, "col"),
        check_vma=False,
    )
```

profile of v0, /device:TPU:1, one launch (start us, length us, event | category | flops | bytes accessed | tf_op | source)
XLA Modules:
  0.0 1134.8 jit_solution(11434348797441830065)
XLA Ops:
  6.5 0.0 copy-start
  6.5 24.0 %copy.23 = bf16[4,32,512,64]{3,1,0,2:T(8,128)(2,1)} copy(bf16[4,32,512,64]{2,3,1,0:T(8,128)(2,1)} %param.10) | data formatting | bytes 16777216 | tf_op args[0]
  30.5 19.6 %reshape.263 = bf16[16,2,131072]{2,1,0:T(2,128)(2,1)} reshape(bf16[512,4,32,64]{3,2,1,0:T(8,128)(2,1)} %bitcast.48) | data formatting | bytes 16777216
  50.1 8.5 all-to-all-start
  58.6 0.0 reduce-scatter.2.cloned.1.call-start
  58.7 16.6 %copy.38 = bf16[256,8,8,512]{3,1,2,0:T(8,128)(2,1)} copy(bf16[256,8,8,512]{3,2,1,0:T(8,128)(2,1)} %bitcast.52) | data formatting | bytes 33554432
  75.3 22.7 %copy.26 = bf16[4096,2048]{1,0:T(8,128)(2,1)} copy(bf16[4096,2048]{0,1:T(8,128)(2,1)} %bitcast.50) | data formatting | bytes 33554432 | tf_op jit(solution)/shard_map/dot_general | solution.py:35
  98.0 0.0 copy-done.8
  98.0 9.5 fusion.4
  107.6 97.2 %all-to-all-done = bf16[16,2,131072]{2,1,0:T(2,128)(2,1)} async-done(((bf16[16,2,131072]{2,1,0:T(2,128)(2,1)}), bf16[16,2,131072]{2,1,0:T(2,128)(2,1)}, u32[]{:S(2)}, u32[]{:S(2)}) %all-to-all-start) | async-done | bytes 8388640 | tf_op jit(solution)/shard_map/all_to_all | solution.py:30
  204.8 19.3 %reshape.264 = bf16[512,4,32,64]{3,2,1,0:T(8,128)(2,1)} reshape(bf16[16,2,131072]{2,1,0:T(2,128)(2,1)} %all-to-all-done) | data formatting | bytes 16777216
  224.0 18.5 %copy.25 = bf16[16,4,32,32,64]{4,3,2,1,0:T(8,128)(2,1)} copy(bf16[16,4,32,32,64]{4,2,1,3,0:T(8,128)(2,1)} %bitcast.49) | data formatting | bytes 16777216 | tf_op jit(solution)/shard_map/all_to_all | solution.py:30
  242.5 10.8 gather_fusion.3
  253.3 7.5 broadcast_select_fusion
  260.8 12.3 %reshape.257 = bf16[32,32,2048,1]{2,1,0,3:T(8,128)(2,1)} reshape(bf16[32,32,32,64]{3,2,1,0:T(8,128)(2,1)} %broadcast_select_fusion) | data formatting | bytes 8388608 | tf_op jit(solution)/shard_map/jit(_take)/select_n | solution.py:31
  273.1 21.8 %fusion.2 = f32[32,32,8,512]{3,1,2,0:T(8,128)S(1)} fusion(bf16[8,512,2048,1]{2,1,0,3:T(8,128)(2,1)} %bitcast.53, bf16[32,32,2048,1]{2,1,0,3:T(8,128)(2,1)} %reshape.257), kind=kOutput, calls=%fused_computation.12 | convolution fusion | flops 17179869184 | bytes 37748736 | tf_op jit(solution)/shard_map/dot_general | solution.py:35
  294.9 0.0 copy-start.4
  294.9 5.7 copy-done.4
  300.6 4.6 bitcast_add_fusion
  305.2 45.6 %dynamic_update_slice.3 = f32[32,32,8,512]{3,1,2,0:T(8,128)} dynamic-update-slice(f32[32,32,8,512]{3,1,2,0:T(8,128)} %copy-done.4, f32[32,32,8,64]{3,1,2,0:T(8,128)} %bitcast_add_fusion, s32[]{:T(128)} %constant.84.clone.1, s32[]{:T(128)} %constant.84.clone.1, s32[]{:T(128)} %constant.84.clone.1, s32[]{:T(128)S(6)} %select_n.98) | dynamic-update-slice | bytes 4194308 | tf_op jit(solution)/shard_map/dynamic_update_slice | solution.py:42
  350.8 24.6 %reshape.191 = f32[16,2,32,8,8,64]{5,4,2,3,1,0:T(8,128)} reshape(f32[32,32,8,512]{3,1,2,0:T(8,128)} %dynamic_update_slice.3) | data formatting | bytes 33554432 | tf_op jit(solution)/shard_map/reshape | solution.py:43
  375.5 54.8 %copy.49 = f32[16,2,32,8,8,64]{5,1,4,0,3,2:T(2,128)} copy(f32[16,2,32,8,8,64]{5,4,2,3,1,0:T(8,128)} %reshape.191) | data formatting | bytes 33554432 | tf_op jit(solution)/shard_map/reshape | solution.py:43
  430.2 34.2 %reshape.192 = f32[16384,256]{0,1:T(8,128)} reshape(f32[16,8,2,64,32,8]{3,2,1,0,5,4:T(2,128)} %bitcast.47) | data formatting | bytes 33554432 | tf_op jit(solution)/shard_map/reshape | solution.py:44
  464.5 0.0 copy-start.10
  464.5 0.0 copy-start.3
  464.5 0.0 reduce-scatter.2.cloned.1.call-update
  464.5 0.6 copy-done.7
  465.1 0.1 compare_select_fusion.4
  465.2 0.6 gather_fusion.4
  465.9 0.7 gather_fusion.5
  466.6 0.6 gather_fusion
  467.2 0.7 gather_fusion.1
  467.9 0.1 dynamic_slice.13
  468.0 0.0 copy-done.10
  468.0 0.6 gather_fusion.2
  468.7 0.0 copy-done.3
  468.7 0.7 gather_fusion.6
  469.3 0.1 dynamic_slice.15
  469.4 0.1 broadcast_select_fusion.3
  469.5 0.1 broadcast_select_fusion.6
  469.6 0.1 broadcast_xor_fusion.1
  469.7 0.1 broadcast_add_fusion
  469.7 0.1 broadcast_xor_fusion
  469.8 0.1 broadcast_subtract_fusion
  469.9 655.9 %reduce-scatter.2.cloned.1.call-done = f32[128,256]{0,1:T(8,128)} async-done(((f32[16384,256]{0,1:T(8,128)}), f32[128,256]{0,1:T(8,128)}) %reduce-scatter.2.cloned.1.call-update) | async-done | bytes 131088 | tf_op jit(solution)/shard_map/reduce_scatter | solution.py:47
  1125.8 1.1 reshape.193
  1126.9 0.4 compare_select_fusion
  1127.3 0.7 copy.31
  (25 shorter events, 0.1 us)
Async XLA Ops:
  6.5 458.7 %copy-start = (f32[64]{0:T(128)S(1)}, f32[64]{0:T(128)}, u32[]{:S(2)}) copy-start(f32[64]{0:T(128)} %param.13) | copy-start | bytes 772
  50.1 154.6 %all-to-all-start = ((bf16[16,2,131072]{2,1,0:T(2,128)(2,1)}), bf16[16,2,131072]{2,1,0:T(2,128)(2,1)}, u32[]{:S(2)}, u32[]{:S(2)}) async-start(bf16[16,2,131072]{2,1,0:T(2,128)(2,1)} %reshape.263), calls=%async_computation | async-start | bytes 16777216 | tf_op jit(solution)/shard_map/all_to_all | solution.py:30
  58.6 1067.2 %reduce-scatter.2.cloned.1.call-start = ((), (), s32[]{:S(2)}) async-start(), calls=%async_computation.2 | async-start | bytes 16908288 | tf_op jit(solution)/shard_map/reduce_scatter | solution.py:47
  75.3 22.7 %copy-start.6 = (s32[32]{0:T(128)S(1)}, s32[32]{0:T(128)}, u32[]{:S(2)}) copy-start(s32[32]{0:T(128)} %param.17) | copy-start | bytes 388
  75.3 22.7 %copy-start.8 = (bf16[32,8,4,512]{3,2,1,0:T(4,128)(2,1)S(1)}, bf16[32,8,4,512]{3,2,1,0:T(4,128)(2,1)}, u32[]{:S(2)}) copy-start(bf16[32,8,4,512]{3,2,1,0:T(4,128)(2,1)} %param.12) | copy-start | bytes 3145732
  273.1 27.5 %copy-start.5 = (f32[32,64,32,8]{1,2,3,0:T(8,128)S(1)}, f32[32,64,32,8]{1,2,3,0:T(8,128)}, u32[]{:S(2)}) copy-start(f32[32,64,32,8]{1,2,3,0:T(8,128)} %fusion.4) | copy-start | bytes 6291460
  294.9 5.7 copy-start.4
  464.5 0.7 copy-start.7
  464.5 1.4 copy-start.9
  464.5 2.1 copy-start.1
  464.5 3.4 copy-start.2
  464.5 3.5 copy-start.10
  464.5 4.2 copy-start.3
Sparse Core Ops, SparseCore 0:
  464.6 661.0 reduce-scatter.1
where the time goes:
time: 1150 us; the launch traced here: 1130 us
  waiting for transfers between devices  753 us (65%)
  local copies, waits for them, and re-layouts  315 us (27%)
  matrix products  31.3 us (3%)
  between operations  13.5 us (1%)
  other arithmetic  13 us (1%)
    reduce_scatter x1, waiting for transfers between devices, shards(): lax.psum_scatter(arranged, ('row', 'col'), scatter_dimension=0, tiled=True)  656 us
    all_to_all x1, waiting for transfers between devices, shards(): lax.all_to_all(amplitudes, 'row', split_axis=2, concat_axis=0, tiled=True)  97.2 us
    unnamed x26, local copies, waits for them, and re-layouts  85.8 us
    reshape x2, local copies, waits for them, and re-layouts, shards(): ladder.reshape(n_rows, i_local, occ_pair, vir_slab, n_cols, d_local)  79.4 us
    dynamic_update_slice x1, local copies, waits for them, and re-layouts, shards(): lax.dynamic_update_slice_in_dim(ladder, current + cycle_part, b_first, 3)  45.6 us
    reshape x1, local copies, waits for them, and re-layouts, shards(): arranged.transpose(0, 4, 1, 5, 2, 3)  34.2 us
  transfers between devices with their start and end apart: 2, of which 2 were waited for; matrix products, arithmetic and copies ran while one was open for 5% of the time, Pallas kernels for 0%

commit v1 on v0

v1 whole, which is shorter than its diff:
```python
import functools

import jax
import jax.numpy as jnp
import numpy as np
from jax import lax
from jax.experimental import pallas as pl
from jax.experimental.pallas import tpu as pltpu
from jax.sharding import PartitionSpec as P

F32 = jnp.float32
BF16 = jnp.bfloat16
VMEM = 48 * 1024 * 1024

NO, NV, OI, OJ, SA = 64, 512, 32, 32, 8
ROWS, COLS, RUN = 16, 8, 64
PIECES = 4
DP = 64 // PIECES
QP = DP // 4
KP = DP * 32


def params(n=1):
    return pltpu.CompilerParams(
        dimension_semantics=("arbitrary",) * n, vmem_limit_bytes=VMEM
    )


def cost(flops, nbytes):
    return pl.CostEstimate(flops=flops, bytes_accessed=nbytes, transcendentals=0)


def one_hot_swap(m, n):
    out = np.zeros((m * n, m * n), np.float32)
    for a in range(m):
        for b in range(n):
            out[b * m + a, a * n + b] = 1
    return out.astype(jnp.bfloat16)


def lane_swap():
    out = np.zeros((4, 4, 32, 4, 4, 32), np.float32)
    for e in range(4):
        for z in range(4):
            for c in range(32):
                out[e, z, c, z, e, c] = 1
    return out.reshape(512, 512).astype(jnp.bfloat16)


def pack_kernel(x_ref, swap_ref, lanes_ref, out_ref, mid_ref):
    for jh in range(2):
        for dh in range(DP // 16):
            x = x_ref[0, 16 * jh : 16 * jh + 16, 16 * dh : 16 * dh + 16, :].reshape(256, NV)
            y = jnp.dot(swap_ref[...], x, preferred_element_type=F32).astype(BF16)
            mid_ref[16 * dh : 16 * dh + 16, 16 * jh : 16 * jh + 16, :] = y.reshape(16, 16, NV)
    for q in range(QP):
        for x in range(4):
            z = jnp.concatenate(
                [mid_ref[4 * q + e, :, 128 * x : 128 * x + 128] for e in range(4)], axis=1
            )
            w = jnp.dot(z, lanes_ref[...], preferred_element_type=F32).astype(BF16)
            for zz in range(4):
                out_ref[4 * x + zz, q, 0, :, :] = w[:, 128 * zz : 128 * zz + 128]


def pack(amp_t, piece):
    return pl.pallas_call(
        pack_kernel,
        grid=(4,),
        in_specs=[
            pl.BlockSpec((1, OJ, DP, NV), lambda k: (k, 0, piece, 0)),
            pl.BlockSpec((256, 256), lambda k: (0, 0)),
            pl.BlockSpec((512, 512), lambda k: (0, 0)),
        ],
        out_specs=pl.BlockSpec((ROWS, QP, 1, OJ, 128), lambda k: (0, 0, k, 0, 0)),
        out_shape=jax.ShapeDtypeStruct((ROWS, QP, 4, OJ, 128), BF16),
        scratch_shapes=[pltpu.VMEM((DP, OJ, NV), BF16)],
        compiler_params=params(),
        cost_estimate=cost(6_400_000_000 // PIECES, 2 * 8 * 2**20 // PIECES),
        name="pack",
    )(amp_t, one_hot_swap(16, 16), lane_swap())


def ints_kernel(gtab_ref, v_ref, swap_ref, out_ref):
    halves = []
    for ch in range(2):
        x = v_ref[16 * ch : 16 * ch + 16, :, :].reshape(256, NV)
        y = jnp.dot(swap_ref[...], x, preferred_element_type=F32)
        halves.append(y.reshape(2, SA, 16, NV))
    for a in range(SA):
        off = 64 * (a % 2)
        for t in range(4):
            tile = jnp.concatenate(
                [halves[ch][d, a, :, 128 * t : 128 * t + 128] for d in range(2) for ch in range(2)],
                axis=0,
            )
            turned = pltpu.roll(tile, 64, 1)
            for e in range(2):
                src = tile if e == a % 2 else turned
                g = gtab_ref[a, 2 * t + e]
                out_ref[0, g, :, 64 * a : 64 * a + 64] = src[:, off : off + 64].astype(BF16)


def arrange_ints(gtab, ints):
    steps = 32 // PIECES
    return pl.pallas_call(
        ints_kernel,
        grid_spec=pltpu.PrefetchScalarGridSpec(
            num_scalar_prefetch=1,
            grid=(32,),
            in_specs=[
                pl.BlockSpec((32, 16, NV), lambda s, *_: (0, s, 0)),
                pl.BlockSpec((256, 256), lambda s, *_: (0, 0)),
            ],
            out_specs=pl.BlockSpec(
                (1, 8, 64, NV), lambda s, *_: (s // steps, 0, s % steps, 0)
            ),
        ),
        out_shape=jax.ShapeDtypeStruct((PIECES, 8, KP, SA * RUN), BF16),
        compiler_params=params(),
        cost_estimate=cost(4_300_000_000, 32 * 2**20),
        name="arrange_ints",
    )(gtab, ints, one_hot_swap(16, 16))


def two_terms(x):
    hi = x.astype(BF16)
    return hi, (x - hi.astype(F32)).astype(BF16)


def gather_rows(iorb_ref, r_ref, pick_ref, rows_ref):
    for blk in range(8):
        slabs = []
        for i in range(4):
            k = iorb_ref[4 * blk + i]
            slabs.append(
                jnp.concatenate([r_ref[k // 4, q, k % 4, :, :] for q in range(QP)], axis=1)
            )
        x = jnp.concatenate(slabs, axis=0)
        y = jnp.dot(pick_ref[blk], x, preferred_element_type=F32).astype(BF16)
        rows_ref[:, 32 * blk : 32 * blk + 32, :] = y.reshape(8, 32, KP)


def ladder_kernel(first, iorb_ref, r_ref, pick_ref, ints_ref, *rest):
    if first:
        out_ref, rows_ref = rest
    else:
        acc_ref, out_ref, rows_ref = rest
    g = pl.program_id(0)

    @pl.when(g == 0)
    def _():
        gather_rows(iorb_ref, r_ref, pick_ref, rows_ref)

    got = jnp.dot(rows_ref[g], ints_ref[0, 0], preferred_element_type=F32)
    out_ref[0] = got if first else got + acc_ref[0]


def last_kernel(iorb_ref, core_ref, r_ref, pick_ref, ints_ref, acc_ref, drop_ref, cycle_ref,
                keep_ref, send_ref, rows_ref, sum_ref):
    g = pl.program_id(0)

    @pl.when(g == 0)
    def _():
        gather_rows(iorb_ref, r_ref, pick_ref, rows_ref)

    sum_ref[g] = acc_ref[0] + jnp.dot(rows_ref[g], ints_ref[0, 0], preferred_element_type=F32)

    @pl.when(g == 7)
    def _():
        core = core_ref[0]
        for blk in range(8):
            x = sum_ref[:, 32 * blk : 32 * blk + 32, :].reshape(256, SA * RUN)
            hi, lo = two_terms(x)
            y = jnp.dot(drop_ref[blk], hi, preferred_element_type=F32)
            y = y + jnp.dot(drop_ref[blk], lo, preferred_element_type=F32)
            for i in range(4):
                p = 4 * blk + i
                got = y[32 * i : 32 * i + 32, :] + cycle_ref[p]

                @pl.when(core == p % 2)
                def _():
                    keep_ref[p // 2] = got

                @pl.when(core != p % 2)
                def _():
                    send_ref[p // 2] = got


def ladder(piece, iorb, core, arrived, pick, ints, acc, drop, cyc):
    first, last = piece == 0, piece == PIECES - 1
    n_scalar = 2 if last else 1
    whole = lambda *dims: pl.BlockSpec(dims, lambda g, *_: (0,) * len(dims))
    acc_spec = pl.BlockSpec((1, 256, 512), lambda g, *_: (g, 0, 0))
    in_specs = [
        whole(ROWS, QP, 4, OJ, 128),
        whole(8, 256, 128),
        pl.BlockSpec((1, 1, KP, 512), lambda g, *_: (piece, g, 0, 0)),
    ]
    args = [arrived, pick, ints]
    if not first:
        in_specs.append(acc_spec)
        args.append(acc)
    scratch = [pltpu.VMEM((8, 256, KP), BF16)]
    if last:
        in_specs += [whole(8, 128, 256), whole(OI, OJ, 512)]
        args += [drop, cyc]
        out_specs = [whole(16, OJ, 512)] * 2
        out_shape = [jax.ShapeDtypeStruct((16, OJ, 512), F32)] * 2
        scratch.append(pltpu.VMEM((8, 256, 512), F32))
        body, scalars = last_kernel, [iorb, core]
    else:
        out_specs = acc_spec
        out_shape = jax.ShapeDtypeStruct((8, 256, 512), F32)
        body, scalars = functools.partial(ladder_kernel, first), [iorb]
    return pl.pallas_call(
        body,
        grid_spec=pltpu.PrefetchScalarGridSpec(
            num_scalar_prefetch=n_scalar,
            grid=(8,),
            in_specs=in_specs,
            out_specs=out_specs,
            scratch_shapes=scratch,
        ),
        out_shape=out_shape,
        compiler_params=params(),
        cost_estimate=cost(5_400_000_000 // PIECES, 14 * 2**20),
        name="ladder",
    )(*scalars, *args)


def by_run_kernel(ltab_ref, x_ref, spread_ref, out_ref):
    hi, lo = two_terms(jnp.sum(x_ref[...], axis=0))
    y = jnp.dot(spread_ref[...], hi, preferred_element_type=F32)
    y = y + jnp.dot(spread_ref[...], lo, preferred_element_type=F32)
    for a in range(SA):
        for t in range(8):
            out_ref[ltab_ref[a, t], :, 64 * a : 64 * a + 64] = y[8 * t : 8 * t + 8, 64 * a : 64 * a + 64]


def by_run(ltab, x, spread):
    return pl.pallas_call(
        by_run_kernel,
        grid_spec=pltpu.PrefetchScalarGridSpec(
            num_scalar_prefetch=1,
            grid=(1,),
            in_specs=[
                pl.BlockSpec((ROWS, OJ, 512), lambda s, *_: (0, 0, 0)),
                pl.BlockSpec((64, OJ), lambda s, *_: (0, 0)),
            ],
            out_specs=pl.BlockSpec((8, 8, 512), lambda s, *_: (0, 0, 0)),
        ),
        out_shape=jax.ShapeDtypeStruct((8, 8, 512), F32),
        compiler_params=params(),
        name="by_run",
    )(ltab, x, spread)


def finish_kernel(slot_ref, irr_ref, energy_ref, x_ref, va_ref, vb_ref, sa_ref, sb_ref, out_ref, tile_ref):
    for h in range(2):
        v = x_ref[h]
        for y in range(1, 4):
            v = v + x_ref[2 * y + h]
        for a in range(SA):
            tile_ref[h, :, a, :] = v[:, 64 * a : 64 * a + 64]
    sym_ab = jnp.bitwise_xor(sa_ref[...], sb_ref[...])
    for h in range(2):
        for j in range(OJ):
            got = tile_ref[h, slot_ref[j]]
            den = energy_ref[h, j] - va_ref[...] - vb_ref[...]
            ok = jnp.bitwise_xor(sym_ab, irr_ref[h, j]) == 0
            out_ref[h, j] = jnp.where(ok, got / den, jnp.zeros_like(got))


def finish(slot, irr, energy, x, va, vb, sa, sb):
    full = lambda *dims: pl.BlockSpec(dims, lambda s, *_: (0,) * len(dims))
    return pl.pallas_call(
        finish_kernel,
        grid_spec=pltpu.PrefetchScalarGridSpec(
            num_scalar_prefetch=3,
            grid=(1,),
            in_specs=[full(8, 8, 512), full(8, 64), full(8, 64), full(8, 64), full(8, 64)],
            out_specs=full(2, OJ, SA, RUN),
            scratch_shapes=[pltpu.VMEM((2, 8, SA, RUN), F32)],
        ),
        out_shape=jax.ShapeDtypeStruct((2, OJ, SA, RUN), F32),
        compiler_params=params(),
        name="finish",
    )(slot, irr, energy, x, va, vb, sa, sb)


def shards(
    amplitudes,
    vvvv_ints,
    ovov_ints,
    occ_energy,
    vir_energy,
    occ_irrep,
    vir_irrep,
    i_orbitals,
    j_orbitals,
    a_orbitals,
):
    row = lax.axis_index("row")
    col = lax.axis_index("col")
    core = lax.rem(col, 2)
    labels = jnp.arange(8, dtype=jnp.int32)

    amp_t = amplitudes.transpose(0, 1, 3, 2)
    arrived = []
    for piece in range(PIECES):
        sent = pack(amp_t, piece)
        arrived.append(lax.all_to_all(sent, "row", split_axis=0, concat_axis=0, tiled=True))

    sym_i = jnp.take(occ_irrep, i_orbitals)
    sym_j = jnp.take(occ_irrep, j_orbitals)
    sym_a = jnp.take(vir_irrep, a_orbitals)
    run_label = vir_irrep.reshape(8, RUN)[:, 0]
    slot = j_orbitals % 8
    gtab = jnp.bitwise_xor(sym_a[:, None], run_label[None, :])
    g_ij = jnp.bitwise_xor(sym_i[:, None], sym_j[None, :])
    hit = (g_ij[:, :, None, None] == labels[:, None]) & (slot[:, None, None] == labels)
    hit = hit.reshape(8, 4, OJ, 8, 8)
    same = (jnp.arange(4)[:, None] == jnp.arange(4)).reshape(1, 4, 1, 1, 4, 1)
    drop = (hit[:, :, :, :, None, :] & same).reshape(8, 128, 256).astype(BF16)
    pick = drop.transpose(0, 2, 1)

    ints = arrange_ints(gtab, vvvv_ints.reshape(32, 512, NV))

    cyc = jnp.einsum("iakc,kjcb->ijab", ovov_ints, amplitudes, preferred_element_type=F32)
    mine_label = lax.dynamic_index_in_dim(run_label, col, keepdims=False)
    wanted = jnp.bitwise_xor(g_ij[:, :, None], sym_a) == mine_label
    cyc = jnp.where(wanted[..., None], cyc, 0.0).reshape(OI, OJ, SA * RUN)

    acc = None
    core1 = core.reshape(1)
    for piece in range(PIECES):
        acc = ladder(piece, i_orbitals, core1, arrived[piece], pick, ints, acc, drop, cyc)
    keep, send = acc

    got = lax.ppermute(send, "col", [(q, q ^ 1) for q in range(COLS)])
    both = lax.all_to_all(keep + got, "row", split_axis=0, concat_axis=0, tiled=True)

    mine_i = lax.dynamic_slice_in_dim(i_orbitals, 2 * row, 2)
    sym_mine = jnp.take(occ_irrep, mine_i)
    label_at = jnp.bitwise_xor(
        jnp.bitwise_xor(lax.dynamic_index_in_dim(sym_mine, core, keepdims=False), sym_a)[:, None],
        labels[None, :],
    )
    ltab = jnp.sum(jnp.where(label_at[..., None] == run_label, labels, 0), axis=-1).astype(jnp.int32)
    spread = (
        (sym_j[None, None, :] == labels[:, None, None]) & (slot[None, None, :] == labels[None, :, None])
    ).reshape(64, OJ).astype(BF16)
    parts = lax.all_to_all(by_run(ltab, both, spread), "col", split_axis=0, concat_axis=0, tiled=True)

    energy = jnp.take(occ_energy, mine_i)[:, None] + jnp.take(occ_energy, j_orbitals)[None, :]
    irr = jnp.bitwise_xor(sym_mine[:, None], sym_j[None, :])
    wide = lambda x: jnp.broadcast_to(x, (SA, RUN))
    va = wide(jnp.take(vir_energy, a_orbitals)[:, None])
    vb = wide(lax.dynamic_slice_in_dim(vir_energy, col * RUN, RUN)[None, :])
    sa = wide(sym_a[:, None])
    sb = wide(lax.dynamic_slice_in_dim(vir_irrep, col * RUN, RUN)[None, :])
    return finish(slot, irr, energy, parts, va, vb, sa, sb)


def solution(mesh):
    return jax.shard_map(
        shards,
        mesh=mesh,
        in_specs=(
            P("row", None, None, "col"),
            P("row", "col", None, None),
            P(None, None, "row", None),
            P(),
            P(),
            P(),
            P(),
            P(),
            P(),
            P(),
        ),
        out_specs=P("row", None, None, "col"),
        check_vma=False,
    )
```

time: 1150 us -> 258 us (0.22); the launches traced: 1130 us -> 256 us
  waiting for transfers between devices: 753 us -> 53.7 us
  local copies, waits for them, and re-layouts: 315 us -> 30.9 us
  Pallas kernels: 0 us -> 109 us
  starting transfers between devices: 8.52 us -> 46.6 us
  matrix products: 31.3 us -> 9.59 us
  between operations: 13.5 us -> 0.31 us
    reduce_scatter x1 -> x0, waiting for transfers between devices: 656 us -> none  [shards(): lax.psum_scatter(arranged, ('row', 'col'), scatter_dimension=0, tiled=True)]
    reshape x4 -> x2, local copies, waits for them, and re-layouts: 115 us -> 4.86 us  [the longest x1 4.78 us: shards(): cyc = jnp.where(wanted[..., None], cyc, 0.0).reshape(OI, OJ, SA * RUN)]
    pallas_call x0 -> x11, Pallas kernels: none -> 109 us  [the longest x4 42.1 us: ladder(): pl.pallas_call(body, grid_spec=pltpu.PrefetchScalarGridSpec(num_scalar_pr...]
    unnamed x26 -> x36, local copies, waits for them, and re-layouts: 85.8 us -> 8.27 us
    dynamic_update_slice x1 -> x0, local copies, waits for them, and re-layouts: 45.6 us -> none  [shards(): lax.dynamic_update_slice_in_dim(ladder, current + cycle_part, b_first, 3)]
    all_to_all x1 -> x6, waiting for transfers between devices: 97.2 us -> 53.5 us  [the longest x4 33.6 us: shards(): lax.all_to_all(sent, 'row', split_axis=0, concat_axis=0, tiled=True)]
    all_to_all x1 -> x6, starting transfers between devices: 8.48 us -> 42.1 us  [the longest x4 25.6 us: shards(): lax.all_to_all(sent, 'row', split_axis=0, concat_axis=0, tiled=True)]
    dot_general x1 -> x0, local copies, waits for them, and re-layouts: 22.7 us -> none  [shards(): ladder = jnp.dot(slab_rows, ints_flat, preferred_element_type=jnp.float32)]
  transfers between devices with their start and end apart: 2 -> 7, of which waited for: 2 -> 6; matrix products, arithmetic and copies ran while one was open for 5% -> 14% of each run, Pallas kernels for 0% -> 33%
where the time goes in v1:
time: 258 us; the launch traced here: 256 us
  Pallas kernels  109 us (42%)
  waiting for transfers between devices  53.7 us (21%)
  starting transfers between devices  46.6 us (18%)
  local copies, waits for them, and re-layouts  30.9 us (12%)
  matrix products  9.59 us (4%)
  other arithmetic  6.4 us (2%)
    pallas_call x4, Pallas kernels, ladder(): pl.pallas_call(body, grid_spec=pltpu.PrefetchScalarGridSpec(num_scalar_pr...  42.1 us
    all_to_all x4, waiting for transfers between devices, shards(): lax.all_to_all(sent, 'row', split_axis=0, concat_axis=0, tiled=True)  33.6 us
    pallas_call x4, Pallas kernels, pack(): pl.pallas_call(pack_kernel, grid=(4,), in_specs=[pl.BlockSpec((1, OJ, DP,...  32.8 us
    pallas_call x1, Pallas kernels, arrange_ints(): pl.pallas_call(ints_kernel, grid_spec=pltpu.PrefetchScalarGridSpec(num_sc...  30.9 us
    all_to_all x4, starting transfers between devices, shards(): lax.all_to_all(sent, 'row', split_axis=0, concat_axis=0, tiled=True)  25.6 us
    all_to_all x1, waiting for transfers between devices, shards(): lax.all_to_all(keep + got, 'row', split_axis=0, concat_axis=0, tiled=True)  14.6 us
    all_to_all x1, starting transfers between devices, shards(): lax.all_to_all(by_run(ltab, both, spread), 'col', split_axis=0, concat_ax...  9.85 us
    dot_general x1, matrix products, shards(): jnp.einsum('iakc,kjcb->ijab', ovov_ints, amplitudes, preferred_element_ty...  9.59 us
  transfers between devices with their start and end apart: 7, of which 6 were waited for; matrix products, arithmetic and copies ran while one was open for 14% of the time, Pallas kernels for 33%

profile of v1, /device:TPU:1, one launch (start us, length us, event | category | flops | bytes accessed | tf_op | source)
XLA Modules:
  0.0 256.3 jit_solution(10323948434363666256)
XLA Ops:
  0.0 1.1 copy-done.2
  1.1 0.9 copy-done.8
  2.0 8.2 %pack.7 = bf16[16,4,4,32,128]{4,3,2,1,0:T(8,128)(2,1)S(1)} custom-call(bf16[4,32,64,512]{3,2,1,0:T(8,128)(2,1)} %bitcast.27, bf16[256,256]{1,0:T(8,128)(2,1)S(1)} %copy-done.8, bf16[512,512]{1,0:T(8,128)(2,1)S(1)} %copy-done.2), custom_call_target="tpu_custom_call" | custom-call | flops 1600000000 | bytes 4194304 | tf_op jit(solution)/shard_map/pack/pallas_call | solution.py:67
  10.2 1.3 copy-done.7
  11.5 8.6 %all-to-all-start.3 = ((bf16[16,4,4,32,128]{4,3,2,1,0:T(8,128)(2,1)}), bf16[16,4,4,32,128]{4,3,2,1,0:T(8,128)(2,1)S(1)}, u32[]{:S(2)}, u32[]{:S(2)}) async-start(bf16[16,4,4,32,128]{4,3,2,1,0:T(8,128)(2,1)} %copy-done.7), calls=%async_computation.3 | async-start | bytes 4194304 | tf_op jit(solution)/shard_map/all_to_all | solution.py:313
  20.2 8.2 %pack.6 = bf16[16,4,4,32,128]{4,3,2,1,0:T(8,128)(2,1)S(1)} custom-call(bf16[4,32,64,512]{3,2,1,0:T(8,128)(2,1)} %bitcast.28, bf16[256,256]{1,0:T(8,128)(2,1)S(1)} %copy-done.9, bf16[512,512]{1,0:T(8,128)(2,1)S(1)} %copy-done.3), custom_call_target="tpu_custom_call" | custom-call | flops 1600000000 | bytes 4194304 | tf_op jit(solution)/shard_map/pack/pallas_call | solution.py:67
  28.4 1.3 copy-done.5
  29.7 18.2 %all-to-all-done.3.r_ref = bf16[16,4,4,32,128]{4,3,2,1,0:T(8,128)(2,1)S(1)} async-done(((bf16[16,4,4,32,128]{4,3,2,1,0:T(8,128)(2,1)}), bf16[16,4,4,32,128]{4,3,2,1,0:T(8,128)(2,1)S(1)}, u32[]{:S(2)}, u32[]{:S(2)}) %all-to-all-start.3) | async-done | bytes 2097184 | tf_op jit(solution)/shard_map/all_to_all | solution.py:313
  47.9 4.4 %all-to-all-start.2 = ((bf16[16,4,4,32,128]{4,3,2,1,0:T(8,128)(2,1)}), bf16[16,4,4,32,128]{4,3,2,1,0:T(8,128)(2,1)}, u32[]{:S(2)}, u32[]{:S(2)}) async-start(bf16[16,4,4,32,128]{4,3,2,1,0:T(8,128)(2,1)} %copy-done.5), calls=%async_computation.2 | async-start | bytes 4194304 | tf_op jit(solution)/shard_map/all_to_all | solution.py:313
  52.5 0.6 gather_fusion
  53.1 0.7 gather_fusion.5
  53.8 0.7 gather_fusion.6
  54.6 8.2 %pack.5 = bf16[16,4,4,32,128]{4,3,2,1,0:T(8,128)(2,1)S(1)} custom-call(bf16[4,32,64,512]{3,2,1,0:T(8,128)(2,1)} %bitcast.29, bf16[256,256]{1,0:T(8,128)(2,1)S(1)} %copy-done.9, bf16[512,512]{1,0:T(8,128)(2,1)S(1)} %copy-done.3), custom_call_target="tpu_custom_call" | custom-call | flops 1600000000 | bytes 4194304 | tf_op jit(solution)/shard_map/pack/pallas_call | solution.py:67
  62.9 1.3 copy-done.4
  64.3 13.1 %all-to-all-done.2.r_ref = bf16[16,4,4,32,128]{4,3,2,1,0:T(8,128)(2,1)} async-done(((bf16[16,4,4,32,128]{4,3,2,1,0:T(8,128)(2,1)}), bf16[16,4,4,32,128]{4,3,2,1,0:T(8,128)(2,1)}, u32[]{:S(2)}, u32[]{:S(2)}) %all-to-all-start.2) | async-done | bytes 2097184 | tf_op jit(solution)/shard_map/all_to_all | solution.py:313
  77.4 5.9 %all-to-all-start.1 = ((bf16[16,4,4,32,128]{4,3,2,1,0:T(8,128)(2,1)}), bf16[16,4,4,32,128]{4,3,2,1,0:T(8,128)(2,1)}, u32[]{:S(2)}, u32[]{:S(2)}) async-start(bf16[16,4,4,32,128]{4,3,2,1,0:T(8,128)(2,1)} %copy-done.4), calls=%async_computation.1 | async-start | bytes 4194304 | tf_op jit(solution)/shard_map/all_to_all | solution.py:313
  83.3 0.6 gather_fusion.3
  84.2 1.7 and.90
  85.9 3.1 %and.91 = pred[8,128,256]{1,2,0:T(8,128)(4,1)S(1)} reshape(pred[8,4,32,8,4,8]{2,1,5,4,3,0:T(4,128)(4,1)} %and.90) | data formatting | bytes 524288 | tf_op jit(solution)/shard_map/and | solution.py:325
  90.0 1.2 and_convert_fusion
  91.2 1.3 copy.53.pick_ref
  92.6 0.7 dynamic_slice.18
  93.9 8.2 %pack.4 = bf16[16,4,4,32,128]{4,3,2,1,0:T(8,128)(2,1)S(1)} custom-call(bf16[4,32,64,512]{3,2,1,0:T(8,128)(2,1)} %bitcast.30, bf16[256,256]{1,0:T(8,128)(2,1)S(1)} %copy-done.9, bf16[512,512]{1,0:T(8,128)(2,1)S(1)} %copy-done.3), custom_call_target="tpu_custom_call" | custom-call | flops 1600000000 | bytes 4194304 | tf_op jit(solution)/shard_map/pack/pallas_call | solution.py:67
  102.2 1.3 copy-done.6
  103.5 0.7 broadcast_xor_fusion.4
  104.2 0.7 xor_compare_fusion
  105.0 2.4 all-to-all-done.1.r_ref
  107.4 6.8 %all-to-all-start = ((bf16[16,4,4,32,128]{4,3,2,1,0:T(8,128)(2,1)}), bf16[16,4,4,32,128]{4,3,2,1,0:T(8,128)(2,1)}, u32[]{:S(2)}, u32[]{:S(2)}) async-start(bf16[16,4,4,32,128]{4,3,2,1,0:T(8,128)(2,1)} %copy-done.6), calls=%async_computation | async-start | bytes 4194304 | tf_op jit(solution)/shard_map/all_to_all | solution.py:313
  114.1 9.6 %bitcast_select_fusion = f32[32,32,8,64]{3,0,2,1:T(8,128)S(1)} fusion(pred[32,32,8]{0,2,1:T(8,128)(4,1)S(1)} %xor_compare_fusion, bf16[32,8,4,512]{3,2,1,0:T(4,128)(2,1)} %param.23, bf16[4,32,512,64]{2,3,1,0:T(8,128)(2,1)} %param.21), kind=kOutput, calls=%fused_computation.9 | convolution fusion | flops 2148007936 | bytes 11542528 | tf_op jit(solution)/shard_map/iakc,kjcb->ijab/dot_general | solution.py:330
  123.7 4.4 %copy.52 = f32[32,32,8,64]{3,2,1,0:T(8,128)} copy(f32[32,32,8,64]{3,0,2,1:T(8,128)S(1)} %bitcast_select_fusion) | data formatting | bytes 4194304 | tf_op jit(solution)/shard_map/jit(_where)/select_n | solution.py:333
  128.1 4.8 %reshape.247.cycle_ref = f32[32,32,512]{2,1,0:T(8,128)} reshape(f32[32,32,8,64]{3,2,1,0:T(8,128)} %copy.52) | data formatting | bytes 4194304 | tf_op jit(solution)/shard_map/reshape | solution.py:333
  133.0 30.9 %arrange_ints.1.ints_ref = bf16[4,8,512,512]{3,2,1,0:T(8,128)(2,1)} custom-call(s32[8,8]{1,0:T(8,128)S(1)} %broadcast_xor_fusion.2.gtab_ref, bf16[32,512,512]{2,1,0:T(8,128)(2,1)} %bitcast.31, bf16[256,256]{1,0:T(8,128)(2,1)S(1)} %copy-done.9), custom_call_target="tpu_custom_call" | custom-call | flops 4300000256 | bytes 33554432 | tf_op jit(solution)/shard_map/arrange_ints/pallas_call | solution.py:106
  163.8 8.8 %ladder.4.rest_0_ = f32[8,256,512]{2,1,0:T(8,128)} custom-call(s32[32]{0:T(128)S(1)} %copy-done.12, bf16[16,4,4,32,128]{4,3,2,1,0:T(8,128)(2,1)S(1)} %all-to-all-done.3.r_ref, bf16[8,256,128]{2,1,0:T(8,128)(2,1)S(1)} %copy.53.pick_ref, bf16[4,8,512,512]{3,2,1,0:T(8,128)(2,1)} %arrange_ints.1.ints_ref), custom_call_target="tpu_custom_call" | custom-call | flops 1350000000 | bytes 14680064 | tf_op jit(solution)/shard_map/ladder/pallas_call | solution.py:216
  172.6 10.4 %ladder.5.rest_0_ = f32[8,256,512]{2,1,0:T(8,128)} custom-call(s32[32]{0:T(128)S(1)} %copy-done.12, bf16[16,4,4,32,128]{4,3,2,1,0:T(8,128)(2,1)} %all-to-all-done.2.r_ref, bf16[8,256,128]{2,1,0:T(8,128)(2,1)S(1)} %copy.53.pick_ref, bf16[4,8,512,512]{3,2,1,0:T(8,128)(2,1)} %arrange_ints.1.ints_ref, f32[8,256,512]{2,1,0:T(8,128)} %ladder.4.rest_0_), custom_call_target="tpu_custom_call" | custom-call | flops 1350000000 | bytes 14680064 | tf_op jit(solution)/shard_map/ladder/pallas_call | solution.py:216
  183.0 10.4 %ladder.6.acc_ref = f32[8,256,512]{2,1,0:T(8,128)} custom-call(s32[32]{0:T(128)S(1)} %copy-done.12, bf16[16,4,4,32,128]{4,3,2,1,0:T(8,128)(2,1)} %all-to-all-done.1.r_ref, bf16[8,256,128]{2,1,0:T(8,128)(2,1)S(1)} %copy.53.pick_ref, bf16[4,8,512,512]{3,2,1,0:T(8,128)(2,1)} %arrange_ints.1.ints_ref, f32[8,256,512]{2,1,0:T(8,128)} %ladder.5.rest_0_), custom_call_target="tpu_custom_call" | custom-call | flops 1350000000 | bytes 14680064 | tf_op jit(solution)/shard_map/ladder/pallas_call | solution.py:216
  193.4 12.6 %ladder.7 = (f32[16,32,512]{2,1,0:T(8,128)S(1)}, f32[16,32,512]{2,1,0:T(8,128)}) custom-call(s32[32]{0:T(128)S(1)} %copy-done.12, s32[1]{0:T(128)} %bitcast.1.core_ref, bf16[16,4,4,32,128]{4,3,2,1,0:T(8,128)(2,1)} %all-to-all-done.r_ref, bf16[8,256,128]{2,1,0:T(8,128)(2,1)S(1)} %copy.53.pick_ref, bf16[4,8,512,512]{3,2,1,0:T(8,128)(2,1)} %arrange_ints.1.ints_ref, ...), custom_call_target="tpu_custom_call" | custom-call | flops 1350000000 | bytes 14680064 | tf_op jit(solution)/shard_map/ladder/pallas_call | solution.py:216
  206.0 1.0 copy-done.11
  207.0 4.5 %collective-permute-start = (f32[16,32,512]{2,1,0:T(8,128)}, f32[16,32,512]{2,1,0:T(8,128)S(1)}, u32[]{:S(2)}, u32[]{:S(2)}) collective-permute-start(f32[16,32,512]{2,1,0:T(8,128)} %get-tuple-element.9), channel_id=1, source_target_pairs={{0,1},{1,0},{2,3},{3,2},{4,5},{5,4},{6,7},{7,6},{8,9},{9,8},{10,11... | collective-permute-start | bytes 3145736 | tf_op jit(solution)/shard_map/ppermute | solution.py:341
  211.5 0.6 gather_fusion.1
  212.1 0.7 gather_fusion.2
  213.0 0.7 gather_fusion.4
  214.0 2.5 add.74
  216.4 6.6 %all-to-all-start.4 = ((f32[16,32,512]{2,1,0:T(8,128)}), f32[16,32,512]{2,1,0:T(8,128)S(1)}, u32[]{:S(2)}, u32[]{:S(2)}) async-start(f32[16,32,512]{2,1,0:T(8,128)} %add.74), calls=%async_computation.4 | async-start | bytes 2097152 | tf_op jit(solution)/shard_map/all_to_all | solution.py:342
  223.5 14.6 %all-to-all-done.4.x_ref = f32[16,32,512]{2,1,0:T(8,128)S(1)} async-done(((f32[16,32,512]{2,1,0:T(8,128)}), f32[16,32,512]{2,1,0:T(8,128)S(1)}, u32[]{:S(2)}, u32[]{:S(2)}) %all-to-all-start.4) | async-done | bytes 1048608 | tf_op jit(solution)/shard_map/all_to_all | solution.py:342
  238.1 1.5 by_run.1
  239.6 9.8 %all-to-all-start.5 = ((f32[8,8,512]{2,1,0:T(8,128)}), f32[8,8,512]{2,1,0:T(8,128)S(1)}, u32[]{:S(2)}, u32[]{:S(2)}) async-start(f32[8,8,512]{2,1,0:T(8,128)} %by_run.1), calls=%async_computation.5 | async-start | bytes 262144 | tf_op jit(solution)/shard_map/all_to_all | solution.py:354
  249.4 5.3 %all-to-all-done.5.x_ref = f32[8,8,512]{2,1,0:T(8,128)S(1)} async-done(((f32[8,8,512]{2,1,0:T(8,128)}), f32[8,8,512]{2,1,0:T(8,128)S(1)}, u32[]{:S(2)}, u32[]{:S(2)}) %all-to-all-start.5) | async-done | bytes 131104 | tf_op jit(solution)/shard_map/all_to_all | solution.py:354
  254.8 1.5 finish.1
  (72 shorter events, 3.7 us)
Async XLA Ops:
  0.0 52.5 %copy-start = (s32[64]{0:T(128)S(1)}, s32[64]{0:T(128)}, u32[]{:S(2)}) copy-start(s32[64]{0:T(128)} %param.26) | copy-start | bytes 772
  0.0 1.1 copy-start.2
  1.1 0.9 copy-start.8
  10.2 1.3 copy-start.7
  11.5 8.6 %copy-start.12 = (s32[32]{0:T(128)S(1)}, s32[32]{0:T(128)}, u32[]{:S(2)}) copy-start(s32[32]{0:T(128)} %iorb_ref.7) | copy-start | bytes 388
  11.5 8.7 %copy-start.3 = (bf16[512,512]{1,0:T(8,128)(2,1)S(1)}, bf16[512,512]{1,0:T(8,128)(2,1)}, u32[]{:S(2)}) copy-start(bf16[512,512]{1,0:T(8,128)(2,1)} %constant.126.clone.lanes_ref) | copy-start | bytes 1572868
  11.5 8.7 %copy-start.9 = (bf16[256,256]{1,0:T(8,128)(2,1)S(1)}, bf16[256,256]{1,0:T(8,128)(2,1)}, u32[]{:S(2)}) copy-start(bf16[256,256]{1,0:T(8,128)(2,1)} %constant.125.clone.swap_ref) | copy-start | bytes 393220
  11.5 36.4 %all-to-all-start.3 = ((bf16[16,4,4,32,128]{4,3,2,1,0:T(8,128)(2,1)}), bf16[16,4,4,32,128]{4,3,2,1,0:T(8,128)(2,1)S(1)}, u32[]{:S(2)}, u32[]{:S(2)}) async-start(bf16[16,4,4,32,128]{4,3,2,1,0:T(8,128)(2,1)} %copy-done.7), calls=%async_computation.3 | async-start | bytes 4194304 | tf_op jit(solution)/shard_map/all_to_all | solution.py:313
  20.2 9.5 %copy-start.17 = (s32[32]{0:T(128)S(1)}, s32[32]{0:T(128)}, u32[]{:S(2)}) copy-start(s32[32]{0:T(128)} %param.29) | copy-start | bytes 388
  28.4 1.3 copy-start.5
  29.7 22.6 %copy-start.14 = (s32[512]{0:T(512)S(1)}, s32[512]{0:T(512)}, u32[]{:S(2)}) copy-start(s32[512]{0:T(512)} %param.27) | copy-start | bytes 6148
  47.9 29.5 %all-to-all-start.2 = ((bf16[16,4,4,32,128]{4,3,2,1,0:T(8,128)(2,1)}), bf16[16,4,4,32,128]{4,3,2,1,0:T(8,128)(2,1)}, u32[]{:S(2)}, u32[]{:S(2)}) async-start(bf16[16,4,4,32,128]{4,3,2,1,0:T(8,128)(2,1)} %copy-done.5), calls=%async_computation.2 | async-start | bytes 4194304 | tf_op jit(solution)/shard_map/all_to_all | solution.py:313
  54.6 9.6 %copy-start.16 = (s32[8]{0:T(128)S(1)}, s32[8]{0:T(128)}, u32[]{:S(2)}) copy-start(s32[8]{0:T(128)} %param.30) | copy-start | bytes 100
  62.8 1.3 copy-start.4
  77.4 29.9 %all-to-all-start.1 = ((bf16[16,4,4,32,128]{4,3,2,1,0:T(8,128)(2,1)}), bf16[16,4,4,32,128]{4,3,2,1,0:T(8,128)(2,1)}, u32[]{:S(2)}, u32[]{:S(2)}) async-start(bf16[16,4,4,32,128]{4,3,2,1,0:T(8,128)(2,1)} %copy-done.4), calls=%async_computation.1 | async-start | bytes 4194304 | tf_op jit(solution)/shard_map/all_to_all | solution.py:313
  102.1 1.3 copy-start.6
  107.4 86.1 %all-to-all-start = ((bf16[16,4,4,32,128]{4,3,2,1,0:T(8,128)(2,1)}), bf16[16,4,4,32,128]{4,3,2,1,0:T(8,128)(2,1)}, u32[]{:S(2)}, u32[]{:S(2)}) async-start(bf16[16,4,4,32,128]{4,3,2,1,0:T(8,128)(2,1)} %copy-done.6), calls=%async_computation | async-start | bytes 4194304 | tf_op jit(solution)/shard_map/all_to_all | solution.py:313
  183.0 10.4 %copy-start.10 = (bf16[8,128,256]{2,1,0:T(8,128)(2,1)S(1)}, bf16[8,128,256]{2,1,0:T(8,128)(2,1)}, u32[]{:S(2)}) copy-start(bf16[8,128,256]{2,1,0:T(8,128)(2,1)} %get-tuple-element.12.drop_ref) | copy-start | bytes 1572868
  193.4 18.1 %copy-start.13 = (f32[64]{0:T(128)S(1)}, f32[64]{0:T(128)}, u32[]{:S(2)}) copy-start(f32[64]{0:T(128)} %param.24) | copy-start | bytes 772
  193.4 19.5 %copy-start.15 = (f32[512]{0:T(512)S(1)}, f32[512]{0:T(512)}, u32[]{:S(2)}) copy-start(f32[512]{0:T(512)} %param.25) | copy-start | bytes 6148
  206.0 1.0 copy-start.11
  207.0 7.0 %collective-permute-start = (f32[16,32,512]{2,1,0:T(8,128)}, f32[16,32,512]{2,1,0:T(8,128)S(1)}, u32[]{:S(2)}, u32[]{:S(2)}) collective-permute-start(f32[16,32,512]{2,1,0:T(8,128)} %get-tuple-element.9), channel_id=1, source_target_pairs={{0,1},{1,0},{2,3},{3,2},{4,5},{5,4},{6,7},{7,6},{8,9},{9,8},{10,11... | collective-permute-start | bytes 3145736 | tf_op jit(solution)/shard_map/ppermute | solution.py:341
  211.5 44.8 %copy-start.1 = (s32[64]{0:T(128)S(1)}, s32[64]{0:T(128)}, u32[]{:S(2)}) copy-start(s32[64]{0:T(128)} %param.26) | copy-start | bytes 772
  216.4 21.6 %all-to-all-start.4 = ((f32[16,32,512]{2,1,0:T(8,128)}), f32[16,32,512]{2,1,0:T(8,128)S(1)}, u32[]{:S(2)}, u32[]{:S(2)}) async-start(f32[16,32,512]{2,1,0:T(8,128)} %add.74), calls=%async_computation.4 | async-start | bytes 2097152 | tf_op jit(solution)/shard_map/all_to_all | solution.py:342
  239.6 15.1 %all-to-all-start.5 = ((f32[8,8,512]{2,1,0:T(8,128)}), f32[8,8,512]{2,1,0:T(8,128)S(1)}, u32[]{:S(2)}, u32[]{:S(2)}) async-start(f32[8,8,512]{2,1,0:T(8,128)} %by_run.1), calls=%async_computation.5 | async-start | bytes 262144 | tf_op jit(solution)/shard_map/all_to_all | solution.py:354

commit v2 on v1

v2 whole, which is shorter than its diff:
```python
import functools

import jax
import jax.numpy as jnp
import numpy as np
from jax import lax
from jax.experimental import pallas as pl
from jax.experimental.pallas import tpu as pltpu
from jax.sharding import PartitionSpec as P

F32 = jnp.float32
BF16 = jnp.bfloat16
VMEM = 22 * 1024 * 1024

NO, NV, OI, OJ, SA = 64, 512, 32, 32, 8
ROWS, COLS, RUN = 16, 8, 64
PIECES = 2
DP = 64 // PIECES
QP = DP // 4
KP = DP * 32


def params(n=1):
    return pltpu.CompilerParams(
        dimension_semantics=("arbitrary",) * n, vmem_limit_bytes=VMEM
    )


def in_hbm(x):
    return pltpu.with_memory_space_constraint(x, pltpu.HBM)


def in_vmem(x):
    return pltpu.with_memory_space_constraint(x, pltpu.VMEM)


def cost(flops, nbytes):
    return pl.CostEstimate(flops=flops, bytes_accessed=nbytes, transcendentals=0)


def lane_swap():
    out = np.zeros((4, 4, 32, 4, 4, 32), np.float32)
    for e in range(4):
        for z in range(4):
            for c in range(32):
                out[e, z, c, z, e, c] = 1
    return out.reshape(512, 512).astype(jnp.bfloat16)


def pack_kernel(x_ref, lanes_ref, out_ref, mid_ref):
    for jh in range(2):
        rows = slice(16 * jh, 16 * jh + 16)
        for dh in range(DP // 16):
            y = jnp.swapaxes(x_ref[0, rows, 16 * dh : 16 * dh + 16, :], 0, 1)
            for q in range(4):
                for e in range(4):
                    for x in range(4):
                        mid_ref[x, 4 * dh + q, rows, 128 * e : 128 * e + 128] = y[
                            4 * q + e, :, 128 * x : 128 * x + 128
                        ]
    for x in range(4):
        w = jnp.dot(mid_ref[x].reshape(QP * OJ, 512), lanes_ref[...], preferred_element_type=F32)
        w = w.astype(BF16)
        for z in range(4):
            out_ref[4 * x + z, 0] = w[:, 128 * z : 128 * z + 128].reshape(QP, OJ, 128)


def pack(amp_t, piece):
    return pl.pallas_call(
        pack_kernel,
        grid=(4,),
        in_specs=[
            pl.BlockSpec((1, OJ, DP, NV), lambda k: (k, 0, piece, 0)),
            pl.BlockSpec((512, 512), lambda k: (0, 0)),
        ],
        out_specs=pl.BlockSpec((ROWS, 1, QP, OJ, 128), lambda k: (0, k, 0, 0, 0)),
        out_shape=pltpu.HBM((ROWS, 4, QP, OJ, 128), BF16),
        scratch_shapes=[pltpu.VMEM((4, QP, OJ, 512), BF16)],
        compiler_params=params(),
        cost_estimate=cost(8_000_000_000 // PIECES, 2 * 8 * 2**20 // PIECES),
        name="pack",
    )(in_hbm(amp_t), in_hbm(jnp.asarray(lane_swap())))


IN_STEP = 8


def ints_kernel(gtab_ref, v_ref, out_ref):
    for dd in range(IN_STEP // 2):
        for ch in range(2):
            x = v_ref[16 * ch : 16 * ch + 16, 16 * dd : 16 * dd + 16, :]
            y = jnp.swapaxes(x, 0, 1)
            for d in range(2):
                row = 64 * dd + 32 * d + 16 * ch
                for a in range(SA):
                    off = 64 * (a % 2)
                    for t in range(4):
                        tile = y[8 * d + a, :, 128 * t : 128 * t + 128]
                        for e in range(2):
                            part = tile[:, 64 * e : 64 * e + 64]
                            out_ref[gtab_ref[a, 2 * t + e], row : row + 16, 64 * a : 64 * a + 64] = part


def arrange_ints(piece, gtab, ints):
    steps = DP // IN_STEP
    return pl.pallas_call(
        ints_kernel,
        grid_spec=pltpu.PrefetchScalarGridSpec(
            num_scalar_prefetch=1,
            grid=(steps,),
            in_specs=[pl.BlockSpec((32, 8 * IN_STEP, NV), lambda s, *_: (0, piece * steps + s, 0))],
            out_specs=pl.BlockSpec((8, 32 * IN_STEP, NV), lambda s, *_: (0, s, 0)),
        ),
        out_shape=jax.ShapeDtypeStruct((8, KP, SA * RUN), BF16),
        compiler_params=params(),
        cost_estimate=cost(4_300_000_000, 32 * 2**20 // PIECES),
        name="arrange_ints",
    )(gtab, in_hbm(ints))


def two_terms(x):
    hi = x.astype(BF16)
    return hi, (x - hi.astype(F32)).astype(BF16)


def gather_rows(iorb_ref, r_ref, pick_ref, rows_ref, slab_ref, sems):
    def slab(p):
        k = iorb_ref[p]
        return pltpu.make_async_copy(r_ref.at[k // 4, k % 4], slab_ref.at[p], sems.at[p])

    def start(p, carry):
        slab(p).start()
        return carry

    def block(blk, carry):
        slabs = []
        for i in range(4):
            slab(4 * blk + i).wait()
        for i in range(4):
            slabs.append(
                jnp.concatenate([slab_ref[4 * blk + i, q] for q in range(QP)], axis=1)
            )
        x = jnp.concatenate(slabs, axis=0)
        y = jnp.dot(pick_ref[blk], x, preferred_element_type=F32).astype(BF16)
        rows_ref[:, pl.ds(pl.multiple_of(32 * blk, 32), 32), :] = y.reshape(8, 32, KP)
        return carry

    lax.fori_loop(0, OI, start, 0)
    lax.fori_loop(0, 8, block, 0)


GATHER_SCRATCH = [
    pltpu.VMEM((8, 256, KP), BF16),
    pltpu.VMEM((OI, QP, OJ, 128), BF16),
    pltpu.SemaphoreType.DMA((OI,)),
]


def ladder_kernel(first, iorb_ref, r_ref, pick_ref, ints_ref, *rest):
    if first:
        out_ref, rows_ref, slab_ref, sems = rest
    else:
        acc_ref, out_ref, rows_ref, slab_ref, sems = rest
    g = pl.program_id(0)

    @pl.when(g == 0)
    def _():
        gather_rows(iorb_ref, r_ref, pick_ref, rows_ref, slab_ref, sems)

    got = jnp.dot(rows_ref[g], ints_ref[0], preferred_element_type=F32)
    out_ref[0] = got if first else got + acc_ref[0]


def last_kernel(iorb_ref, core_ref, r_ref, pick_ref, ints_ref, acc_ref, drop_ref, cycle_ref,
                keep_ref, send_ref, rows_ref, slab_ref, sems, sum_ref):
    core = core_ref[0]
    gather_rows(iorb_ref, r_ref, pick_ref, rows_ref, slab_ref, sems)

    def group(g, carry):
        sum_ref[g] = acc_ref[g] + jnp.dot(rows_ref[g], ints_ref[g], preferred_element_type=F32)
        return carry

    lax.fori_loop(0, 8, group, 0)

    def block(blk, carry):
        x = sum_ref[:, pl.ds(pl.multiple_of(32 * blk, 32), 32), :].reshape(256, SA * RUN)
        hi, lo = two_terms(x)
        y = jnp.dot(drop_ref[blk], hi, preferred_element_type=F32)
        y = y + jnp.dot(drop_ref[blk], lo, preferred_element_type=F32)
        for i in range(4):
            got = y[32 * i : 32 * i + 32, :] + cycle_ref[4 * blk + i]

            @pl.when(core == i % 2)
            def _():
                keep_ref[2 * blk + i // 2] = got

            @pl.when(core != i % 2)
            def _():
                send_ref[2 * blk + i // 2] = got

        return carry

    lax.fori_loop(0, 8, block, 0)


def ladder(first, iorb, arrived, pick, ints, acc):
    whole = lambda *dims: pl.BlockSpec(dims, lambda g, *_: (0,) * len(dims))
    acc_spec = pl.BlockSpec((1, 256, 512), lambda g, *_: (g, 0, 0))
    in_specs = [
        pl.BlockSpec(memory_space=pltpu.HBM),
        whole(8, 256, 128),
        pl.BlockSpec((1, KP, 512), lambda g, *_: (g, 0, 0)),
    ]
    args = [in_hbm(arrived), pick, ints]
    if not first:
        in_specs.append(acc_spec)
        args.append(acc)
    return pl.pallas_call(
        functools.partial(ladder_kernel, first),
        grid_spec=pltpu.PrefetchScalarGridSpec(
            num_scalar_prefetch=1,
            grid=(8,),
            in_specs=in_specs,
            out_specs=acc_spec,
            scratch_shapes=GATHER_SCRATCH,
        ),
        out_shape=jax.ShapeDtypeStruct((8, 256, 512), F32),
        compiler_params=params(),
        cost_estimate=cost(5_400_000_000 // PIECES, 14 * 2**20),
        name="ladder",
    )(iorb, *args)


def last_ladder(iorb, core, arrived, *args):
    smem = pl.BlockSpec(memory_space=pltpu.SMEM)
    vmem = pl.BlockSpec(memory_space=pltpu.VMEM)
    return pl.pallas_call(
        last_kernel,
        in_specs=[smem, smem, pl.BlockSpec(memory_space=pltpu.HBM)] + [vmem] * len(args),
        out_specs=[vmem] * 2,
        out_shape=[jax.ShapeDtypeStruct((16, OJ, 512), F32)] * 2,
        scratch_shapes=GATHER_SCRATCH + [pltpu.VMEM((8, 256, 512), F32)],
        compiler_params=pltpu.CompilerParams(vmem_limit_bytes=VMEM),
        cost_estimate=cost(5_400_000_000 // PIECES, 14 * 2**20),
        name="last_ladder",
    )(iorb, core, in_hbm(arrived), *[in_vmem(x) for x in args])


def by_run_kernel(ltab_ref, x_ref, spread_ref, out_ref):
    hi, lo = two_terms(jnp.sum(x_ref[...], axis=0))
    y = jnp.dot(spread_ref[...], hi, preferred_element_type=F32)
    y = y + jnp.dot(spread_ref[...], lo, preferred_element_type=F32)
    for a in range(SA):
        for t in range(8):
            out_ref[ltab_ref[a, t], :, 64 * a : 64 * a + 64] = y[8 * t : 8 * t + 8, 64 * a : 64 * a + 64]


def by_run(ltab, x, spread):
    return pl.pallas_call(
        by_run_kernel,
        grid_spec=pltpu.PrefetchScalarGridSpec(
            num_scalar_prefetch=1,
            grid=(1,),
            in_specs=[
                pl.BlockSpec((ROWS, OJ, 512), lambda s, *_: (0, 0, 0)),
                pl.BlockSpec((64, OJ), lambda s, *_: (0, 0)),
            ],
            out_specs=pl.BlockSpec((8, 8, 512), lambda s, *_: (0, 0, 0)),
        ),
        out_shape=jax.ShapeDtypeStruct((8, 8, 512), F32),
        compiler_params=params(),
        name="by_run",
    )(ltab, x, spread)


def finish_kernel(slot_ref, irr_ref, energy_ref, x_ref, va_ref, vb_ref, sa_ref, sb_ref, out_ref, tile_ref):
    for h in range(2):
        v = x_ref[h]
        for y in range(1, 4):
            v = v + x_ref[2 * y + h]
        for a in range(SA):
            tile_ref[h, :, a, :] = v[:, 64 * a : 64 * a + 64]
    sym_ab = jnp.bitwise_xor(sa_ref[...], sb_ref[...])
    for h in range(2):
        for j in range(OJ):
            got = tile_ref[h, slot_ref[j]]
            den = energy_ref[h, j] - va_ref[...] - vb_ref[...]
            ok = jnp.bitwise_xor(sym_ab, irr_ref[h, j]) == 0
            out_ref[h, j] = jnp.where(ok, got / den, jnp.zeros_like(got))


def finish(slot, irr, energy, x, va, vb, sa, sb):
    full = lambda *dims: pl.BlockSpec(dims, lambda s, *_: (0,) * len(dims))
    return pl.pallas_call(
        finish_kernel,
        grid_spec=pltpu.PrefetchScalarGridSpec(
            num_scalar_prefetch=3,
            grid=(1,),
            in_specs=[full(8, 8, 512), full(8, 64), full(8, 64), full(8, 64), full(8, 64)],
            out_specs=full(2, OJ, SA, RUN),
            scratch_shapes=[pltpu.VMEM((2, 8, SA, RUN), F32)],
        ),
        out_shape=jax.ShapeDtypeStruct((2, OJ, SA, RUN), F32),
        compiler_params=params(),
        name="finish",
    )(slot, irr, energy, x, va, vb, sa, sb)


def shards(
    amplitudes,
    vvvv_ints,
    ovov_ints,
    occ_energy,
    vir_energy,
    occ_irrep,
    vir_irrep,
    i_orbitals,
    j_orbitals,
    a_orbitals,
):
    row = lax.axis_index("row")
    col = lax.axis_index("col")
    core = lax.rem(col, 2)
    labels = jnp.arange(8, dtype=jnp.int32)

    amp_t = amplitudes.transpose(0, 1, 3, 2)
    arrived = []
    for piece in range(PIECES):
        sent = pack(amp_t, piece)
        arrived.append(lax.all_to_all(sent, "row", split_axis=0, concat_axis=0, tiled=True))

    sym_i = jnp.take(occ_irrep, i_orbitals)
    sym_j = jnp.take(occ_irrep, j_orbitals)
    sym_a = jnp.take(vir_irrep, a_orbitals)
    run_label = vir_irrep.reshape(8, RUN)[:, 0]
    slot = j_orbitals % 8
    gtab = jnp.bitwise_xor(sym_a[:, None], run_label[None, :])
    g_ij = jnp.bitwise_xor(sym_i[:, None], sym_j[None, :])
    hit = (g_ij[:, :, None, None] == labels[:, None]) & (slot[:, None, None] == labels)
    hit = hit.reshape(8, 4, OJ, 8, 8)
    same = (jnp.arange(4)[:, None] == jnp.arange(4)).reshape(1, 4, 1, 1, 4, 1)
    drop = (hit[:, :, :, :, None, :] & same).reshape(8, 128, 256).astype(BF16)
    pick = drop.transpose(0, 2, 1)

    ints = [arrange_ints(piece, gtab, vvvv_ints.reshape(32, 512, NV)) for piece in range(PIECES)]

    cyc = jnp.einsum("iakc,kjcb->ijab", ovov_ints, amplitudes, preferred_element_type=F32)
    mine_label = lax.dynamic_index_in_dim(run_label, col, keepdims=False)
    wanted = jnp.bitwise_xor(g_ij[:, :, None], sym_a) == mine_label
    cyc = jnp.where(wanted[..., None], cyc, 0.0).reshape(OI, OJ, SA * RUN)

    acc = None
    for piece in range(PIECES - 1):
        acc = ladder(piece == 0, i_orbitals, arrived[piece], pick, ints[piece], acc)
    keep, send = last_ladder(i_orbitals, core.reshape(1), arrived[-1], pick, ints[-1], acc, drop, cyc)

    got = lax.ppermute(send, "col", [(q, q ^ 1) for q in range(COLS)])
    both = lax.all_to_all(keep + got, "row", split_axis=0, concat_axis=0, tiled=True)

    mine_i = lax.dynamic_slice_in_dim(i_orbitals, 2 * row, 2)
    sym_mine = jnp.take(occ_irrep, mine_i)
    label_at = jnp.bitwise_xor(
        jnp.bitwise_xor(lax.dynamic_index_in_dim(sym_mine, core, keepdims=False), sym_a)[:, None],
        labels[None, :],
    )
    ltab = jnp.sum(jnp.where(label_at[..., None] == run_label, labels, 0), axis=-1).astype(jnp.int32)
    spread = (
        (sym_j[None, None, :] == labels[:, None, None]) & (slot[None, None, :] == labels[None, :, None])
    ).reshape(64, OJ).astype(BF16)
    parts = lax.all_to_all(by_run(ltab, both, spread), "col", split_axis=0, concat_axis=0, tiled=True)

    energy = jnp.take(occ_energy, mine_i)[:, None] + jnp.take(occ_energy, j_orbitals)[None, :]
    irr = jnp.bitwise_xor(sym_mine[:, None], sym_j[None, :])
    wide = lambda x: jnp.broadcast_to(x, (SA, RUN))
    va = wide(jnp.take(vir_energy, a_orbitals)[:, None])
    vb = wide(lax.dynamic_slice_in_dim(vir_energy, col * RUN, RUN)[None, :])
    sa = wide(sym_a[:, None])
    sb = wide(lax.dynamic_slice_in_dim(vir_irrep, col * RUN, RUN)[None, :])
    return finish(slot, irr, energy, parts, va, vb, sa, sb)


def solution(mesh):
    return jax.shard_map(
        shards,
        mesh=mesh,
        in_specs=(
            P("row", None, None, "col"),
            P("row", "col", None, None),
            P(None, None, "row", None),
            P(),
            P(),
            P(),
            P(),
            P(),
            P(),
            P(),
        ),
        out_specs=P("row", None, None, "col"),
        check_vma=False,
    )
```

time: 258 us -> 205 us (0.79)
  Pallas kernels: 109 us -> 50.8 us
  waiting for transfers between devices: 53.7 us -> 72.9 us
  starting transfers between devices: 46.6 us -> 36.1 us
    pallas_call x4 -> x2, Pallas kernels: 42.1 us -> 18.6 us  [the longest x1 11 us: last_ladder(): pl.pallas_call(last_kernel, in_specs=[smem, smem, pl.BlockSpec(memory_spa...]
    pallas_call x4 -> x2, Pallas kernels: 32.8 us -> 13.1 us  [pack(): pl.pallas_call(pack_kernel, grid=(4,), in_specs=[pl.BlockSpec((1, OJ, DP,...]
    all_to_all x4 -> x2, waiting for transfers between devices: 33.6 us -> 52.8 us  [shards(): lax.all_to_all(sent, 'row', split_axis=0, concat_axis=0, tiled=True)]
    pallas_call x1 -> x2, Pallas kernels: 30.9 us -> 16.1 us  [arrange_ints(): pl.pallas_call(ints_kernel, grid_spec=pltpu.PrefetchScalarGridSpec(num_sc...]
    all_to_all x4 -> x2, starting transfers between devices: 25.6 us -> 18.4 us  [shards(): lax.all_to_all(sent, 'row', split_axis=0, concat_axis=0, tiled=True)]
    unnamed x36 -> x28, local copies, waits for them, and re-layouts: 8.27 us -> 11.7 us
    and x6, local copies, waits for them, and re-layouts: 5.7 us -> 2.89 us  [shards(): drop = (hit[:, :, :, :, None, :] & same).reshape(8, 128, 256).astype(BF16)]
  transfers between devices with their start and end apart: 7 -> 5, of which waited for: 6 -> 4; matrix products, arithmetic and copies ran while one was open for 14% -> 14% of each run, Pallas kernels for 33% -> 15%
where the time goes in v2:
time: 205 us; the launch traced here: 204 us
  waiting for transfers between devices  72.9 us (36%)
  Pallas kernels  50.8 us (25%)
  starting transfers between devices  36.1 us (18%)
  local copies, waits for them, and re-layouts  29.1 us (14%)
  matrix products  9.42 us (5%)
  other arithmetic  5.28 us (3%)
    all_to_all x2, waiting for transfers between devices, shards(): lax.all_to_all(sent, 'row', split_axis=0, concat_axis=0, tiled=True)  52.8 us
    all_to_all x2, starting transfers between devices, shards(): lax.all_to_all(sent, 'row', split_axis=0, concat_axis=0, tiled=True)  18.4 us
    pallas_call x2, Pallas kernels, arrange_ints(): pl.pallas_call(ints_kernel, grid_spec=pltpu.PrefetchScalarGridSpec(num_sc...  16.1 us
    all_to_all x1, waiting for transfers between devices, shards(): lax.all_to_all(keep + got, 'row', split_axis=0, concat_axis=0, tiled=True)  14.6 us
    pallas_call x2, Pallas kernels, pack(): pl.pallas_call(pack_kernel, grid=(4,), in_specs=[pl.BlockSpec((1, OJ, DP,...  13.1 us
    unnamed x28, local copies, waits for them, and re-layouts  11.7 us
    pallas_call x1, Pallas kernels, last_ladder(): pl.pallas_call(last_kernel, in_specs=[smem, smem, pl.BlockSpec(memory_spa...  11 us
    dot_general x1, matrix products, shards(): jnp.einsum('iakc,kjcb->ijab', ovov_ints, amplitudes, preferred_element_ty...  9.42 us
  transfers between devices with their start and end apart: 5, of which 4 were waited for; matrix products, arithmetic and copies ran while one was open for 14% of the time, Pallas kernels for 15%

profile of v2, /device:TPU:1, one launch (start us, length us, event | category | flops | bytes accessed | tf_op | source)
XLA Modules:
  0.0 203.9 jit_solution(17002363808369383730)
XLA Ops:
  0.0 6.5 %pack.3 = bf16[16,4,8,32,128]{4,3,2,1,0:T(8,128)(2,1)} custom-call(bf16[4,32,64,512]{3,2,1,0:T(8,128)(2,1)} %bitcast.29, bf16[512,512]{1,0:T(8,128)(2,1)} %constant.123.clone.lanes_ref), custom_call_target="tpu_custom_call" | custom-call | flops 4000000000 | bytes 8388608 | tf_op jit(solution)/shard_map/pack/pallas_call | solution.py:69
  6.6 8.6 %all-to-all-start.1 = ((bf16[16,4,8,32,128]{4,3,2,1,0:T(8,128)(2,1)}), bf16[16,4,8,32,128]{4,3,2,1,0:T(8,128)(2,1)}, u32[]{:S(2)}, u32[]{:S(2)}) async-start(bf16[16,4,8,32,128]{4,3,2,1,0:T(8,128)(2,1)} %pack.3), calls=%async_computation.1 | async-start | bytes 8388608 | tf_op jit(solution)/shard_map/all_to_all | solution.py:330
  15.2 0.7 gather_fusion.5
  16.0 0.7 gather_fusion.6
  17.0 0.3 broadcast_and_fusion
  17.3 6.6 %pack.2 = bf16[16,4,8,32,128]{4,3,2,1,0:T(8,128)(2,1)} custom-call(bf16[4,32,64,512]{3,2,1,0:T(8,128)(2,1)} %bitcast.30, bf16[512,512]{1,0:T(8,128)(2,1)} %constant.123.clone.lanes_ref), custom_call_target="tpu_custom_call" | custom-call | flops 4000000000 | bytes 8388608 | tf_op jit(solution)/shard_map/pack/pallas_call | solution.py:69
  23.8 52.8 %all-to-all-done.1.r_ref = bf16[16,4,8,32,128]{4,3,2,1,0:T(8,128)(2,1)} async-done(((bf16[16,4,8,32,128]{4,3,2,1,0:T(8,128)(2,1)}), bf16[16,4,8,32,128]{4,3,2,1,0:T(8,128)(2,1)}, u32[]{:S(2)}, u32[]{:S(2)}) %all-to-all-start.1) | async-done | bytes 4194336 | tf_op jit(solution)/shard_map/all_to_all | solution.py:330
  76.7 9.8 %all-to-all-start = ((bf16[16,4,8,32,128]{4,3,2,1,0:T(8,128)(2,1)}), bf16[16,4,8,32,128]{4,3,2,1,0:T(8,128)(2,1)}, u32[]{:S(2)}, u32[]{:S(2)}) async-start(bf16[16,4,8,32,128]{4,3,2,1,0:T(8,128)(2,1)} %pack.2), calls=%async_computation | async-start | bytes 8388608 | tf_op jit(solution)/shard_map/all_to_all | solution.py:330
  86.5 0.6 gather_fusion
  87.2 0.6 gather_fusion.3
  87.9 0.7 and.90
  88.5 1.3 and.91
  89.8 0.5 copy.33
  90.3 0.1 and.92
  90.5 0.2 and.93
  90.7 0.1 copy.32
  90.8 0.1 and_convert_fusion
  90.9 0.3 copy.38.pick_ref
  91.3 0.6 dynamic_slice.18
  92.0 0.1 fusion.9
  92.1 0.5 constant_dynamic-slice_fusion
  92.6 0.6 broadcast_xor_fusion.4
  93.3 0.7 xor_compare_fusion
  94.0 9.4 %bitcast_select_fusion = f32[32,32,8,64]{3,0,2,1:T(8,128)S(1)} fusion(pred[32,32,8]{0,2,1:T(8,128)(4,1)S(1)} %xor_compare_fusion, bf16[32,8,4,512]{3,2,1,0:T(4,128)(2,1)S(1)} %copy-done.13, bf16[4,32,512,64]{2,3,1,0:T(8,128)(2,1)} %param.14), kind=kOutput, calls=%fused_computation.9 | convolution fusion | flops 2148007936 | bytes 11542528 | tf_op jit(solution)/shard_map/iakc,kjcb->ijab/dot_general | solution.py:347
  103.5 4.4 %copy.37 = f32[32,32,8,64]{3,2,1,0:T(8,128)} copy(f32[32,32,8,64]{3,0,2,1:T(8,128)S(1)} %bitcast_select_fusion) | data formatting | bytes 4194304 | tf_op jit(solution)/shard_map/jit(_where)/select_n | solution.py:350
  107.8 3.4 %reshape.248.cycle_ref = f32[32,32,512]{2,1,0:T(8,128)S(1)} reshape(f32[32,32,8,64]{3,2,1,0:T(8,128)} %copy.37) | data formatting | bytes 4194304 | tf_op jit(solution)/shard_map/reshape | solution.py:350
  111.3 8.1 %arrange_ints.3.ints_ref = bf16[8,1024,512]{2,1,0:T(8,128)(2,1)S(1)} custom-call(s32[8,8]{1,0:T(8,128)S(1)} %broadcast_xor_fusion.2.gtab_ref, bf16[32,512,512]{2,1,0:T(8,128)(2,1)} %bitcast.27), custom_call_target="tpu_custom_call" | custom-call | flops 4300000256 | bytes 16777216 | tf_op jit(solution)/shard_map/arrange_ints/pallas_call | solution.py:106
  119.4 8.1 %arrange_ints.2.ints_ref = bf16[8,1024,512]{2,1,0:T(8,128)(2,1)S(1)} custom-call(s32[8,8]{1,0:T(8,128)S(1)} %broadcast_xor_fusion.2.gtab_ref, bf16[32,512,512]{2,1,0:T(8,128)(2,1)} %bitcast.28), custom_call_target="tpu_custom_call" | custom-call | flops 4300000256 | bytes 16777216 | tf_op jit(solution)/shard_map/arrange_ints/pallas_call | solution.py:106
  127.5 3.2 %copy-done.2 = bf16[8,1024,512]{2,1,0:T(8,128)(2,1)} copy-done((bf16[8,1024,512]{2,1,0:T(8,128)(2,1)}, bf16[8,1024,512]{2,1,0:T(8,128)(2,1)S(1)}, u32[]{:S(2)}) %copy-start.2) | copy-done | bytes 8388632
  130.7 7.6 %ladder.1.acc_ref = f32[8,256,512]{2,1,0:T(8,128)S(1)} custom-call(s32[32]{0:T(128)S(1)} %copy-done.7, bf16[16,4,8,32,128]{4,3,2,1,0:T(8,128)(2,1)} %all-to-all-done.1.r_ref, bf16[8,256,128]{2,1,0:T(8,128)(2,1)S(1)} %copy.38.pick_ref, bf16[8,1024,512]{2,1,0:T(8,128)(2,1)S(1)} %arrange_ints.3.ints_ref), custom_call_target="tpu_custom_call" | custom-call | flops 2700000000 | bytes 14680064 | tf_op jit(solution)/shard_map/ladder/pallas_call | solution.py:218
  138.4 1.9 copy-done.4
  140.3 3.4 %copy-done.3 = bf16[8,1024,512]{2,1,0:T(8,128)(2,1)S(1)} copy-done((bf16[8,1024,512]{2,1,0:T(8,128)(2,1)S(1)}, bf16[8,1024,512]{2,1,0:T(8,128)(2,1)}, u32[]{:S(2)}) %copy-start.3) | copy-done | bytes 8388632
  143.7 2.2 %copy-done.5 = f32[8,256,512]{2,1,0:T(8,128)S(1)} copy-done((f32[8,256,512]{2,1,0:T(8,128)S(1)}, f32[8,256,512]{2,1,0:T(8,128)}, u32[]{:S(2)}) %copy-start.5) | copy-done | bytes 4194328
  145.9 11.0 %last_ladder.1 = (f32[16,32,512]{2,1,0:T(8,128)S(1)}, f32[16,32,512]{2,1,0:T(8,128)}) custom-call(s32[32]{0:T(128)S(1)} %copy-done.7, s32[1]{0:T(128)} %bitcast.1.core_ref, bf16[16,4,8,32,128]{4,3,2,1,0:T(8,128)(2,1)} %all-to-all-done.r_ref, bf16[8,256,128]{2,1,0:T(8,128)(2,1)S(1)} %copy.38.pick_ref, bf16[8,1024,512]{2,1,0:T(8,128)(2,1)S(1)} %copy-done.3, ...), custom_call_target="tpu_custom_call" | custom-call | flops 2700000000 | bytes 14680064 | tf_op jit(solution)/shard_map/last_ladder/pallas_call | solution.py:237
  156.9 1.0 copy-done.6
  157.8 2.8 %collective-permute-start = (f32[16,32,512]{2,1,0:T(8,128)}, f32[16,32,512]{2,1,0:T(8,128)S(1)}, u32[]{:S(2)}, u32[]{:S(2)}) collective-permute-start(f32[16,32,512]{2,1,0:T(8,128)} %get-tuple-element.9), channel_id=1, source_target_pairs={{0,1},{1,0},{2,3},{3,2},{4,5},{5,4},{6,7},{7,6},{8,9},{9,8},{10,11... | collective-permute-start | bytes 3145736 | tf_op jit(solution)/shard_map/ppermute | solution.py:357
  160.6 0.6 gather_fusion.1
  161.2 0.7 gather_fusion.2
  162.1 0.7 gather_fusion.4
  162.9 0.2 collective-permute-done
  163.1 2.5 %add.74 = f32[16,32,512]{2,1,0:T(8,128)} add(f32[16,32,512]{2,1,0:T(8,128)} %copy-done.6, f32[16,32,512]{2,1,0:T(8,128)S(1)} %collective-permute-done) | non-fusion elementwise | flops 262144 | bytes 3145728 | tf_op jit(solution)/shard_map/add | solution.py:358
  165.6 6.9 %all-to-all-start.2 = ((f32[16,32,512]{2,1,0:T(8,128)}), f32[16,32,512]{2,1,0:T(8,128)S(1)}, u32[]{:S(2)}, u32[]{:S(2)}) async-start(f32[16,32,512]{2,1,0:T(8,128)} %add.74), calls=%async_computation.2 | async-start | bytes 2097152 | tf_op jit(solution)/shard_map/all_to_all | solution.py:358
  172.5 0.3 select_reduce_fusion.ltab_ref
  172.9 14.6 %all-to-all-done.2.x_ref = f32[16,32,512]{2,1,0:T(8,128)S(1)} async-done(((f32[16,32,512]{2,1,0:T(8,128)}), f32[16,32,512]{2,1,0:T(8,128)S(1)}, u32[]{:S(2)}, u32[]{:S(2)}) %all-to-all-start.2) | async-done | bytes 1048608 | tf_op jit(solution)/shard_map/all_to_all | solution.py:358
  187.5 1.5 by_run.1
  189.0 8.1 %all-to-all-start.3 = ((f32[8,8,512]{2,1,0:T(8,128)}), f32[8,8,512]{2,1,0:T(8,128)S(1)}, u32[]{:S(2)}, u32[]{:S(2)}) async-start(f32[8,8,512]{2,1,0:T(8,128)} %by_run.1), calls=%async_computation.3 | async-start | bytes 262144 | tf_op jit(solution)/shard_map/all_to_all | solution.py:370
  197.0 5.3 %all-to-all-done.3.x_ref = f32[8,8,512]{2,1,0:T(8,128)S(1)} async-done(((f32[8,8,512]{2,1,0:T(8,128)}), f32[8,8,512]{2,1,0:T(8,128)S(1)}, u32[]{:S(2)}, u32[]{:S(2)}) %all-to-all-start.3) | async-done | bytes 131104 | tf_op jit(solution)/shard_map/all_to_all | solution.py:370
  202.4 1.5 finish.1
  (57 shorter events, 1.3 us)
Async XLA Ops:
  0.0 15.2 %copy-start = (s32[64]{0:T(128)S(1)}, s32[64]{0:T(128)}, u32[]{:S(2)}) copy-start(s32[64]{0:T(128)} %param.19) | copy-start | bytes 772
  6.5 8.7 %copy-start.12 = (s32[32]{0:T(128)S(1)}, s32[32]{0:T(128)}, u32[]{:S(2)}) copy-start(s32[32]{0:T(128)} %param.22) | copy-start | bytes 388
  6.6 9.4 %copy-start.7 = (s32[32]{0:T(128)S(1)}, s32[32]{0:T(128)}, u32[]{:S(2)}) copy-start(s32[32]{0:T(128)} %iorb_ref.3) | copy-start | bytes 388
  6.6 10.3 %copy-start.11 = (s32[8]{0:T(128)S(1)}, s32[8]{0:T(128)}, u32[]{:S(2)}) copy-start(s32[8]{0:T(128)} %param.23) | copy-start | bytes 100
  6.6 70.1 %all-to-all-start.1 = ((bf16[16,4,8,32,128]{4,3,2,1,0:T(8,128)(2,1)}), bf16[16,4,8,32,128]{4,3,2,1,0:T(8,128)(2,1)}, u32[]{:S(2)}, u32[]{:S(2)}) async-start(bf16[16,4,8,32,128]{4,3,2,1,0:T(8,128)(2,1)} %pack.3), calls=%async_computation.1 | async-start | bytes 8388608 | tf_op jit(solution)/shard_map/all_to_all | solution.py:330
  23.8 63.3 %copy-start.9 = (s32[512]{0:T(512)S(1)}, s32[512]{0:T(512)}, u32[]{:S(2)}) copy-start(s32[512]{0:T(512)} %param.20) | copy-start | bytes 6148
  76.7 63.6 %all-to-all-start = ((bf16[16,4,8,32,128]{4,3,2,1,0:T(8,128)(2,1)}), bf16[16,4,8,32,128]{4,3,2,1,0:T(8,128)(2,1)}, u32[]{:S(2)}, u32[]{:S(2)}) async-start(bf16[16,4,8,32,128]{4,3,2,1,0:T(8,128)(2,1)} %pack.2), calls=%async_computation | async-start | bytes 8388608 | tf_op jit(solution)/shard_map/all_to_all | solution.py:330
  86.5 7.6 %copy-start.13 = (bf16[32,8,4,512]{3,2,1,0:T(4,128)(2,1)S(1)}, bf16[32,8,4,512]{3,2,1,0:T(4,128)(2,1)}, u32[]{:S(2)}) copy-start(bf16[32,8,4,512]{3,2,1,0:T(4,128)(2,1)} %param.16) | copy-start | bytes 3145732
  127.5 3.3 %copy-start.2 = (bf16[8,1024,512]{2,1,0:T(8,128)(2,1)}, bf16[8,1024,512]{2,1,0:T(8,128)(2,1)S(1)}, u32[]{:S(2)}) copy-start(bf16[8,1024,512]{2,1,0:T(8,128)(2,1)S(1)} %arrange_ints.2.ints_ref) | copy-start | bytes 25165828
  138.3 1.9 copy-start.4
  140.3 3.4 %copy-start.3 = (bf16[8,1024,512]{2,1,0:T(8,128)(2,1)S(1)}, bf16[8,1024,512]{2,1,0:T(8,128)(2,1)}, u32[]{:S(2)}) copy-start(bf16[8,1024,512]{2,1,0:T(8,128)(2,1)} %copy-done.2) | copy-start | bytes 25165828
  143.7 2.2 %copy-start.5 = (f32[8,256,512]{2,1,0:T(8,128)S(1)}, f32[8,256,512]{2,1,0:T(8,128)}, u32[]{:S(2)}) copy-start(f32[8,256,512]{2,1,0:T(8,128)} %copy-done.4) | copy-start | bytes 12582916
  145.9 14.8 %copy-start.8 = (f32[64]{0:T(128)S(1)}, f32[64]{0:T(128)}, u32[]{:S(2)}) copy-start(f32[64]{0:T(128)} %param.17) | copy-start | bytes 772
  145.9 16.2 %copy-start.10 = (f32[512]{0:T(512)S(1)}, f32[512]{0:T(512)}, u32[]{:S(2)}) copy-start(f32[512]{0:T(512)} %param.18) | copy-start | bytes 6148
  156.8 1.0 copy-start.6
  157.8 5.3 %collective-permute-start = (f32[16,32,512]{2,1,0:T(8,128)}, f32[16,32,512]{2,1,0:T(8,128)S(1)}, u32[]{:S(2)}, u32[]{:S(2)}) collective-permute-start(f32[16,32,512]{2,1,0:T(8,128)} %get-tuple-element.9), channel_id=1, source_target_pairs={{0,1},{1,0},{2,3},{3,2},{4,5},{5,4},{6,7},{7,6},{8,9},{9,8},{10,11... | collective-permute-start | bytes 3145736 | tf_op jit(solution)/shard_map/ppermute | solution.py:357
  160.6 43.3 %copy-start.1 = (s32[64]{0:T(128)S(1)}, s32[64]{0:T(128)}, u32[]{:S(2)}) copy-start(s32[64]{0:T(128)} %param.19) | copy-start | bytes 772
  165.6 21.9 %all-to-all-start.2 = ((f32[16,32,512]{2,1,0:T(8,128)}), f32[16,32,512]{2,1,0:T(8,128)S(1)}, u32[]{:S(2)}, u32[]{:S(2)}) async-start(f32[16,32,512]{2,1,0:T(8,128)} %add.74), calls=%async_computation.2 | async-start | bytes 2097152 | tf_op jit(solution)/shard_map/all_to_all | solution.py:358
  189.0 13.3 %all-to-all-start.3 = ((f32[8,8,512]{2,1,0:T(8,128)}), f32[8,8,512]{2,1,0:T(8,128)S(1)}, u32[]{:S(2)}, u32[]{:S(2)}) async-start(f32[8,8,512]{2,1,0:T(8,128)} %by_run.1), calls=%async_computation.3 | async-start | bytes 262144 | tf_op jit(solution)/shard_map/all_to_all | solution.py:370

commit v3 on v2

v3 whole, which is shorter than its diff:
```python
import functools

import jax
import jax.numpy as jnp
import numpy as np
from jax import lax
from jax.experimental import pallas as pl
from jax.experimental.pallas import tpu as pltpu
from jax.sharding import PartitionSpec as P

F32 = jnp.float32
BF16 = jnp.bfloat16
VMEM = 50 * 1024 * 1024

NO, NV, OI, OJ, SA = 64, 512, 32, 32, 8
ROWS, COLS, RUN = 16, 8, 64
PIECES = 2
DP = 64 // PIECES
QP = DP // 4
KP = DP * 32


def params(n=1):
    return pltpu.CompilerParams(
        dimension_semantics=("arbitrary",) * n, vmem_limit_bytes=VMEM
    )


def in_hbm(x):
    return pltpu.with_memory_space_constraint(x, pltpu.HBM)


def in_vmem(x):
    return pltpu.with_memory_space_constraint(x, pltpu.VMEM)


def cost(flops, nbytes):
    return pl.CostEstimate(flops=0, bytes_accessed=1024, transcendentals=0)


def after(values, *others):
    return lax.optimization_barrier((tuple(values), tuple(others)))[0]


def lane_swap():
    out = np.zeros((4, 4, 4, 32, 4, 4, 32), np.float32)
    for first in range(4):
        for e in range(4):
            for z in range(4):
                for c in range(32):
                    out[first, e, z, c, (z - first) % 4, e, c] = 1
    return out.reshape(4, 512, 512).astype(jnp.bfloat16)


def pack_kernel(piece, tab_ref, amp_ref, lanes_ref, *rest):
    outs, mid_ref = rest[:4], rest[4]
    for jh in range(2):
        rows = slice(16 * jh, 16 * jh + 16)
        for dh in range(DP // 16):
            y = jnp.swapaxes(amp_ref[0, rows, 16 * dh : 16 * dh + 16, :], 0, 1)
            for x in range(4):
                to = x if piece else (x - tab_ref[4]) & 3
                for q in range(4):
                    for e in range(4):
                        mid_ref[to, 4 * dh + q, rows, 128 * e : 128 * e + 128] = y[
                            4 * q + e, :, 128 * x : 128 * x + 128
                        ]
    w = jnp.dot(mid_ref[...].reshape(4 * QP * OJ, 512), lanes_ref[0], preferred_element_type=F32)
    w = w.astype(BF16).reshape(4, QP, OJ, 512)
    for x in range(4):
        for z in range(4):
            block = w[x, :, :, 128 * z : 128 * z + 128]
            if piece:
                outs[z][x, 0] = block
            else:
                outs[x][z, 0] = block


def pack(amp_t, piece, slots, tab):
    return pl.pallas_call(
        functools.partial(pack_kernel, piece),
        grid_spec=pltpu.PrefetchScalarGridSpec(
            num_scalar_prefetch=1,
            grid=(slots,),
            in_specs=[
                pl.BlockSpec((1, OJ, DP, NV), lambda s, tab: (tab[s], 0, piece, 0)),
                pl.BlockSpec((1, 512, 512), lambda s, tab: (tab[5] * piece, 0, 0)),
            ],
            out_specs=[pl.BlockSpec((4, 1, QP, OJ, 128), lambda s, tab: (0, s, 0, 0, 0))] * 4,
            scratch_shapes=[pltpu.VMEM((4, QP, OJ, 512), BF16)],
        ),
        out_shape=[pltpu.HBM((4, slots, QP, OJ, 128), BF16)] * 4,
        compiler_params=params(),
        cost_estimate=cost(8_000_000_000 // PIECES, 2 * 8 * 2**20 // PIECES),
        name="pack",
    )(tab, in_hbm(amp_t), in_hbm(jnp.asarray(lane_swap())))


def regroup_kernel(count, tab_ref, *refs):
    got, outs, (buf_ref, sems, out_sems) = refs[:4], refs[4:8], refs[8:]

    def copy(n, away, rel):
        src = got[away].at[(tab_ref[2, n] + rel) & 3, tab_ref[1, n]]
        return pltpu.make_async_copy(src, buf_ref.at[rel, n], sems.at[rel, n])

    def ship(rel):
        return pltpu.make_async_copy(buf_ref.at[rel], outs[rel], out_sems.at[rel])

    def start(n, carry):
        for away in range(4):

            @pl.when(tab_ref[0, n] == away)
            def _():
                for rel in range(4):
                    copy(n, away, rel).start()

        return carry

    lax.fori_loop(0, count, start, 0)
    for rel in range(4):

        def arrive(n, carry):
            copy(n, 0, rel).wait()
            return carry

        lax.fori_loop(0, count, arrive, 0)
        ship(rel).start()
    for rel in range(4):
        ship(rel).wait()


def regroup(tab, got):
    count = tab.shape[1]
    hbm = pl.BlockSpec(memory_space=pltpu.HBM)
    return pl.pallas_call(
        functools.partial(regroup_kernel, count),
        in_specs=[pl.BlockSpec(memory_space=pltpu.SMEM)] + [hbm] * 4,
        out_specs=[hbm] * 4,
        out_shape=[pltpu.HBM((count, QP, OJ, 128), BF16)] * 4,
        scratch_shapes=[
            pltpu.VMEM((4, count, QP, OJ, 128), BF16),
            pltpu.SemaphoreType.DMA((4, count)),
            pltpu.SemaphoreType.DMA((4,)),
        ],
        compiler_params=pltpu.CompilerParams(vmem_limit_bytes=VMEM),
        cost_estimate=cost(0, 16 * count * 2**15),
        name="regroup",
    )(tab, *[in_hbm(x) for x in got])


def move(x, n, along_x):
    dx, dz = (n, 0) if along_x else (0, n)
    pairs = [(4 * a + b, 4 * ((a + dx) % 4) + (b + dz) % 4) for a in range(4) for b in range(4)]
    return lax.ppermute(x, "row", pairs)


IN_STEP = 8


def ints_kernel(gtab_ref, v_ref, out_ref):
    for dd in range(IN_STEP // 2):
        for ch in range(2):
            x = v_ref[16 * ch : 16 * ch + 16, 16 * dd : 16 * dd + 16, :]
            y = jnp.swapaxes(x, 0, 1)
            for d in range(2):
                row = 64 * dd + 32 * d + 16 * ch
                for a in range(SA):
                    off = 64 * (a % 2)
                    for t in range(4):
                        tile = y[8 * d + a, :, 128 * t : 128 * t + 128]
                        for e in range(2):
                            part = tile[:, 64 * e : 64 * e + 64]
                            out_ref[0, gtab_ref[a, 2 * t + e], row : row + 16, 64 * a : 64 * a + 64] = part


def arrange_ints(first, pieces, gtab, ints, space):
    steps = DP // IN_STEP
    return pl.pallas_call(
        ints_kernel,
        grid_spec=pltpu.PrefetchScalarGridSpec(
            num_scalar_prefetch=1,
            grid=(steps * pieces,),
            in_specs=[pl.BlockSpec((32, 8 * IN_STEP, NV), lambda s, *_: (0, first * steps + s, 0))],
            out_specs=pl.BlockSpec(
                (1, 8, 32 * IN_STEP, NV), lambda s, *_: (s // steps, 0, s % steps, 0)
            ),
        ),
        out_shape=space((pieces, 8, KP, SA * RUN), BF16),
        compiler_params=params(),
        cost_estimate=cost(0, pieces * 8 * 2**20),
        name="arrange_ints",
    )(gtab, in_hbm(ints))


def two_terms(x):
    hi = x.astype(BF16)
    return hi, (x - hi.astype(F32)).astype(BF16)


def ladder_kernel(where_ref, core_ref, *refs):
    r_refs, ints_refs, (cycle_hbm, pick_ref, drop_ref) = refs[:8], refs[8:10], refs[10:13]
    keep_ref, send_ref, rows_ref, slab_ref, ints_ref, cycle_ref, sum_ref, sems, ints_sems, cycle_sem = refs[13:]
    core = core_ref[0]

    def copy(p, piece, away):
        src = r_refs[4 * piece + away].at[where_ref[2 * piece + 1, p]]
        return pltpu.make_async_copy(src, slab_ref.at[p, piece], sems.at[p, piece])

    def copy_ints(g, piece):
        return pltpu.make_async_copy(ints_refs[piece].at[0, g], ints_ref.at[piece, g], ints_sems.at[piece, g])

    copy_cycle = pltpu.make_async_copy(cycle_hbm, cycle_ref, cycle_sem)

    def start(p, carry):
        for piece in range(PIECES):
            for away in range(4):

                @pl.when(where_ref[2 * piece, p] == away)
                def _():
                    copy(p, piece, away).start()

        return carry

    def sort(blk, carry):
        for i in range(4):
            for piece in range(PIECES):
                copy(4 * blk + i, piece, 0).wait()
        x = jnp.concatenate(
            [
                jnp.concatenate(
                    [slab_ref[4 * blk + i, piece, q] for piece in range(PIECES) for q in range(QP)], axis=1
                )
                for i in range(4)
            ],
            axis=0,
        )
        y = jnp.dot(pick_ref[blk], x, preferred_element_type=F32).astype(BF16)
        rows_ref[:, pl.ds(pl.multiple_of(32 * blk, 32), 32), :] = y.reshape(8, 32, PIECES * KP)
        return carry

    def group(g, carry):
        for piece in range(PIECES):
            copy_ints(g, piece).wait()
        sum_ref[g] = sum(
            jnp.dot(
                rows_ref[g, :, KP * piece : KP * piece + KP], ints_ref[piece, g], preferred_element_type=F32
            )
            for piece in range(PIECES)
        )
        return carry

    def unsort(blk, carry):
        x = sum_ref[:, pl.ds(pl.multiple_of(32 * blk, 32), 32), :].reshape(256, SA * RUN)
        hi, lo = two_terms(x)
        y = jnp.dot(drop_ref[blk], hi, preferred_element_type=F32)
        y = y + jnp.dot(drop_ref[blk], lo, preferred_element_type=F32)
        for i in range(4):
            got = y[32 * i : 32 * i + 32, :] + cycle_ref[4 * blk + i]

            @pl.when(core == i % 2)
            def _():
                keep_ref[2 * blk + i // 2] = got

            @pl.when(core != i % 2)
            def _():
                send_ref[2 * blk + i // 2] = got

        return carry

    lax.fori_loop(0, OI, start, 0)
    for g in range(8):
        for piece in range(PIECES):
            copy_ints(g, piece).start()
    copy_cycle.start()
    lax.fori_loop(0, 8, sort, 0)
    lax.fori_loop(0, 8, group, 0)
    copy_cycle.wait()
    lax.fori_loop(0, 8, unsort, 0)


def ladder(where, core, arrived, pick, early, late, drop, cyc):
    smem = pl.BlockSpec(memory_space=pltpu.SMEM)
    vmem = pl.BlockSpec(memory_space=pltpu.VMEM)
    hbm = pl.BlockSpec(memory_space=pltpu.HBM)
    return pl.pallas_call(
        ladder_kernel,
        in_specs=[smem] * 2 + [hbm] * 11 + [vmem] * 2,
        out_specs=[vmem] * 2,
        out_shape=[jax.ShapeDtypeStruct((16, OJ, 512), F32)] * 2,
        scratch_shapes=[
            pltpu.VMEM((8, 256, PIECES * KP), BF16),
            pltpu.VMEM((OI, PIECES, QP, OJ, 128), BF16),
            pltpu.VMEM((PIECES, 8, KP, 512), BF16),
            pltpu.VMEM((OI, OJ, 512), F32),
            pltpu.VMEM((8, 256, 512), F32),
            pltpu.SemaphoreType.DMA((OI, PIECES)),
            pltpu.SemaphoreType.DMA((PIECES, 8)),
            pltpu.SemaphoreType.DMA(()),
        ],
        compiler_params=pltpu.CompilerParams(vmem_limit_bytes=VMEM),
        cost_estimate=cost(5_400_000_000, 30 * 2**20),
        name="ladder",
    )(where, core, *[in_hbm(x) for x in (*arrived, early, late, cyc)], pick, drop)


def cycle_kernel(ovov_ref, amp_ref, want_ref, sym_ref, out_ref, mid_ref, turn_ref):
    acc = None
    for k in range(4):
        part = lax.dot_general(
            ovov_ref[:, NV * k : NV * k + NV],
            amp_ref[k].reshape(512, NV),
            (((1,), (1,)), ((), ())),
            preferred_element_type=F32,
        )
        acc = part if acc is None else acc + part
    low = lax.broadcasted_iota(jnp.int32, (OI, 128), 1) < 64
    for t in range(4):
        mid_ref[t] = acc[:, 128 * t : 128 * t + 128]
    for t in range(4):
        keep = [
            jnp.broadcast_to(want_ref[2 * t + e], (OI, 128)) for e in range(2)
        ]
        for m in range(4):
            x0 = mid_ref[t, pl.ds(2 * m, OI, stride=SA), :]
            x1 = mid_ref[t, pl.ds(2 * m + 1, OI, stride=SA), :]
            sym = sym_ref[0:1, 128 * m : 128 * m + 128]
            y0 = jnp.where(low, x0, pltpu.roll(x1, 64, 1))
            y1 = jnp.where(low, pltpu.roll(x0, 64, 1), x1)
            turn_ref[m, pl.ds(2 * t, OI, stride=8), :] = jnp.where(keep[0] == sym, y0, 0.0)
            turn_ref[m, pl.ds(2 * t + 1, OI, stride=8), :] = jnp.where(keep[1] == sym, y1, 0.0)
    for m in range(4):
        out_ref[:, :, 128 * m : 128 * m + 128] = turn_ref[m].reshape(OI, 8, 128)


def cycle_term(ovov, amp_t, want, sym):
    return pl.pallas_call(
        cycle_kernel,
        grid=(4,),
        in_specs=[
            pl.BlockSpec((OI * SA, 4 * NV), lambda s: (0, 0)),
            pl.BlockSpec((4, 8, RUN, NV), lambda s: (0, s, 0, 0)),
            pl.BlockSpec((8, OI, 1), lambda s: (s, 0, 0)),
            pl.BlockSpec((8, 512), lambda s: (0, 0)),
        ],
        out_specs=pl.BlockSpec((OI, 8, 512), lambda s: (0, s, 0)),
        out_shape=jax.ShapeDtypeStruct((OI, OJ, 512), F32),
        scratch_shapes=[pltpu.VMEM((4, OI * SA, 128), F32), pltpu.VMEM((4, OI * 8, 128), F32)],
        compiler_params=params(),
        cost_estimate=cost(2_100_000_000, 11 * 2**20),
        name="cycle_term",
    )(in_hbm(ovov), in_hbm(amp_t), want, sym)


def by_run_kernel(ltab_ref, x_ref, spread_ref, out_ref):
    hi, lo = two_terms(jnp.sum(x_ref[...], axis=0))
    y = jnp.dot(spread_ref[...], hi, preferred_element_type=F32)
    y = y + jnp.dot(spread_ref[...], lo, preferred_element_type=F32)
    for a in range(SA):
        for t in range(8):
            out_ref[ltab_ref[a, t], :, 64 * a : 64 * a + 64] = y[8 * t : 8 * t + 8, 64 * a : 64 * a + 64]


def by_run(ltab, x, spread):
    return pl.pallas_call(
        by_run_kernel,
        grid_spec=pltpu.PrefetchScalarGridSpec(
            num_scalar_prefetch=1,
            grid=(1,),
            in_specs=[
                pl.BlockSpec((ROWS, OJ, 512), lambda s, *_: (0, 0, 0)),
                pl.BlockSpec((64, OJ), lambda s, *_: (0, 0)),
            ],
            out_specs=pl.BlockSpec((8, 8, 512), lambda s, *_: (0, 0, 0)),
        ),
        out_shape=jax.ShapeDtypeStruct((8, 8, 512), F32),
        compiler_params=params(),
        name="by_run",
    )(ltab, x, spread)


def finish_kernel(slot_ref, irr_ref, energy_ref, x_ref, va_ref, vb_ref, sa_ref, sb_ref, out_ref, tile_ref):
    for h in range(2):
        v = x_ref[h]
        for y in range(1, 4):
            v = v + x_ref[2 * y + h]
        for a in range(SA):
            tile_ref[h, :, a, :] = v[:, 64 * a : 64 * a + 64]
    sym_ab = jnp.bitwise_xor(sa_ref[...], sb_ref[...])
    for h in range(2):
        for j in range(OJ):
            got = tile_ref[h, slot_ref[j]]
            den = energy_ref[h, j] - va_ref[...] - vb_ref[...]
            ok = jnp.bitwise_xor(sym_ab, irr_ref[h, j]) == 0
            out_ref[h, j] = jnp.where(ok, got / den, jnp.zeros_like(got))


def finish(slot, irr, energy, x, va, vb, sa, sb):
    full = lambda *dims: pl.BlockSpec(dims, lambda s, *_: (0,) * len(dims))
    return pl.pallas_call(
        finish_kernel,
        grid_spec=pltpu.PrefetchScalarGridSpec(
            num_scalar_prefetch=3,
            grid=(1,),
            in_specs=[full(8, 8, 512), full(8, 64), full(8, 64), full(8, 64), full(8, 64)],
            out_specs=full(2, OJ, SA, RUN),
            scratch_shapes=[pltpu.VMEM((2, 8, SA, RUN), F32)],
        ),
        out_shape=jax.ShapeDtypeStruct((2, OJ, SA, RUN), F32),
        compiler_params=params(),
        name="finish",
    )(slot, irr, energy, x, va, vb, sa, sb)


def body(
    slots,
    count,
    amplitudes,
    vvvv_ints,
    ovov_ints,
    occ_energy,
    vir_energy,
    occ_irrep,
    vir_irrep,
    i_orbitals,
    j_orbitals,
    a_orbitals,
):
    row = lax.axis_index("row")
    col = lax.axis_index("col")
    core = lax.rem(col, 2)
    labels = jnp.arange(8, dtype=jnp.int32)
    amp_t = amplitudes.transpose(0, 1, 3, 2)

    x_pos, z_pos = row // 4, row % 4
    lane = jnp.arange(4, dtype=jnp.int32)
    is_i = i_orbitals[:, None] == jnp.arange(NO)
    chosen = is_i.any(axis=0).reshape(4, 4, 4)
    if slots == 4:
        slot_of = jnp.broadcast_to(lane, (4, 4, 4))
        ktab = lane
    else:
        slot_of = jnp.sum(chosen[:, :, None, :] & (lane[:, None] > lane), axis=-1).astype(jnp.int32)
        own = lambda x: lax.dynamic_index_in_dim(x.reshape(ROWS, 4), row, keepdims=False)
        ktab = jnp.sum(jnp.where(own(chosen) & (own(slot_of) == lane[:, None]), lane, 0), axis=-1)
    ptab = jnp.concatenate([ktab, jnp.stack([x_pos, z_pos])]).astype(jnp.int32)
    packed = pack(amp_t, 1, slots, ptab)
    second = {n: move(packed[n], n, False) for n in (1, 3)}
    sent = [pack(amp_t, 0, slots, *after([ptab], packed[0])), packed]
    first = {n: move(sent[0][n], n, True) for n in (1, 3, 2)}

    line_before = jnp.arange(16)[:, None] > jnp.arange(16)
    others = jnp.arange(16, dtype=jnp.int32) // 4
    tabs, where = [], []
    for piece in range(2):
        mine, other = (x_pos, z_pos) if piece else (z_pos, x_pos)
        by_line = lambda x: (x if piece else x.transpose(1, 0, 2)).reshape(4, 16)
        line = by_line(chosen)
        rank = jnp.sum(line[:, None, :] & line_before, axis=-1).astype(jnp.int32)
        here, here_rank, here_slot = [
            lax.dynamic_index_in_dim(x, mine, keepdims=False) for x in (line, rank, by_line(slot_of))
        ]
        nth = here & (here_rank == jnp.arange(count)[:, None])
        nth_other = jnp.sum(jnp.where(nth, others, 0), axis=-1)
        nth_slot = jnp.sum(jnp.where(nth, here_slot, 0), axis=-1)
        tabs.append(jnp.stack([(other - nth_other) & 3, nth_slot, jnp.full_like(nth_slot, mine)]).astype(jnp.int32))
        rank = rank.reshape(4, 4, 4)
        rank = (rank if piece else rank.transpose(1, 0, 2)).reshape(NO)
        away = (mine - (i_orbitals // (16 if piece else 4)) % 4) & 3
        where.append(jnp.stack([away, jnp.sum(jnp.where(is_i, rank, 0), axis=-1)]).astype(jnp.int32))

    sym_i = jnp.take(occ_irrep, i_orbitals)
    sym_j = jnp.take(occ_irrep, j_orbitals)
    sym_a = jnp.take(vir_irrep, a_orbitals)
    run_label = vir_irrep.reshape(8, RUN)[:, 0]
    slot = j_orbitals % 8
    gtab = jnp.bitwise_xor(sym_a[:, None], run_label[None, :])
    g_ij = jnp.bitwise_xor(sym_i[:, None], sym_j[None, :])
    hit = (g_ij[:, :, None, None] == labels[:, None]) & (slot[:, None, None] == labels)
    hit = hit.reshape(8, 4, OJ, 8, 8)
    same = (jnp.arange(4)[:, None] == jnp.arange(4)).reshape(1, 4, 1, 1, 4, 1)
    drop = (hit[:, :, :, :, None, :] & same).reshape(8, 128, 256).astype(BF16)
    pick = drop.transpose(0, 2, 1)
    mine_label = lax.dynamic_index_in_dim(run_label, col, keepdims=False)
    want = jnp.bitwise_xor(g_ij.T, mine_label)[:, :, None]
    sym_lanes = jnp.broadcast_to(jnp.repeat(sym_a, RUN)[None, :], (8, SA * RUN))

    mine_i = lax.dynamic_slice_in_dim(i_orbitals, 2 * row, 2)
    sym_mine = jnp.take(occ_irrep, mine_i)
    label_at = jnp.bitwise_xor(
        jnp.bitwise_xor(lax.dynamic_index_in_dim(sym_mine, core, keepdims=False), sym_a)[:, None],
        labels[None, :],
    )
    ltab = jnp.sum(jnp.where(label_at[..., None] == run_label, labels, 0), axis=-1).astype(jnp.int32)
    spread = (
        (sym_j[None, None, :] == labels[:, None, None]) & (slot[None, None, :] == labels[None, :, None])
    ).reshape(64, OJ).astype(BF16)
    energy = jnp.take(occ_energy, mine_i)[:, None] + jnp.take(occ_energy, j_orbitals)[None, :]
    irr = jnp.bitwise_xor(sym_mine[:, None], sym_j[None, :])
    wide = lambda x: jnp.broadcast_to(x, (SA, RUN))
    va = wide(jnp.take(vir_energy, a_orbitals)[:, None])
    vb = wide(lax.dynamic_slice_in_dim(vir_energy, col * RUN, RUN)[None, :])
    sa = wide(sym_a[:, None])
    sb = wide(lax.dynamic_slice_in_dim(vir_irrep, col * RUN, RUN)[None, :])
    tail = (ltab, spread, slot, irr, energy, va, vb, sa, sb)

    ints = vvvv_ints.reshape(32, 512, NV)
    (held,) = after([sent[1][2]], second[1], second[3])
    second[2] = move(held, 2, False)
    (want,) = after([want], second[1], second[3])
    cyc = cycle_term(ovov_ints.reshape(OI * SA, 4 * NV), amp_t, want, sym_lanes)
    (gate,) = after([gtab], cyc)
    early = arrange_ints(0, 1, gate, ints, pltpu.HBM)
    (tab1,) = after([tabs[1]], early, pick)
    packed1 = regroup(tab1, [sent[1][0], second[1], second[2], second[3]])
    (tab0,) = after([tabs[0]], packed1[0])
    packed0 = regroup(tab0, [sent[0][0], first[1], first[2], first[3]])
    sides1 = after([packed1[1], packed1[3]], first[1], first[2], first[3])
    arrived0 = {n: move(packed0[n], n, False) for n in (1, 3)}
    arrived1 = {n: move(x, n, True) for n, x in zip((1, 3), sides1)}
    (gate,) = after([gtab], packed0[0], *tail)
    late = arrange_ints(1, 1, gate, ints, pltpu.HBM)
    across0, across1 = after(
        [packed0[2], packed1[2]], late, list(arrived0.values()), list(arrived1.values())
    )
    arrived0[2] = move(across0, 2, False)
    arrived1[2] = move(across1, 2, True)
    keep, give = ladder(
        jnp.concatenate(where),
        core.reshape(1),
        [packed0[0], arrived0[1], arrived0[2], arrived0[3], packed1[0], arrived1[1], arrived1[2], arrived1[3]],
        pick, early, late, drop, cyc,
    )

    got = lax.ppermute(give, "col", [(q, q ^ 1) for q in range(COLS)])
    both = lax.all_to_all(keep + got, "row", split_axis=0, concat_axis=0, tiled=True)
    parts = lax.all_to_all(by_run(ltab, both, spread), "col", split_axis=0, concat_axis=0, tiled=True)
    return finish(slot, irr, energy, parts, va, vb, sa, sb)


def shards(*args):
    lines = jnp.stack([args[7] // 16, args[7] // 4 % 4])
    on_line = jnp.max(jnp.sum(lines[:, None, :] == jnp.arange(4)[:, None], axis=-1))
    return lax.cond(
        on_line > 12, functools.partial(body, 4, 16), functools.partial(body, 4, 12), *args
    )


def solution(mesh):
    return jax.shard_map(
        shards,
        mesh=mesh,
        in_specs=(
            P("row", None, None, "col"),
            P("row", "col", None, None),
            P(None, None, "row", None),
            P(),
            P(),
            P(),
            P(),
            P(),
            P(),
            P(),
        ),
        out_specs=P("row", None, None, "col"),
        check_vma=False,
    )
```

time: 205 us -> 174 us (0.85)
  waiting for transfers between devices: 72.9 us -> 28.1 us
  blocking collectives: 0 us -> 34.4 us
  local copies, waits for them, and re-layouts: 29.1 us -> 12.5 us
  Pallas kernels: 50.8 us -> 66.8 us
  starting transfers between devices: 36.1 us -> 24.6 us
  matrix products: 9.42 us -> 0 us
    all_to_all x4 -> x0, waiting for transfers between devices: 72.7 us -> none  [the longest x2 52.8 us: shards(): lax.all_to_all(sent, 'row', split_axis=0, concat_axis=0, tiled=True)]
    all_to_all x0 -> x2, blocking collectives: none -> 34.4 us  [the longest x1 22.8 us: body(): lax.all_to_all(keep + got, 'row', split_axis=0, concat_axis=0, tiled=True)]
    all_to_all x4 -> x0, starting transfers between devices: 33.3 us -> none  [the longest x2 18.4 us: shards(): lax.all_to_all(sent, 'row', split_axis=0, concat_axis=0, tiled=True)]
    ppermute x1 -> x13, waiting for transfers between devices: 0.2 us -> 28.1 us  [the longest x12 25.8 us: move(): return lax.ppermute(x, 'row', pairs)]
    ppermute x1 -> x13, starting transfers between devices: 2.79 us -> 24.6 us  [the longest x12 20.7 us: move(): return lax.ppermute(x, 'row', pairs)]
    pallas_call x4 -> x6, Pallas kernels: 31.7 us -> 45.2 us  [the longest x2 14.5 us: pack(): pl.pallas_call(functools.partial(pack_kernel, piece), grid_spec=pltpu.Pre...]
    unnamed x28 -> x2, local copies, waits for them, and re-layouts: 11.7 us -> 0.7 us
    dot_general x1 -> x0, matrix products: 9.42 us -> none  [shards(): jnp.einsum('iakc,kjcb->ijab', ovov_ints, amplitudes, preferred_element_ty...]
  transfers between devices with their start and end apart: 5 -> 13, of which waited for: 4 -> 7; matrix products, arithmetic and copies ran while one was open for 14% -> 9% of each run, Pallas kernels for 15% -> 23%
where the time goes in v3:
time: 174 us; the launch traced here: 173 us
  Pallas kernels  66.8 us (38%)
  blocking collectives  34.4 us (20%)
  waiting for transfers between devices  28.1 us (16%)
  starting transfers between devices  24.6 us (14%)
  local copies, waits for them, and re-layouts  12.5 us (7%)
  other arithmetic  5.34 us (3%)
    ppermute x12, waiting for transfers between devices, move(): return lax.ppermute(x, 'row', pairs)  25.8 us
    all_to_all x1, blocking collectives, body(): lax.all_to_all(keep + got, 'row', split_axis=0, concat_axis=0, tiled=True)  22.8 us
    ppermute x12, starting transfers between devices, move(): return lax.ppermute(x, 'row', pairs)  20.7 us
    pallas_call x2, Pallas kernels, arrange_ints(): pl.pallas_call(ints_kernel, grid_spec=pltpu.PrefetchScalarGridSpec(num_sc...  20 us
    pallas_call x2, Pallas kernels, pack(): pl.pallas_call(functools.partial(pack_kernel, piece), grid_spec=pltpu.Pre...  14.5 us
    pallas_call x1, Pallas kernels, ladder(): pl.pallas_call(ladder_kernel, in_specs=[smem] * 2 + [hbm] * 11 + [vmem] *...  14.1 us
    all_to_all x1, blocking collectives, body(): lax.all_to_all(by_run(ltab, both, spread), 'col', split_axis=0, concat_ax...  11.6 us
    pallas_call x2, Pallas kernels, regroup(): pl.pallas_call(functools.partial(regroup_kernel, count), in_specs=[pl.Blo...  9.89 us
  transfers between devices with their start and end apart: 13, of which 7 were waited for; matrix products, arithmetic and copies ran while one was open for 9% of the time, Pallas kernels for 23%

profile of v3, /device:TPU:1, one launch (start us, length us, event | category | flops | bytes accessed | tf_op | source)
XLA Modules:
  0.0 173.3 jit_solution(18142349600088091801)
XLA Ops:
  0.0 0.7 fusion.38
  0.8 0.6 reduce_max.9
  2.1 170.5 %conditional.1 = (f32[2,32,8,64]{3,2,1,0:T(8,128)S(1)}) conditional(s32[]{:T(128)} %convert_element_type.35, (s32[32]{0:T(128)}, s32[32]{0:T(128)}, s32[64]{0:T(128)}, f32[64]{0:T(128)}, s32[512]{0:T(512)}, /*index=5*/s32[8]{0:T(128)}, bf16[32,8,4,512]{3,2,1,0:T(4,128)(2,1)}, bf16[4,32,512,64]{2,3,1,0:T(8,128)(2,1)}, ...), branch_computations={%region_2.19_spmd, %region_13.30_spmd} | conditional | flops 901215 | bytes 87230584 | solution.py:543
  2.3 7.0 %pack.4 = (bf16[4,4,8,32,128]{4,3,2,1,0:T(8,128)(2,1)}, bf16[4,4,8,32,128]{4,3,2,1,0:T(8,128)(2,1)}, bf16[4,4,8,32,128]{4,3,2,1,0:T(8,128)(2,1)}, bf16[4,4,8,32,128]{4,3,2,1,0:T(8,128)(2,1)}) custom-call(s32[6]{0:T(128)S(1)} %pad_add_fusion.1.tab_ref, bf16[4,32,64,512]{3,2,1,0:T(8,128)(2,1)} %bitcast.96, bf16[4,512,512]{2,1,0:T(8,128)(2,1)} %get-tuple-element.83.lanes_ref), custom_call_target="tpu_custom_call" | custom-call | bytes 1024 | tf_op jit(solution)/shard_map/cond/branch_0_fun/pack/pallas_call | solution.py:80
  9.3 2.5 %collective-permute-start = (bf16[4,4,8,32,128]{4,3,2,1,0:T(8,128)(2,1)}, bf16[4,4,8,32,128]{4,3,2,1,0:T(8,128)(2,1)S(1)}, u32[]{:S(2)}, u32[]{:S(2)}) collective-permute-start(bf16[4,4,8,32,128]{4,3,2,1,0:T(8,128)(2,1)} %get-tuple-element.71), channel_id=1, source_target_pairs={{0,8},{8,16},{16,24},{24,0},{32,40},{40,48},{48,56},{56,32},{64,72... | collective-permute-start | bytes 3145736 | tf_op jit(solution)/shard_map/cond/branch_0_fun/ppermute | solution.py:154
  11.8 2.2 %collective-permute-start.1 = (bf16[4,4,8,32,128]{4,3,2,1,0:T(8,128)(2,1)}, bf16[4,4,8,32,128]{4,3,2,1,0:T(8,128)(2,1)}, u32[]{:S(2)}, u32[]{:S(2)}) collective-permute-start(bf16[4,4,8,32,128]{4,3,2,1,0:T(8,128)(2,1)} %get-tuple-element.72), channel_id=1, source_target_pairs={{0,24},{8,0},{16,8},{24,16},{32,56},{40,32},{48,40},{56,48},{64,88... | collective-permute-start | bytes 3145736 | tf_op jit(solution)/shard_map/cond/branch_0_fun/ppermute | solution.py:154
  14.1 7.5 %pack.5 = (bf16[4,4,8,32,128]{4,3,2,1,0:T(8,128)(2,1)}, bf16[4,4,8,32,128]{4,3,2,1,0:T(8,128)(2,1)}, bf16[4,4,8,32,128]{4,3,2,1,0:T(8,128)(2,1)}, bf16[4,4,8,32,128]{4,3,2,1,0:T(8,128)(2,1)}) custom-call(s32[6]{0:T(128)S(1)} %pad_add_fusion.1.tab_ref, bf16[4,32,64,512]{3,2,1,0:T(8,128)(2,1)} %bitcast.97, bf16[4,512,512]{2,1,0:T(8,128)(2,1)} %get-tuple-element.83.lanes_ref), custom_call_target="tpu_custom_call" | custom-call | bytes 1024 | tf_op jit(solution)/shard_map/cond/branch_0_fun/pack/pallas_call | solution.py:80
  21.5 1.2 collective-permute-start.3
  22.8 2.5 %collective-permute-start.4 = (bf16[4,4,8,32,128]{4,3,2,1,0:T(8,128)(2,1)}, bf16[4,4,8,32,128]{4,3,2,1,0:T(8,128)(2,1)}, u32[]{:S(2)}, u32[]{:S(2)}) collective-permute-start(bf16[4,4,8,32,128]{4,3,2,1,0:T(8,128)(2,1)} %get-tuple-element.86), channel_id=1, source_target_pairs={{0,64},{8,72},{16,80},{24,88},{32,96},{40,104},{48,112},{56,120},{... | collective-permute-start | bytes 3145736 | tf_op jit(solution)/shard_map/cond/branch_0_fun/ppermute | solution.py:154
  25.3 1.1 collective-permute-start.5
  27.0 0.6 gather_fusion.6
  27.7 0.7 gather_fusion.4
  28.4 0.6 gather_fusion.2
  29.1 0.6 gather_fusion
  29.7 0.7 gather_fusion.5
  30.4 0.7 gather_fusion.3
  31.1 0.7 gather_fusion.1
  32.2 0.6 dynamic_slice.49
  32.8 0.6 broadcast_xor_fusion.3
  34.9 2.3 %collective-permute-done.refs_1_ = bf16[4,4,8,32,128]{4,3,2,1,0:T(8,128)(2,1)S(1)} collective-permute-done((bf16[4,4,8,32,128]{4,3,2,1,0:T(8,128)(2,1)}, bf16[4,4,8,32,128]{4,3,2,1,0:T(8,128)(2,1)S(1)}, u32[]{:S(2)}, u32[]{:S(2)}) %collective-permute-start) | collective-permute-done | bytes 1048608 | tf_op jit(solution)/shard_map/cond/branch_0_fun/ppermute | solution.py:154
  37.2 2.0 %collective-permute-start.2 = (bf16[4,4,8,32,128]{4,3,2,1,0:T(8,128)(2,1)}, bf16[4,4,8,32,128]{4,3,2,1,0:T(8,128)(2,1)}, u32[]{:S(2)}, u32[]{:S(2)}) collective-permute-start(bf16[4,4,8,32,128]{4,3,2,1,0:T(8,128)(2,1)} %get-tuple-element.79), channel_id=1, source_target_pairs={{0,16},{8,24},{16,0},{24,8},{32,48},{40,56},{48,32},{56,40},{64,80... | collective-permute-start | bytes 3145736 | tf_op jit(solution)/shard_map/cond/branch_0_fun/ppermute | solution.py:154
  39.7 0.7 and.330
  40.4 1.3 and.331
  42.1 1.3 copy.59
  43.4 0.5 constant_dynamic-slice_fusion
  44.1 0.8 xor_xor_fusion.want_ref
  45.0 6.7 %cycle_term.2.refs_10_ = f32[32,32,512]{2,1,0:T(8,128)S(1)} custom-call(bf16[256,2048]{1,0:T(8,128)(2,1)} %bitcast.106, bf16[4,32,64,512]{3,2,1,0:T(8,128)(2,1)} %bitcast.98, s32[32,32,1]{2,1,0:T(8,128)S(1)} %xor_xor_fusion.want_ref, s32[8,512]{1,0:T(8,128)S(1)} %broadcast_in_dim.173.sym_ref), custom_call_target="tpu_custom_call" | custom-call | bytes 1024 | tf_op jit(solution)/shard_map/cond/branch_0_fun/cycle_term/pallas_call | solution.py:336
  51.7 10.0 %arrange_ints.4.refs_8_ = bf16[1,8,1024,512]{3,2,1,0:T(8,128)(2,1)} custom-call(s32[8,8]{1,0:T(8,128)S(1)} %get-tuple-element.93.gtab_ref, bf16[32,512,512]{2,1,0:T(8,128)(2,1)} %bitcast.102), custom_call_target="tpu_custom_call" | custom-call | bytes 1024 | tf_op jit(solution)/shard_map/cond/branch_0_fun/arrange_ints/pallas_call | solution.py:178
  61.7 0.8 collective-permute-done.2.refs_2_
  62.5 4.9 %regroup.4 = (bf16[12,8,32,128]{3,2,1,0:T(8,128)(2,1)}, bf16[12,8,32,128]{3,2,1,0:T(8,128)(2,1)}, bf16[12,8,32,128]{3,2,1,0:T(8,128)(2,1)}, bf16[12,8,32,128]{3,2,1,0:T(8,128)(2,1)}) custom-call(s32[3,12]{1,0:T(4,128)S(1)} %add_add_fusion.1.tab_ref, bf16[4,4,8,32,128]{4,3,2,1,0:T(8,128)(2,1)} %get-tuple-element.77.refs_0_, ...), custom_call_target="tpu_custom_call" | custom-call | bytes 1024 | tf_op jit(solution)/shard_map/cond/branch_0_fun/regroup/pallas_call | solution.py:135
  67.5 2.8 %collective-permute-done.4.refs_2_ = bf16[4,4,8,32,128]{4,3,2,1,0:T(8,128)(2,1)} collective-permute-done((bf16[4,4,8,32,128]{4,3,2,1,0:T(8,128)(2,1)}, bf16[4,4,8,32,128]{4,3,2,1,0:T(8,128)(2,1)}, u32[]{:S(2)}, u32[]{:S(2)}) %collective-permute-start.4) | collective-permute-done | bytes 1048608 | tf_op jit(solution)/shard_map/cond/branch_0_fun/ppermute | solution.py:154
  70.3 5.0 %regroup.5 = (bf16[12,8,32,128]{3,2,1,0:T(8,128)(2,1)}, bf16[12,8,32,128]{3,2,1,0:T(8,128)(2,1)}, bf16[12,8,32,128]{3,2,1,0:T(8,128)(2,1)}, bf16[12,8,32,128]{3,2,1,0:T(8,128)(2,1)}) custom-call(s32[3,12]{1,0:T(4,128)S(1)} %add_add_fusion.tab_ref, bf16[4,4,8,32,128]{4,3,2,1,0:T(8,128)(2,1)} %get-tuple-element.84.refs_0_, ...), custom_call_target="tpu_custom_call" | custom-call | bytes 1024 | tf_op jit(solution)/shard_map/cond/branch_0_fun/regroup/pallas_call | solution.py:135
  75.3 2.7 %collective-permute-start.7 = (bf16[12,8,32,128]{3,2,1,0:T(8,128)(2,1)}, bf16[12,8,32,128]{3,2,1,0:T(8,128)(2,1)S(1)}, u32[]{:S(2)}, u32[]{:S(2)}) collective-permute-start(bf16[12,8,32,128]{3,2,1,0:T(8,128)(2,1)} %get-tuple-element.94), channel_id=1, source_target_pairs={{0,24},{8,0},{16,8},{24,16},{32,56},{40,32},{48,40},{56,48},{64,88... | collective-permute-start | bytes 2359304 | tf_op jit(solution)/shard_map/cond/branch_0_fun/ppermute | solution.py:154
  78.0 1.5 collective-permute-start.8
  79.5 1.8 %collective-permute-start.9 = (bf16[12,8,32,128]{3,2,1,0:T(8,128)(2,1)}, bf16[12,8,32,128]{3,2,1,0:T(8,128)(2,1)}, u32[]{:S(2)}, u32[]{:S(2)}) collective-permute-start(bf16[12,8,32,128]{3,2,1,0:T(8,128)(2,1)} %get-tuple-element.98), channel_id=1, source_target_pairs={{0,96},{8,104},{16,112},{24,120},{32,0},{40,8},{48,16},{56,24},{64... | collective-permute-start | bytes 2359304 | tf_op jit(solution)/shard_map/cond/branch_0_fun/ppermute | solution.py:154
  81.8 10.0 %arrange_ints.5.refs_9_ = bf16[1,8,1024,512]{3,2,1,0:T(8,128)(2,1)} custom-call(s32[8,8]{1,0:T(8,128)S(1)} %get-tuple-element.93.gtab_ref, bf16[32,512,512]{2,1,0:T(8,128)(2,1)} %bitcast.103), custom_call_target="tpu_custom_call" | custom-call | bytes 1024 | tf_op jit(solution)/shard_map/cond/branch_0_fun/arrange_ints/pallas_call | solution.py:178
  91.8 2.2 %collective-permute-done.6.refs_1_ = bf16[12,8,32,128]{3,2,1,0:T(8,128)(2,1)S(1)} collective-permute-done((bf16[12,8,32,128]{3,2,1,0:T(8,128)(2,1)}, bf16[12,8,32,128]{3,2,1,0:T(8,128)(2,1)S(1)}, u32[]{:S(2)}, u32[]{:S(2)}) %collective-permute-start.6) | collective-permute-done | bytes 786464 | tf_op jit(solution)/shard_map/cond/branch_0_fun/ppermute | solution.py:154
  94.0 3.4 %collective-permute-done.8.refs_5_ = bf16[12,8,32,128]{3,2,1,0:T(8,128)(2,1)} collective-permute-done((bf16[12,8,32,128]{3,2,1,0:T(8,128)(2,1)}, bf16[12,8,32,128]{3,2,1,0:T(8,128)(2,1)}, u32[]{:S(2)}, u32[]{:S(2)}) %collective-permute-start.8) | collective-permute-done | bytes 786464 | tf_op jit(solution)/shard_map/cond/branch_0_fun/ppermute | solution.py:154
  97.4 3.1 %collective-permute-start.11 = (bf16[12,8,32,128]{3,2,1,0:T(8,128)(2,1)}, bf16[12,8,32,128]{3,2,1,0:T(8,128)(2,1)}, u32[]{:S(2)}, u32[]{:S(2)}) collective-permute-start(bf16[12,8,32,128]{3,2,1,0:T(8,128)(2,1)} %get-tuple-element.100), channel_id=1, source_target_pairs={{0,64},{8,72},{16,80},{24,88},{32,96},{40,104},{48,112},{56,120},{... | collective-permute-start | bytes 2359304 | tf_op jit(solution)/shard_map/cond/branch_0_fun/ppermute | solution.py:154
  101.3 14.3 %collective-permute-done.10.refs_2_ = bf16[12,8,32,128]{3,2,1,0:T(8,128)(2,1)} collective-permute-done((bf16[12,8,32,128]{3,2,1,0:T(8,128)(2,1)}, bf16[12,8,32,128]{3,2,1,0:T(8,128)(2,1)}, u32[]{:S(2)}, u32[]{:S(2)}) %collective-permute-start.10) | collective-permute-done | bytes 786464 | tf_op jit(solution)/shard_map/cond/branch_0_fun/ppermute | solution.py:154
  115.6 14.1 %ladder.2 = (f32[16,32,512]{2,1,0:T(8,128)S(1)}, f32[16,32,512]{2,1,0:T(8,128)S(1)}) custom-call(s32[4,32]{1,0:T(4,128)S(1)} %pad_add_fusion.where_ref, s32[1]{0:T(128)} %bitcast.7.core_ref, bf16[12,8,32,128]{3,2,1,0:T(8,128)(2,1)} %get-tuple-element.88.refs_0_, bf16[12,8,32,128]{3,2,1,0:T(8,128)(2,1)} %copy-done.15, ...), custom_call_target="tpu_custom_call" | custom-call | bytes 1024 | tf_op jit(solution)/shard_map/cond/branch_0_fun/ladder/pallas_call | solution.py:285
  129.7 3.8 %collective-permute-start.12 = (f32[16,32,512]{2,1,0:T(8,128)S(1)}, f32[16,32,512]{2,1,0:T(8,128)S(1)}, u32[]{:S(2)}, u32[]{:S(2)}) collective-permute-start(f32[16,32,512]{2,1,0:T(8,128)S(1)} %get-tuple-element.102), channel_id=1, source_target_pairs={{0,1},{1,0},{2,3},{3,2},{4,5},{5,4},{6,7},{7,6},{8,9},{9,8},{10,11... | collective-permute-start | bytes 3145736 | tf_op jit(solution)/shard_map/cond/branch_0_fun/ppermute | solution.py:534
  133.5 2.3 %collective-permute-done.12 = f32[16,32,512]{2,1,0:T(8,128)S(1)} collective-permute-done((f32[16,32,512]{2,1,0:T(8,128)S(1)}, f32[16,32,512]{2,1,0:T(8,128)S(1)}, u32[]{:S(2)}, u32[]{:S(2)}) %collective-permute-start.12) | collective-permute-done | bytes 1048608 | tf_op jit(solution)/shard_map/cond/branch_0_fun/ppermute | solution.py:534
  136.0 22.8 %all_to_all.16.x_ref = f32[16,32,512]{2,1,0:T(8,128)S(1)} all-to-all(f32[16,32,512]{2,1,0:T(8,128)S(1)} %add.137), channel_id=1, replica_groups=mesh['row'=16,'col'=8] {'row'}, dimensions={0} | all-to-all | bytes 2097152 | tf_op jit(solution)/shard_map/cond/branch_0_fun/all_to_all | solution.py:535
  158.8 0.8 by_run.2
  159.7 11.6 %all_to_all.17.x_ref = f32[8,8,512]{2,1,0:T(8,128)S(1)} all-to-all(f32[8,8,512]{2,1,0:T(8,128)S(1)} %by_run.2), channel_id=1, replica_groups=mesh['row'=16,'col'=8] {'col'}, dimensions={0} | all-to-all | bytes 262144 | tf_op jit(solution)/shard_map/cond/branch_0_fun/all_to_all | solution.py:536
  171.3 0.8 finish.2
  172.6 0.7 copy-done.17
  (108 shorter events, 5.5 us)
Async XLA Ops:
  2.3 24.1 %copy-start.18 = (s32[32]{0:T(128)S(1)}, s32[32]{0:T(128)}, u32[]{:S(2)}) copy-start(s32[32]{0:T(128)} %get-tuple-element.48) | copy-start | bytes 388 | tf_op jit(solution)/shard_map/cond
  2.3 24.6 %copy-start.8 = (f32[512]{0:T(512)S(1)}, f32[512]{0:T(512)}, u32[]{:S(2)}) copy-start(f32[512]{0:T(512)} %get-tuple-element.92) | copy-start | bytes 6148 | tf_op jit(solution)/shard_map/cond
  2.3 24.7 %copy-start.6 = (s32[512]{0:T(512)S(1)}, s32[512]{0:T(512)}, u32[]{:S(2)}) copy-start(s32[512]{0:T(512)} %get-tuple-element.64) | copy-start | bytes 6148 | tf_op jit(solution)/shard_map/cond
  2.3 24.8 %copy-start.22 = (s32[8]{0:T(128)S(1)}, s32[8]{0:T(128)}, u32[]{:S(2)}) copy-start(s32[8]{0:T(128)} %get-tuple-element.66) | copy-start | bytes 100 | tf_op jit(solution)/shard_map/cond
  9.3 19.1 %copy-start.4 = (f32[64]{0:T(128)S(1)}, f32[64]{0:T(128)}, u32[]{:S(2)}) copy-start(f32[64]{0:T(128)} %get-tuple-element.50) | copy-start | bytes 772 | tf_op jit(solution)/shard_map/cond
  9.3 19.8 %copy-start.2 = (s32[64]{0:T(128)S(1)}, s32[64]{0:T(128)}, u32[]{:S(2)}) copy-start(s32[64]{0:T(128)} %get-tuple-element.24) | copy-start | bytes 772 | tf_op jit(solution)/shard_map/cond
  9.3 21.1 %copy-start.20 = (s32[32]{0:T(128)S(1)}, s32[32]{0:T(128)}, u32[]{:S(2)}) copy-start(s32[32]{0:T(128)} %get-tuple-element.11) | copy-start | bytes 388 | tf_op jit(solution)/shard_map/cond
  9.3 27.8 %collective-permute-start = (bf16[4,4,8,32,128]{4,3,2,1,0:T(8,128)(2,1)}, bf16[4,4,8,32,128]{4,3,2,1,0:T(8,128)(2,1)S(1)}, u32[]{:S(2)}, u32[]{:S(2)}) collective-permute-start(bf16[4,4,8,32,128]{4,3,2,1,0:T(8,128)(2,1)} %get-tuple-element.71), channel_id=1, source_target_pairs={{0,8},{8,16},{16,24},{24,0},{32,40},{40,48},{48,56},{56,32},{64,72... | collective-permute-start | bytes 3145736 | tf_op jit(solution)/shard_map/cond/branch_0_fun/ppermute | solution.py:154
  11.8 25.3 %collective-permute-start.1 = (bf16[4,4,8,32,128]{4,3,2,1,0:T(8,128)(2,1)}, bf16[4,4,8,32,128]{4,3,2,1,0:T(8,128)(2,1)}, u32[]{:S(2)}, u32[]{:S(2)}) collective-permute-start(bf16[4,4,8,32,128]{4,3,2,1,0:T(8,128)(2,1)} %get-tuple-element.72), channel_id=1, source_target_pairs={{0,24},{8,0},{16,8},{24,16},{32,56},{40,32},{48,40},{56,48},{64,88... | collective-permute-start | bytes 3145736 | tf_op jit(solution)/shard_map/cond/branch_0_fun/ppermute | solution.py:154
  14.1 28.1 %copy-start.10 = (bf16[32,8,4,512]{3,2,1,0:T(4,128)(2,1)S(1)}, bf16[32,8,4,512]{3,2,1,0:T(4,128)(2,1)}, u32[]{:S(2)}) copy-start(bf16[32,8,4,512]{3,2,1,0:T(4,128)(2,1)} %get-tuple-element.223) | copy-start | bytes 3145732 | tf_op jit(solution)/shard_map/cond
  21.5 45.9 %collective-permute-start.3 = (bf16[4,4,8,32,128]{4,3,2,1,0:T(8,128)(2,1)}, bf16[4,4,8,32,128]{4,3,2,1,0:T(8,128)(2,1)}, u32[]{:S(2)}, u32[]{:S(2)}) collective-permute-start(bf16[4,4,8,32,128]{4,3,2,1,0:T(8,128)(2,1)} %get-tuple-element.85), channel_id=1, source_target_pairs={{0,32},{8,40},{16,48},{24,56},{32,64},{40,72},{48,80},{56,88},{64,... | collective-permute-start | bytes 3145736 | tf_op jit(solution)/shard_map/cond/branch_0_fun/ppermute | solution.py:154
  22.8 47.5 %collective-permute-start.4 = (bf16[4,4,8,32,128]{4,3,2,1,0:T(8,128)(2,1)}, bf16[4,4,8,32,128]{4,3,2,1,0:T(8,128)(2,1)}, u32[]{:S(2)}, u32[]{:S(2)}) collective-permute-start(bf16[4,4,8,32,128]{4,3,2,1,0:T(8,128)(2,1)} %get-tuple-element.86), channel_id=1, source_target_pairs={{0,64},{8,72},{16,80},{24,88},{32,96},{40,104},{48,112},{56,120},{... | collective-permute-start | bytes 3145736 | tf_op jit(solution)/shard_map/cond/branch_0_fun/ppermute | solution.py:154
  25.3 45.0 %collective-permute-start.5 = (bf16[4,4,8,32,128]{4,3,2,1,0:T(8,128)(2,1)}, bf16[4,4,8,32,128]{4,3,2,1,0:T(8,128)(2,1)}, u32[]{:S(2)}, u32[]{:S(2)}) collective-permute-start(bf16[4,4,8,32,128]{4,3,2,1,0:T(8,128)(2,1)} %get-tuple-element.87), channel_id=1, source_target_pairs={{0,96},{8,104},{16,112},{24,120},{32,0},{40,8},{48,16},{56,24},{64... | collective-permute-start | bytes 3145736 | tf_op jit(solution)/shard_map/cond/branch_0_fun/ppermute | solution.py:154
  37.2 2.4 %copy-start.12 = (bf16[4,4,8,32,128]{4,3,2,1,0:T(8,128)(2,1)}, bf16[4,4,8,32,128]{4,3,2,1,0:T(8,128)(2,1)S(1)}, u32[]{:S(2)}) copy-start(bf16[4,4,8,32,128]{4,3,2,1,0:T(8,128)(2,1)S(1)} %collective-permute-done.refs_1_) | copy-start | bytes 3145732 | tf_op jit(solution)/shard_map/cond
  37.2 25.3 %collective-permute-start.2 = (bf16[4,4,8,32,128]{4,3,2,1,0:T(8,128)(2,1)}, bf16[4,4,8,32,128]{4,3,2,1,0:T(8,128)(2,1)}, u32[]{:S(2)}, u32[]{:S(2)}) collective-permute-start(bf16[4,4,8,32,128]{4,3,2,1,0:T(8,128)(2,1)} %get-tuple-element.79), channel_id=1, source_target_pairs={{0,16},{8,24},{16,0},{24,8},{32,48},{40,56},{48,32},{56,40},{64,80... | collective-permute-start | bytes 3145736 | tf_op jit(solution)/shard_map/cond/branch_0_fun/ppermute | solution.py:154
  51.7 10.0 %copy-start = (f32[32,32,512]{2,1,0:T(8,128)}, f32[32,32,512]{2,1,0:T(8,128)S(1)}, u32[]{:S(2)}) copy-start(f32[32,32,512]{2,1,0:T(8,128)S(1)} %cycle_term.2.refs_10_) | copy-start | bytes 6291460 | tf_op jit(solution)/shard_map/cond
  75.3 18.8 %collective-permute-start.6 = (bf16[12,8,32,128]{3,2,1,0:T(8,128)(2,1)}, bf16[12,8,32,128]{3,2,1,0:T(8,128)(2,1)S(1)}, u32[]{:S(2)}, u32[]{:S(2)}) collective-permute-start(bf16[12,8,32,128]{3,2,1,0:T(8,128)(2,1)} %get-tuple-element.89), channel_id=1, source_target_pairs={{0,8},{8,16},{16,24},{24,0},{32,40},{40,48},{48,56},{56,32},{64,72... | collective-permute-start | bytes 2359304 | tf_op jit(solution)/shard_map/cond/branch_0_fun/ppermute | solution.py:154
  75.3 18.7 %collective-permute-start.7 = (bf16[12,8,32,128]{3,2,1,0:T(8,128)(2,1)}, bf16[12,8,32,128]{3,2,1,0:T(8,128)(2,1)S(1)}, u32[]{:S(2)}, u32[]{:S(2)}) collective-permute-start(bf16[12,8,32,128]{3,2,1,0:T(8,128)(2,1)} %get-tuple-element.94), channel_id=1, source_target_pairs={{0,24},{8,0},{16,8},{24,16},{32,56},{40,32},{48,40},{56,48},{64,88... | collective-permute-start | bytes 2359304 | tf_op jit(solution)/shard_map/cond/branch_0_fun/ppermute | solution.py:154
  78.0 19.4 %collective-permute-start.8 = (bf16[12,8,32,128]{3,2,1,0:T(8,128)(2,1)}, bf16[12,8,32,128]{3,2,1,0:T(8,128)(2,1)}, u32[]{:S(2)}, u32[]{:S(2)}) collective-permute-start(bf16[12,8,32,128]{3,2,1,0:T(8,128)(2,1)} %get-tuple-element.97), channel_id=1, source_target_pairs={{0,32},{8,40},{16,48},{24,56},{32,64},{40,72},{48,80},{56,88},{64,... | collective-permute-start | bytes 2359304 | tf_op jit(solution)/shard_map/cond/branch_0_fun/ppermute | solution.py:154
  79.5 17.8 %collective-permute-start.9 = (bf16[12,8,32,128]{3,2,1,0:T(8,128)(2,1)}, bf16[12,8,32,128]{3,2,1,0:T(8,128)(2,1)}, u32[]{:S(2)}, u32[]{:S(2)}) collective-permute-start(bf16[12,8,32,128]{3,2,1,0:T(8,128)(2,1)} %get-tuple-element.98), channel_id=1, source_target_pairs={{0,96},{8,104},{16,112},{24,120},{32,0},{40,8},{48,16},{56,24},{64... | collective-permute-start | bytes 2359304 | tf_op jit(solution)/shard_map/cond/branch_0_fun/ppermute | solution.py:154
  94.0 21.6 %copy-start.15 = (bf16[12,8,32,128]{3,2,1,0:T(8,128)(2,1)}, bf16[12,8,32,128]{3,2,1,0:T(8,128)(2,1)S(1)}, u32[]{:S(2)}) copy-start(bf16[12,8,32,128]{3,2,1,0:T(8,128)(2,1)S(1)} %collective-permute-done.6.refs_1_) | copy-start | bytes 2359300 | tf_op jit(solution)/shard_map/cond
  94.0 21.5 %copy-start.16 = (bf16[12,8,32,128]{3,2,1,0:T(8,128)(2,1)}, bf16[12,8,32,128]{3,2,1,0:T(8,128)(2,1)S(1)}, u32[]{:S(2)}) copy-start(bf16[12,8,32,128]{3,2,1,0:T(8,128)(2,1)S(1)} %collective-permute-done.7.refs_3_) | copy-start | bytes 2359300 | tf_op jit(solution)/shard_map/cond
  97.4 18.1 %collective-permute-start.10 = (bf16[12,8,32,128]{3,2,1,0:T(8,128)(2,1)}, bf16[12,8,32,128]{3,2,1,0:T(8,128)(2,1)}, u32[]{:S(2)}, u32[]{:S(2)}) collective-permute-start(bf16[12,8,32,128]{3,2,1,0:T(8,128)(2,1)} %get-tuple-element.99), channel_id=1, source_target_pairs={{0,16},{8,24},{16,0},{24,8},{32,48},{40,56},{48,32},{56,40},{64,80... | collective-permute-start | bytes 2359304 | tf_op jit(solution)/shard_map/cond/branch_0_fun/ppermute | solution.py:154
  97.4 18.2 %collective-permute-start.11 = (bf16[12,8,32,128]{3,2,1,0:T(8,128)(2,1)}, bf16[12,8,32,128]{3,2,1,0:T(8,128)(2,1)}, u32[]{:S(2)}, u32[]{:S(2)}) collective-permute-start(bf16[12,8,32,128]{3,2,1,0:T(8,128)(2,1)} %get-tuple-element.100), channel_id=1, source_target_pairs={{0,64},{8,72},{16,80},{24,88},{32,96},{40,104},{48,112},{56,120},{... | collective-permute-start | bytes 2359304 | tf_op jit(solution)/shard_map/cond/branch_0_fun/ppermute | solution.py:154
  129.7 6.1 %collective-permute-start.12 = (f32[16,32,512]{2,1,0:T(8,128)S(1)}, f32[16,32,512]{2,1,0:T(8,128)S(1)}, u32[]{:S(2)}, u32[]{:S(2)}) collective-permute-start(f32[16,32,512]{2,1,0:T(8,128)S(1)} %get-tuple-element.102), channel_id=1, source_target_pairs={{0,1},{1,0},{2,3},{3,2},{4,5},{5,4},{6,7},{7,6},{8,9},{9,8},{10,11... | collective-permute-start | bytes 3145736 | tf_op jit(solution)/shard_map/cond/branch_0_fun/ppermute | solution.py:534
  172.6 0.7 copy-start.17

commit v4 on v3

--- a/solution.py
+++ b/solution.py
@@ -2,7 +2,6 @@
 
 import jax
 import jax.numpy as jnp
-import numpy as np
 from jax import lax
 from jax.experimental import pallas as pl
 from jax.experimental.pallas import tpu as pltpu
@@ -42,108 +41,127 @@
     return lax.optimization_barrier((tuple(values), tuple(others)))[0]
 
 
-def lane_swap():
-    out = np.zeros((4, 4, 4, 32, 4, 4, 32), np.float32)
-    for first in range(4):
-        for e in range(4):
+def lane_swap(z):
+    src = lax.broadcasted_iota(jnp.int32, (512, 128), 0)
+    dst = lax.broadcasted_iota(jnp.int32, (512, 128), 1)
+    return (src == (dst & 31) + 32 * z + 128 * (dst >> 5)).astype(F32).astype(BF16)
+
+
+def pack_kernel(piece, slots, tab_ref, amp_ref, *rest):
+    outs, (in_ref, mid_ref, turn_ref, out_ref, in_sems, out_sems) = rest[:4], rest[4:]
+
+    def fetch(slot):
+        src = amp_ref.at[tab_ref[slot], :, pl.ds(DP * piece, DP), :]
+        return pltpu.make_async_copy(src, in_ref.at[slot], in_sems.at[slot])
+
+    def ship(slot, n):
+        return pltpu.make_async_copy(out_ref.at[slot, n], outs[n].at[:, slot], out_sems.at[slot, n])
+
+    for slot in range(slots):
+        fetch(slot).start()
+    for z in range(4):
+        turn_ref[:, 128 * z : 128 * z + 128] = lane_swap((z + tab_ref[5]) & 3 if piece else z)
+
+    def work(slot, carry):
+        fetch(slot).wait()
+        for jh in range(2):
+            rows = slice(16 * jh, 16 * jh + 16)
+            for dh in range(DP // 16):
+                y = jnp.swapaxes(in_ref[slot, rows, 16 * dh : 16 * dh + 16, :], 0, 1)
+                for x in range(4):
+                    for q in range(4):
+                        for e in range(4):
+                            mid_ref[x, 4 * dh + q, rows, 128 * e : 128 * e + 128] = y[
+                                4 * q + e, :, 128 * x : 128 * x + 128
+                            ]
+        w = jnp.dot(mid_ref[...].reshape(4 * QP * OJ, 512), turn_ref[...], preferred_element_type=F32)
+        w = w.astype(BF16).reshape(4, QP, OJ, 512)
+        for x in range(4):
             for z in range(4):
-                for c in range(32):
-                    out[first, e, z, c, (z - first) % 4, e, c] = 1
-    return out.reshape(4, 512, 512).astype(jnp.bfloat16)
-
-
-def pack_kernel(piece, tab_ref, amp_ref, lanes_ref, *rest):
-    outs, mid_ref = rest[:4], rest[4]
-    for jh in range(2):
-        rows = slice(16 * jh, 16 * jh + 16)
-        for dh in range(DP // 16):
-            y = jnp.swapaxes(amp_ref[0, rows, 16 * dh : 16 * dh + 16, :], 0, 1)
-            for x in range(4):
-                to = x if piece else (x - tab_ref[4]) & 3
-                for q in range(4):
-                    for e in range(4):
-                        mid_ref[to, 4 * dh + q, rows, 128 * e : 128 * e + 128] = y[
-                            4 * q + e, :, 128 * x : 128 * x + 128
-                        ]
-    w = jnp.dot(mid_ref[...].reshape(4 * QP * OJ, 512), lanes_ref[0], preferred_element_type=F32)
-    w = w.astype(BF16).reshape(4, QP, OJ, 512)
-    for x in range(4):
-        for z in range(4):
-            block = w[x, :, :, 128 * z : 128 * z + 128]
-            if piece:
-                outs[z][x, 0] = block
-            else:
-                outs[x][z, 0] = block
+                block = w[x, :, :, 128 * z : 128 * z + 128]
+                if piece:
+                    out_ref[slot, z, x] = block
+                else:
+                    out_ref[slot, (x - tab_ref[4]) & 3, z] = block
+        for n in range(4):
+            ship(slot, n).start()
+        return carry
+
+    lax.fori_loop(0, slots, work, 0)
+    for slot in range(slots):
+        for n in range(4):
+            ship(slot, n).wait()
 
 
 def pack(amp_t, piece, slots, tab):
+    hbm = pl.BlockSpec(memory_space=pltpu.HBM)
     return pl.pallas_call(
-        functools.partial(pack_kernel, piece),
-        grid_spec=pltpu.PrefetchScalarGridSpec(
-            num_scalar_prefetch=1,
-            grid=(slots,),
-            in_specs=[
-                pl.BlockSpec((1, OJ, DP, NV), lambda s, tab: (tab[s], 0, piece, 0)),
-                pl.BlockSpec((1, 512, 512), lambda s, tab: (tab[5] * piece, 0, 0)),
-            ],
-            out_specs=[pl.BlockSpec((4, 1, QP, OJ, 128), lambda s, tab: (0, s, 0, 0, 0))] * 4,
-            scratch_shapes=[pltpu.VMEM((4, QP, OJ, 512), BF16)],
-        ),
+        functools.partial(pack_kernel, piece, slots),
+        in_specs=[pl.BlockSpec(memory_space=pltpu.SMEM), hbm],
+        out_specs=[hbm] * 4,
         out_shape=[pltpu.HBM((4, slots, QP, OJ, 128), BF16)] * 4,
-        compiler_params=params(),
+        scratch_shapes=[
+            pltpu.VMEM((slots, OJ, DP, NV), BF16),
+            pltpu.VMEM((4, QP, OJ, 512), BF16),
+            pltpu.VMEM((512, 512), BF16),
+            pltpu.VMEM((slots, 4, 4, QP, OJ, 128), BF16),
+            pltpu.SemaphoreType.DMA((slots,)),
+            pltpu.SemaphoreType.DMA((slots, 4)),
+        ],
+        compiler_params=pltpu.CompilerParams(vmem_limit_bytes=VMEM),
         cost_estimate=cost(8_000_000_000 // PIECES, 2 * 8 * 2**20 // PIECES),
         name="pack",
-    )(tab, in_hbm(amp_t), in_hbm(jnp.asarray(lane_swap())))
-
-
-def regroup_kernel(count, tab_ref, *refs):
-    got, outs, (buf_ref, sems, out_sems) = refs[:4], refs[4:8], refs[8:]
-
-    def copy(n, away, rel):
-        src = got[away].at[(tab_ref[2, n] + rel) & 3, tab_ref[1, n]]
-        return pltpu.make_async_copy(src, buf_ref.at[rel, n], sems.at[rel, n])
-
-    def ship(rel):
-        return pltpu.make_async_copy(buf_ref.at[rel], outs[rel], out_sems.at[rel])
+    )(tab, in_hbm(amp_t))
+
+
+def regroup_kernel(count, rels, tab_ref, *refs):
+    got, outs, (buf_ref, sems, out_sems) = refs[:4], refs[4:6], refs[6:]
+
+    def copy(n, away, at):
+        src = got[away].at[(tab_ref[2, n] + rels[at]) & 3, tab_ref[1, n]]
+        return pltpu.make_async_copy(src, buf_ref.at[at, n], sems.at[at, n])
+
+    def ship(at):
+        return pltpu.make_async_copy(buf_ref.at[at], outs[at], out_sems.at[at])
 
     def start(n, carry):
         for away in range(4):
 
             @pl.when(tab_ref[0, n] == away)
             def _():
-                for rel in range(4):
-                    copy(n, away, rel).start()
+                for at in range(2):
+                    copy(n, away, at).start()
 
         return carry
 
     lax.fori_loop(0, count, start, 0)
-    for rel in range(4):
+    for at in range(2):
 
         def arrive(n, carry):
-            copy(n, 0, rel).wait()
+            copy(n, 0, at).wait()
             return carry
 
         lax.fori_loop(0, count, arrive, 0)
-        ship(rel).start()
-    for rel in range(4):
-        ship(rel).wait()
-
-
-def regroup(tab, got):
+        ship(at).start()
+    for at in range(2):
+        ship(at).wait()
+
+
+def regroup(tab, got, *rels):
     count = tab.shape[1]
     hbm = pl.BlockSpec(memory_space=pltpu.HBM)
     return pl.pallas_call(
-        functools.partial(regroup_kernel, count),
+        functools.partial(regroup_kernel, count, rels),
         in_specs=[pl.BlockSpec(memory_space=pltpu.SMEM)] + [hbm] * 4,
-        out_specs=[hbm] * 4,
-        out_shape=[pltpu.HBM((count, QP, OJ, 128), BF16)] * 4,
+        out_specs=[hbm] * 2,
+        out_shape=[pltpu.HBM((count, QP, OJ, 128), BF16)] * 2,
         scratch_shapes=[
-            pltpu.VMEM((4, count, QP, OJ, 128), BF16),
-            pltpu.SemaphoreType.DMA((4, count)),
-            pltpu.SemaphoreType.DMA((4,)),
+            pltpu.VMEM((2, count, QP, OJ, 128), BF16),
+            pltpu.SemaphoreType.DMA((2, count)),
+            pltpu.SemaphoreType.DMA((2,)),
         ],
         compiler_params=pltpu.CompilerParams(vmem_limit_bytes=VMEM),
-        cost_estimate=cost(0, 16 * count * 2**15),
+        cost_estimate=cost(0, 8 * count * 2**15),
         name="regroup",
     )(tab, *[in_hbm(x) for x in got])
 
@@ -198,8 +216,10 @@
 
 
 def ladder_kernel(where_ref, core_ref, *refs):
-    r_refs, ints_refs, (cycle_hbm, pick_ref, drop_ref) = refs[:8], refs[8:10], refs[10:13]
-    keep_ref, send_ref, rows_ref, slab_ref, ints_ref, cycle_ref, sum_ref, sems, ints_sems, cycle_sem = refs[13:]
+    r_refs, ints_hbm, small_hbm = refs[:8], refs[8:10], refs[10:13]
+    keep_ref, send_ref, rows_ref, slab_ref, ints_ref, sum_ref = refs[13:19]
+    small_refs, sems, ints_sems, small_sems = refs[19:22], *refs[22:]
+    pick_ref, drop_ref, cycle_ref = small_refs
     core = core_ref[0]
 
     def copy(p, piece, away):
@@ -207,9 +227,11 @@
         return pltpu.make_async_copy(src, slab_ref.at[p, piece], sems.at[p, piece])
 
     def copy_ints(g, piece):
-        return pltpu.make_async_copy(ints_refs[piece].at[0, g], ints_ref.at[piece, g], ints_sems.at[piece, g])
-
-    copy_cycle = pltpu.make_async_copy(cycle_hbm, cycle_ref, cycle_sem)
+        dst = ints_ref.at[g, pl.ds(KP * piece, KP)]
+        return pltpu.make_async_copy(ints_hbm[piece].at[0, g], dst, ints_sems.at[piece, g])
+
+    def copy_small(n):
+        return pltpu.make_async_copy(small_hbm[n], small_refs[n], small_sems.at[n])
 
     def start(p, carry):
         for piece in range(PIECES):
@@ -243,7 +265,9 @@
             copy_ints(g, piece).wait()
         sum_ref[g] = sum(
             jnp.dot(
-                rows_ref[g, :, KP * piece : KP * piece + KP], ints_ref[piece, g], preferred_element_type=F32
+                rows_ref[g, :, KP * piece : KP * piece + KP],
+                ints_ref[g, KP * piece : KP * piece + KP],
+                preferred_element_type=F32,
             )
             for piece in range(PIECES)
         )
@@ -267,14 +291,18 @@
 
         return carry
 
+    copy_small(0).start()
     lax.fori_loop(0, OI, start, 0)
     for g in range(8):
         for piece in range(PIECES):
             copy_ints(g, piece).start()
-    copy_cycle.start()
+    for n in (1, 2):
+        copy_small(n).start()
+    copy_small(0).wait()
     lax.fori_loop(0, 8, sort, 0)
     lax.fori_loop(0, 8, group, 0)
-    copy_cycle.wait()
+    for n in (1, 2):
+        copy_small(n).wait()
     lax.fori_loop(0, 8, unsort, 0)
 
 
@@ -284,23 +312,25 @@
     hbm = pl.BlockSpec(memory_space=pltpu.HBM)
     return pl.pallas_call(
         ladder_kernel,
-        in_specs=[smem] * 2 + [hbm] * 11 + [vmem] * 2,
+        in_specs=[smem] * 2 + [hbm] * 13,
         out_specs=[vmem] * 2,
         out_shape=[jax.ShapeDtypeStruct((16, OJ, 512), F32)] * 2,
         scratch_shapes=[
             pltpu.VMEM((8, 256, PIECES * KP), BF16),
             pltpu.VMEM((OI, PIECES, QP, OJ, 128), BF16),
-            pltpu.VMEM((PIECES, 8, KP, 512), BF16),
+            pltpu.VMEM((8, PIECES * KP, 512), BF16),
+            pltpu.VMEM((8, 256, 512), F32),
+            pltpu.VMEM((8, 256, 128), BF16),
+            pltpu.VMEM((8, 128, 256), BF16),
             pltpu.VMEM((OI, OJ, 512), F32),
-            pltpu.VMEM((8, 256, 512), F32),
             pltpu.SemaphoreType.DMA((OI, PIECES)),
             pltpu.SemaphoreType.DMA((PIECES, 8)),
-            pltpu.SemaphoreType.DMA(()),
+            pltpu.SemaphoreType.DMA((3,)),
         ],
         compiler_params=pltpu.CompilerParams(vmem_limit_bytes=VMEM),
         cost_estimate=cost(5_400_000_000, 30 * 2**20),
         name="ladder",
-    )(where, core, *[in_hbm(x) for x in (*arrived, early, late, cyc)], pick, drop)
+    )(where, core, *[in_hbm(x) for x in (*arrived, early, late, pick, drop, cyc)])
 
 
 def cycle_kernel(ovov_ref, amp_ref, want_ref, sym_ref, out_ref, mid_ref, turn_ref):
@@ -405,7 +435,7 @@
             out_specs=full(2, OJ, SA, RUN),
             scratch_shapes=[pltpu.VMEM((2, 8, SA, RUN), F32)],
         ),
-        out_shape=jax.ShapeDtypeStruct((2, OJ, SA, RUN), F32),
+        out_shape=pltpu.HBM((2, OJ, SA, RUN), F32),
         compiler_params=params(),
         name="finish",
     )(slot, irr, energy, x, va, vb, sa, sb)
@@ -511,23 +541,27 @@
     (gate,) = after([gtab], cyc)
     early = arrange_ints(0, 1, gate, ints, pltpu.HBM)
     (tab1,) = after([tabs[1]], early, pick)
-    packed1 = regroup(tab1, [sent[1][0], second[1], second[2], second[3]])
-    (tab0,) = after([tabs[0]], packed1[0])
-    packed0 = regroup(tab0, [sent[0][0], first[1], first[2], first[3]])
-    sides1 = after([packed1[1], packed1[3]], first[1], first[2], first[3])
-    arrived0 = {n: move(packed0[n], n, False) for n in (1, 3)}
+    lines1 = [sent[1][0], second[1], second[2], second[3]]
+    sides1 = regroup(tab1, lines1, 1, 3)
+    (tab0,) = after([tabs[0]], sides1)
+    lines0 = [sent[0][0], first[1], first[2], first[3]]
+    sides0 = regroup(tab0, lines0, 1, 3)
+    arrived0 = {n: move(x, n, False) for n, x in zip((1, 3), sides0)}
+    sides1 = after(sides1, first[1], first[2], first[3])
     arrived1 = {n: move(x, n, True) for n, x in zip((1, 3), sides1)}
-    (gate,) = after([gtab], packed0[0], *tail)
+    rest1, rest0 = after([tab1, tab0], sides0)
+    across1, arrived1[0] = regroup(rest1, lines1, 2, 0)
+    across0, arrived0[0] = regroup(rest0, lines0, 2, 0)
+    (across1,) = after([across1], arrived1[1], arrived1[3])
+    (across0,) = after([across0], arrived0[1], arrived0[3], across1)
+    (gate,) = after([gtab], across0, *tail)
+    arrived1[2] = move(across1, 2, True)
+    arrived0[2] = move(across0, 2, False)
     late = arrange_ints(1, 1, gate, ints, pltpu.HBM)
-    across0, across1 = after(
-        [packed0[2], packed1[2]], late, list(arrived0.values()), list(arrived1.values())
-    )
-    arrived0[2] = move(across0, 2, False)
-    arrived1[2] = move(across1, 2, True)
     keep, give = ladder(
         jnp.concatenate(where),
         core.reshape(1),
-        [packed0[0], arrived0[1], arrived0[2], arrived0[3], packed1[0], arrived1[1], arrived1[2], arrived1[3]],
+        [arrived0[n] for n in range(4)] + [arrived1[n] for n in range(4)],
         pick, early, late, drop, cyc,
     )
 
@@ -538,8 +572,8 @@
 
 
 def shards(*args):
-    lines = jnp.stack([args[7] // 16, args[7] // 4 % 4])
-    on_line = jnp.max(jnp.sum(lines[:, None, :] == jnp.arange(4)[:, None], axis=-1))
+    spots = jnp.stack([args[7] // 16, args[7] // 4 % 4])
+    on_line = jnp.max(jnp.sum(spots[:, None, :] == jnp.arange(4)[:, None], axis=-1))
     return lax.cond(
         on_line > 12, functools.partial(body, 4, 16), functools.partial(body, 4, 12), *args
     )

time: 174 us -> 169 us (0.971)
  waiting for transfers between devices: 28.1 us -> 13.6 us
  other arithmetic: 5.34 us -> 10.1 us
  local copies, waits for them, and re-layouts: 12.5 us -> 15.6 us
  Pallas kernels: 66.8 us -> 69.4 us
    ppermute x12, waiting for transfers between devices: 25.8 us -> 11.3 us  [move(): return lax.ppermute(x, 'row', pairs)]
    pallas_call x5 -> x7, Pallas kernels: 38.5 us -> 40.4 us  [the longest x4 14.1 us: regroup(): pl.pallas_call(functools.partial(regroup_kernel, count, rels), in_specs=[...]
  transfers between devices with their start and end apart: 13 -> 13, of which waited for: 7 -> 7; matrix products, arithmetic and copies ran while one was open for 9% -> 14% of each run, Pallas kernels for 23% -> 28%
where the time goes in v4:
time: 169 us; the launch traced here: 168 us
  Pallas kernels  69.4 us (41%)
  blocking collectives  32.9 us (19%)
  starting transfers between devices  25.5 us (15%)
  local copies, waits for them, and re-layouts  15.6 us (9%)
  waiting for transfers between devices  13.6 us (8%)
  other arithmetic  10.1 us (6%)
    ppermute x12, starting transfers between devices, move(): return lax.ppermute(x, 'row', pairs)  21.8 us
    all_to_all x1, blocking collectives, body(): lax.all_to_all(keep + got, 'row', split_axis=0, concat_axis=0, tiled=True)  21.3 us
    pallas_call x2, Pallas kernels, arrange_ints(): pl.pallas_call(ints_kernel, grid_spec=pltpu.PrefetchScalarGridSpec(num_sc...  20 us
    pallas_call x4, Pallas kernels, regroup(): pl.pallas_call(functools.partial(regroup_kernel, count, rels), in_specs=[...  14.1 us
    pallas_call x1, Pallas kernels, ladder(): pl.pallas_call(ladder_kernel, in_specs=[smem] * 2 + [hbm] * 13, out_specs...  14.1 us
    pallas_call x2, Pallas kernels, pack(): pl.pallas_call(functools.partial(pack_kernel, piece, slots), in_specs=[pl...  12.2 us
    all_to_all x1, blocking collectives, body(): lax.all_to_all(by_run(ltab, both, spread), 'col', split_axis=0, concat_ax...  11.6 us
    ppermute x12, waiting for transfers between devices, move(): return lax.ppermute(x, 'row', pairs)  11.3 us
  transfers between devices with their start and end apart: 13, of which 7 were waited for; matrix products, arithmetic and copies ran while one was open for 14% of the time, Pallas kernels for 28%

profile of v4, /device:TPU:1, one launch (start us, length us, event | category | flops | bytes accessed | tf_op | source)
XLA Modules:
  0.0 168.3 jit_solution(8032009044997353604)
XLA Ops:
  0.0 0.7 fusion.38
  2.1 166.1 %conditional.1 = (f32[2,32,8,64]{3,2,1,0:T(8,128)}) conditional(s32[]{:T(128)} %convert_element_type.35, (s32[32]{0:T(128)}, s32[32]{0:T(128)}, s32[64]{0:T(128)}, f32[64]{0:T(128)}, s32[512]{0:T(512)}, /*index=5*/s32[8]{0:T(128)}, bf16[32,8,4,512]{3,2,1,0:T(4,128)(2,1)}, bf16[4,32,512,64]{2,3,1,0:T(8,128)(2,1)}, ...), branch_computations={%region_2.19_spmd, %region_13.30_spmd} | conditional | flops 901215 | bytes 96673048 | solution.py:577
  2.3 6.1 %pack.4 = (bf16[4,4,8,32,128]{4,3,2,1,0:T(8,128)(2,1)}, bf16[4,4,8,32,128]{4,3,2,1,0:T(8,128)(2,1)}, bf16[4,4,8,32,128]{4,3,2,1,0:T(8,128)(2,1)}, bf16[4,4,8,32,128]{4,3,2,1,0:T(8,128)(2,1)}) custom-call(s32[6]{0:T(128)S(1)} %pad_add_fusion.1.tab_ref, bf16[4,32,64,512]{3,2,1,0:T(8,128)(2,1)} %bitcast.96), custom_call_target="tpu_custom_call" | custom-call | bytes 1024 | tf_op jit(solution)/shard_map/cond/branch_0_fun/pack/pallas_call | solution.py:98
  8.4 2.5 %collective-permute-start = (bf16[4,4,8,32,128]{4,3,2,1,0:T(8,128)(2,1)}, bf16[4,4,8,32,128]{4,3,2,1,0:T(8,128)(2,1)S(1)}, u32[]{:S(2)}, u32[]{:S(2)}) collective-permute-start(bf16[4,4,8,32,128]{4,3,2,1,0:T(8,128)(2,1)} %get-tuple-element.62), channel_id=1, source_target_pairs={{0,8},{8,16},{16,24},{24,0},{32,40},{40,48},{48,56},{56,32},{64,72... | collective-permute-start | bytes 3145736 | tf_op jit(solution)/shard_map/cond/branch_0_fun/ppermute | solution.py:172
  10.9 2.2 %collective-permute-start.1 = (bf16[4,4,8,32,128]{4,3,2,1,0:T(8,128)(2,1)}, bf16[4,4,8,32,128]{4,3,2,1,0:T(8,128)(2,1)S(1)}, u32[]{:S(2)}, u32[]{:S(2)}) collective-permute-start(bf16[4,4,8,32,128]{4,3,2,1,0:T(8,128)(2,1)} %get-tuple-element.63), channel_id=1, source_target_pairs={{0,24},{8,0},{16,8},{24,16},{32,56},{40,32},{48,40},{56,48},{64,88... | collective-permute-start | bytes 3145736 | tf_op jit(solution)/shard_map/cond/branch_0_fun/ppermute | solution.py:172
  13.1 6.2 %pack.5 = (bf16[4,4,8,32,128]{4,3,2,1,0:T(8,128)(2,1)}, bf16[4,4,8,32,128]{4,3,2,1,0:T(8,128)(2,1)}, bf16[4,4,8,32,128]{4,3,2,1,0:T(8,128)(2,1)}, bf16[4,4,8,32,128]{4,3,2,1,0:T(8,128)(2,1)}) custom-call(s32[6]{0:T(128)S(1)} %pad_add_fusion.1.tab_ref, bf16[4,32,64,512]{3,2,1,0:T(8,128)(2,1)} %bitcast.97), custom_call_target="tpu_custom_call" | custom-call | bytes 1024 | tf_op jit(solution)/shard_map/cond/branch_0_fun/pack/pallas_call | solution.py:98
  19.3 1.3 collective-permute-start.3
  20.6 2.4 %collective-permute-start.4 = (bf16[4,4,8,32,128]{4,3,2,1,0:T(8,128)(2,1)}, bf16[4,4,8,32,128]{4,3,2,1,0:T(8,128)(2,1)}, u32[]{:S(2)}, u32[]{:S(2)}) collective-permute-start(bf16[4,4,8,32,128]{4,3,2,1,0:T(8,128)(2,1)} %get-tuple-element.77), channel_id=1, source_target_pairs={{0,64},{8,72},{16,80},{24,88},{32,96},{40,104},{48,112},{56,120},{... | collective-permute-start | bytes 3145736 | tf_op jit(solution)/shard_map/cond/branch_0_fun/ppermute | solution.py:172
  23.0 1.2 collective-permute-start.5
  24.4 0.7 pad.8.clone
  25.2 0.7 gather_fusion.5
  26.5 0.7 gather_fusion.1
  33.4 0.7 select_reduce_fusion.4
  35.2 1.1 collective-permute-done.refs_1_
  36.2 2.0 %collective-permute-start.2 = (bf16[4,4,8,32,128]{4,3,2,1,0:T(8,128)(2,1)}, bf16[4,4,8,32,128]{4,3,2,1,0:T(8,128)(2,1)}, u32[]{:S(2)}, u32[]{:S(2)}) collective-permute-start(bf16[4,4,8,32,128]{4,3,2,1,0:T(8,128)(2,1)} %get-tuple-element.70), channel_id=1, source_target_pairs={{0,16},{8,24},{16,0},{24,8},{32,48},{40,56},{48,32},{56,40},{64,80... | collective-permute-start | bytes 3145736 | tf_op jit(solution)/shard_map/cond/branch_0_fun/ppermute | solution.py:172
  38.2 0.8 and.326
  39.0 1.1 and.327
  40.3 0.7 and.324
  41.0 1.3 and.325
  42.7 1.3 copy.55
  44.5 0.7 add_add_fusion.tab_ref
  45.3 0.8 xor_xor_fusion.want_ref
  46.1 1.0 and_convert_fusion
  47.1 6.7 %cycle_term.2.refs_12_ = f32[32,32,512]{2,1,0:T(8,128)S(1)} custom-call(bf16[256,2048]{1,0:T(8,128)(2,1)} %bitcast.106, bf16[4,32,64,512]{3,2,1,0:T(8,128)(2,1)} %bitcast.98, s32[32,32,1]{2,1,0:T(8,128)S(1)} %xor_xor_fusion.want_ref, s32[8,512]{1,0:T(8,128)S(1)} %broadcast_in_dim.169.sym_ref), custom_call_target="tpu_custom_call" | custom-call | bytes 1024 | tf_op jit(solution)/shard_map/cond/branch_0_fun/cycle_term/pallas_call | solution.py:366
  53.8 10.0 %arrange_ints.4.refs_8_ = bf16[1,8,1024,512]{3,2,1,0:T(8,128)(2,1)} custom-call(s32[8,8]{1,0:T(8,128)S(1)} %broadcast_xor_fusion.1.gtab_ref, bf16[32,512,512]{2,1,0:T(8,128)(2,1)} %bitcast.102), custom_call_target="tpu_custom_call" | custom-call | bytes 1024 | tf_op jit(solution)/shard_map/cond/branch_0_fun/arrange_ints/pallas_call | solution.py:196
  63.8 3.6 %regroup.8 = (bf16[12,8,32,128]{3,2,1,0:T(8,128)(2,1)}, bf16[12,8,32,128]{3,2,1,0:T(8,128)(2,1)}) custom-call(s32[3,12]{1,0:T(4,128)S(1)} %add_add_fusion.tab_ref, bf16[4,4,8,32,128]{4,3,2,1,0:T(8,128)(2,1)} %get-tuple-element.68.refs_0_, bf16[4,4,8,32,128]{4,3,2,1,0:T(8,128)(2,1)} %copy-done.12, bf16[4,4,8,32,128]{4,3,2,1,0:T(8,128)(2,1)} %collective-permute-done.2.refs_2_, ...), custom_call_target="tpu_custom_call" | custom-call | bytes 1024 | tf_op jit(solution)/shard_map/cond/branch_0_fun/regroup/pallas_call | solution.py:153
  68.1 1.7 collective-permute-start.8
  69.7 1.7 collective-permute-start.9
  71.4 3.5 %regroup.9 = (bf16[12,8,32,128]{3,2,1,0:T(8,128)(2,1)}, bf16[12,8,32,128]{3,2,1,0:T(8,128)(2,1)}) custom-call(s32[3,12]{1,0:T(4,128)S(1)} %add_add_fusion.1.tab_ref, bf16[4,4,8,32,128]{4,3,2,1,0:T(8,128)(2,1)} %get-tuple-element.75.refs_0_, bf16[4,4,8,32,128]{4,3,2,1,0:T(8,128)(2,1)} %collective-permute-done.3.refs_1_, ...), custom_call_target="tpu_custom_call" | custom-call | bytes 1024 | tf_op jit(solution)/shard_map/cond/branch_0_fun/regroup/pallas_call | solution.py:153
  75.1 2.6 %collective-permute-start.7 = (bf16[12,8,32,128]{3,2,1,0:T(8,128)(2,1)}, bf16[12,8,32,128]{3,2,1,0:T(8,128)(2,1)}, u32[]{:S(2)}, u32[]{:S(2)}) collective-permute-start(bf16[12,8,32,128]{3,2,1,0:T(8,128)(2,1)} %get-tuple-element.80), channel_id=1, source_target_pairs={{0,24},{8,0},{16,8},{24,16},{32,56},{40,32},{48,40},{56,48},{64,88... | collective-permute-start | bytes 2359304 | tf_op jit(solution)/shard_map/cond/branch_0_fun/ppermute | solution.py:172
  78.7 0.7 gather_fusion.3
  79.4 1.0 copy.49.refs_10_
  80.5 3.5 %regroup.11 = (bf16[12,8,32,128]{3,2,1,0:T(8,128)(2,1)}, bf16[12,8,32,128]{3,2,1,0:T(8,128)(2,1)}) custom-call(s32[3,12]{1,0:T(4,128)S(1)} %add_add_fusion.tab_ref, bf16[4,4,8,32,128]{4,3,2,1,0:T(8,128)(2,1)} %get-tuple-element.68.refs_0_, bf16[4,4,8,32,128]{4,3,2,1,0:T(8,128)(2,1)} %copy-done.12, ...), custom_call_target="tpu_custom_call" | custom-call | bytes 1024 | tf_op jit(solution)/shard_map/cond/branch_0_fun/regroup/pallas_call | solution.py:153
  84.0 3.5 %regroup.10 = (bf16[12,8,32,128]{3,2,1,0:T(8,128)(2,1)}, bf16[12,8,32,128]{3,2,1,0:T(8,128)(2,1)}) custom-call(s32[3,12]{1,0:T(4,128)S(1)} %add_add_fusion.1.tab_ref, bf16[4,4,8,32,128]{4,3,2,1,0:T(8,128)(2,1)} %get-tuple-element.75.refs_0_, bf16[4,4,8,32,128]{4,3,2,1,0:T(8,128)(2,1)} %collective-permute-done.3.refs_1_, ...), custom_call_target="tpu_custom_call" | custom-call | bytes 1024 | tf_op jit(solution)/shard_map/cond/branch_0_fun/regroup/pallas_call | solution.py:153
  88.0 2.9 %collective-permute-start.11 = (bf16[12,8,32,128]{3,2,1,0:T(8,128)(2,1)}, bf16[12,8,32,128]{3,2,1,0:T(8,128)(2,1)S(1)}, u32[]{:S(2)}, u32[]{:S(2)}) collective-permute-start(bf16[12,8,32,128]{3,2,1,0:T(8,128)(2,1)} %get-tuple-element.88), channel_id=1, source_target_pairs={{0,64},{8,72},{16,80},{24,88},{32,96},{40,104},{48,112},{56,120},{... | collective-permute-start | bytes 2359304 | tf_op jit(solution)/shard_map/cond/branch_0_fun/ppermute | solution.py:172
  90.9 2.8 %collective-permute-done.6.refs_1_ = bf16[12,8,32,128]{3,2,1,0:T(8,128)(2,1)S(1)} collective-permute-done((bf16[12,8,32,128]{3,2,1,0:T(8,128)(2,1)}, bf16[12,8,32,128]{3,2,1,0:T(8,128)(2,1)S(1)}, u32[]{:S(2)}, u32[]{:S(2)}) %collective-permute-start.6) | collective-permute-done | bytes 786464 | tf_op jit(solution)/shard_map/cond/branch_0_fun/ppermute | solution.py:172
  93.7 1.2 collective-permute-start.10
  95.4 10.0 %arrange_ints.5.refs_9_ = bf16[1,8,1024,512]{3,2,1,0:T(8,128)(2,1)} custom-call(s32[8,8]{1,0:T(8,128)S(1)} %broadcast_xor_fusion.1.gtab_ref, bf16[32,512,512]{2,1,0:T(8,128)(2,1)} %bitcast.103), custom_call_target="tpu_custom_call" | custom-call | bytes 1024 | tf_op jit(solution)/shard_map/cond/branch_0_fun/arrange_ints/pallas_call | solution.py:196
  105.4 1.3 collective-permute-done.11.refs_6_
  106.7 5.1 %collective-permute-done.10.refs_2_ = bf16[12,8,32,128]{3,2,1,0:T(8,128)(2,1)S(1)} collective-permute-done((bf16[12,8,32,128]{3,2,1,0:T(8,128)(2,1)}, bf16[12,8,32,128]{3,2,1,0:T(8,128)(2,1)S(1)}, u32[]{:S(2)}, u32[]{:S(2)}) %collective-permute-start.10) | collective-permute-done | bytes 786464 | tf_op jit(solution)/shard_map/cond/branch_0_fun/ppermute | solution.py:172
  111.8 0.9 copy-done.22
  112.7 14.1 %ladder.2 = (f32[16,32,512]{2,1,0:T(8,128)S(1)}, f32[16,32,512]{2,1,0:T(8,128)S(1)}) custom-call(s32[4,32]{1,0:T(4,128)S(1)} %pad_add_fusion.where_ref, s32[1]{0:T(128)} %bitcast.7.core_ref, bf16[12,8,32,128]{3,2,1,0:T(8,128)(2,1)} %get-tuple-element.82.refs_0_, bf16[12,8,32,128]{3,2,1,0:T(8,128)(2,1)} %copy-done.20, bf16[12,8,32,128]{3,2,1,0:T(8,128)(2,1)} %copy-done.22, ...), custom_call_target="tpu_custom_call" | custom-call | bytes 1024 | tf_op jit(solution)/shard_map/cond/branch_0_fun/ladder/pallas_call | solution.py:313
  126.8 3.6 %collective-permute-start.12 = (f32[16,32,512]{2,1,0:T(8,128)S(1)}, f32[16,32,512]{2,1,0:T(8,128)S(1)}, u32[]{:S(2)}, u32[]{:S(2)}) collective-permute-start(f32[16,32,512]{2,1,0:T(8,128)S(1)} %get-tuple-element.94), channel_id=1, source_target_pairs={{0,1},{1,0},{2,3},{3,2},{4,5},{5,4},{6,7},{7,6},{8,9},{9,8},{10,11... | collective-permute-start | bytes 3145736 | tf_op jit(solution)/shard_map/cond/branch_0_fun/ppermute | solution.py:568
  130.5 2.3 %collective-permute-done.12 = f32[16,32,512]{2,1,0:T(8,128)S(1)} collective-permute-done((f32[16,32,512]{2,1,0:T(8,128)S(1)}, f32[16,32,512]{2,1,0:T(8,128)S(1)}, u32[]{:S(2)}, u32[]{:S(2)}) %collective-permute-start.12) | collective-permute-done | bytes 1048608 | tf_op jit(solution)/shard_map/cond/branch_0_fun/ppermute | solution.py:568
  133.0 21.3 %all_to_all.16.x_ref = f32[16,32,512]{2,1,0:T(8,128)S(1)} all-to-all(f32[16,32,512]{2,1,0:T(8,128)S(1)} %add.137), channel_id=1, replica_groups=mesh['row'=16,'col'=8] {'row'}, dimensions={0} | all-to-all | bytes 2097152 | tf_op jit(solution)/shard_map/cond/branch_0_fun/all_to_all | solution.py:569
  154.3 0.8 by_run.2
  155.1 11.6 %all_to_all.17.x_ref = f32[8,8,512]{2,1,0:T(8,128)S(1)} all-to-all(f32[8,8,512]{2,1,0:T(8,128)S(1)} %by_run.2), channel_id=1, replica_groups=mesh['row'=16,'col'=8] {'col'}, dimensions={0} | all-to-all | bytes 262144 | tf_op jit(solution)/shard_map/cond/branch_0_fun/all_to_all | solution.py:570
  166.8 1.5 finish.2
  (131 shorter events, 13.3 us)
Async XLA Ops:
  2.3 21.9 %copy-start.23 = (s32[32]{0:T(128)S(1)}, s32[32]{0:T(128)}, u32[]{:S(2)}) copy-start(s32[32]{0:T(128)} %get-tuple-element.42) | copy-start | bytes 388 | tf_op jit(solution)/shard_map/cond
  2.3 23.0 %copy-start.2 = (s32[64]{0:T(128)S(1)}, s32[64]{0:T(128)}, u32[]{:S(2)}) copy-start(s32[64]{0:T(128)} %get-tuple-element.40) | copy-start | bytes 772 | tf_op jit(solution)/shard_map/cond
  2.3 23.7 %copy-start.25 = (s32[32]{0:T(128)S(1)}, s32[32]{0:T(128)}, u32[]{:S(2)}) copy-start(s32[32]{0:T(128)} %get-tuple-element.22) | copy-start | bytes 388 | tf_op jit(solution)/shard_map/cond
  2.3 26.1 %copy-start.27 = (s32[8]{0:T(128)S(1)}, s32[8]{0:T(128)}, u32[]{:S(2)}) copy-start(s32[8]{0:T(128)} %get-tuple-element.58) | copy-start | bytes 100 | tf_op jit(solution)/shard_map/cond
  2.3 26.8 %copy-start.4 = (f32[64]{0:T(128)S(1)}, f32[64]{0:T(128)}, u32[]{:S(2)}) copy-start(f32[64]{0:T(128)} %get-tuple-element.44) | copy-start | bytes 772 | tf_op jit(solution)/shard_map/cond
  2.3 28.1 %copy-start.6 = (s32[512]{0:T(512)S(1)}, s32[512]{0:T(512)}, u32[]{:S(2)}) copy-start(s32[512]{0:T(512)} %get-tuple-element.56) | copy-start | bytes 6148 | tf_op jit(solution)/shard_map/cond
  8.4 34.4 %copy-start.10 = (bf16[32,8,4,512]{3,2,1,0:T(4,128)(2,1)S(1)}, bf16[32,8,4,512]{3,2,1,0:T(4,128)(2,1)}, u32[]{:S(2)}) copy-start(bf16[32,8,4,512]{3,2,1,0:T(4,128)(2,1)} %get-tuple-element.203) | copy-start | bytes 3145732 | tf_op jit(solution)/shard_map/cond
  8.4 27.9 %collective-permute-start = (bf16[4,4,8,32,128]{4,3,2,1,0:T(8,128)(2,1)}, bf16[4,4,8,32,128]{4,3,2,1,0:T(8,128)(2,1)S(1)}, u32[]{:S(2)}, u32[]{:S(2)}) collective-permute-start(bf16[4,4,8,32,128]{4,3,2,1,0:T(8,128)(2,1)} %get-tuple-element.62), channel_id=1, source_target_pairs={{0,8},{8,16},{16,24},{24,0},{32,40},{40,48},{48,56},{56,32},{64,72... | collective-permute-start | bytes 3145736 | tf_op jit(solution)/shard_map/cond/branch_0_fun/ppermute | solution.py:172
  10.9 25.3 %collective-permute-start.1 = (bf16[4,4,8,32,128]{4,3,2,1,0:T(8,128)(2,1)}, bf16[4,4,8,32,128]{4,3,2,1,0:T(8,128)(2,1)S(1)}, u32[]{:S(2)}, u32[]{:S(2)}) collective-permute-start(bf16[4,4,8,32,128]{4,3,2,1,0:T(8,128)(2,1)} %get-tuple-element.63), channel_id=1, source_target_pairs={{0,24},{8,0},{16,8},{24,16},{32,56},{40,32},{48,40},{56,48},{64,88... | collective-permute-start | bytes 3145736 | tf_op jit(solution)/shard_map/cond/branch_0_fun/ppermute | solution.py:172
  19.3 48.2 %collective-permute-start.3 = (bf16[4,4,8,32,128]{4,3,2,1,0:T(8,128)(2,1)}, bf16[4,4,8,32,128]{4,3,2,1,0:T(8,128)(2,1)}, u32[]{:S(2)}, u32[]{:S(2)}) collective-permute-start(bf16[4,4,8,32,128]{4,3,2,1,0:T(8,128)(2,1)} %get-tuple-element.76), channel_id=1, source_target_pairs={{0,32},{8,40},{16,48},{24,56},{32,64},{40,72},{48,80},{56,88},{64,... | collective-permute-start | bytes 3145736 | tf_op jit(solution)/shard_map/cond/branch_0_fun/ppermute | solution.py:172
  20.6 47.5 %collective-permute-start.4 = (bf16[4,4,8,32,128]{4,3,2,1,0:T(8,128)(2,1)}, bf16[4,4,8,32,128]{4,3,2,1,0:T(8,128)(2,1)}, u32[]{:S(2)}, u32[]{:S(2)}) collective-permute-start(bf16[4,4,8,32,128]{4,3,2,1,0:T(8,128)(2,1)} %get-tuple-element.77), channel_id=1, source_target_pairs={{0,64},{8,72},{16,80},{24,88},{32,96},{40,104},{48,112},{56,120},{... | collective-permute-start | bytes 3145736 | tf_op jit(solution)/shard_map/cond/branch_0_fun/ppermute | solution.py:172
  23.0 45.0 %collective-permute-start.5 = (bf16[4,4,8,32,128]{4,3,2,1,0:T(8,128)(2,1)}, bf16[4,4,8,32,128]{4,3,2,1,0:T(8,128)(2,1)}, u32[]{:S(2)}, u32[]{:S(2)}) collective-permute-start(bf16[4,4,8,32,128]{4,3,2,1,0:T(8,128)(2,1)} %get-tuple-element.78), channel_id=1, source_target_pairs={{0,96},{8,104},{16,112},{24,120},{32,0},{40,8},{48,16},{56,24},{64... | collective-permute-start | bytes 3145736 | tf_op jit(solution)/shard_map/cond/branch_0_fun/ppermute | solution.py:172
  29.8 2.5 %copy-start.31 = (s32[2]{0:T(128)}, s32[2]{0:T(128)S(1)}, u32[]{:S(2)}) copy-start(s32[2]{0:T(128)S(1)} %broadcast_select_fusion.5) | copy-start | bytes 28 | tf_op jit(solution)/shard_map/cond
  36.2 17.5 %copy-start.12 = (bf16[4,4,8,32,128]{4,3,2,1,0:T(8,128)(2,1)}, bf16[4,4,8,32,128]{4,3,2,1,0:T(8,128)(2,1)S(1)}, u32[]{:S(2)}) copy-start(bf16[4,4,8,32,128]{4,3,2,1,0:T(8,128)(2,1)S(1)} %collective-permute-done.refs_1_) | copy-start | bytes 3145732 | tf_op jit(solution)/shard_map/cond
  36.2 3.9 %copy-start.13 = (bf16[4,4,8,32,128]{4,3,2,1,0:T(8,128)(2,1)}, bf16[4,4,8,32,128]{4,3,2,1,0:T(8,128)(2,1)S(1)}, u32[]{:S(2)}) copy-start(bf16[4,4,8,32,128]{4,3,2,1,0:T(8,128)(2,1)S(1)} %collective-permute-done.1.refs_3_) | copy-start | bytes 3145732 | tf_op jit(solution)/shard_map/cond
  36.2 27.6 %collective-permute-start.2 = (bf16[4,4,8,32,128]{4,3,2,1,0:T(8,128)(2,1)}, bf16[4,4,8,32,128]{4,3,2,1,0:T(8,128)(2,1)}, u32[]{:S(2)}, u32[]{:S(2)}) collective-permute-start(bf16[4,4,8,32,128]{4,3,2,1,0:T(8,128)(2,1)} %get-tuple-element.70), channel_id=1, source_target_pairs={{0,16},{8,24},{16,0},{24,8},{32,48},{40,56},{48,32},{56,40},{64,80... | collective-permute-start | bytes 3145736 | tf_op jit(solution)/shard_map/cond/branch_0_fun/ppermute | solution.py:172
  53.8 10.0 %copy-start = (f32[32,32,512]{2,1,0:T(8,128)}, f32[32,32,512]{2,1,0:T(8,128)S(1)}, u32[]{:S(2)}) copy-start(f32[32,32,512]{2,1,0:T(8,128)S(1)} %cycle_term.2.refs_12_) | copy-start | bytes 6291460 | tf_op jit(solution)/shard_map/cond
  63.8 14.1 %copy-start.8 = (f32[512]{0:T(512)S(1)}, f32[512]{0:T(512)}, u32[]{:S(2)}) copy-start(f32[512]{0:T(512)} %get-tuple-element.91) | copy-start | bytes 6148 | tf_op jit(solution)/shard_map/cond
  63.8 16.6 %copy-start.29 = (s32[1,32]{1,0:T(1,128)S(1)}, s32[1,32]{1,0:T(1,128)}, u32[]{:S(2)}) copy-start(s32[1,32]{1,0:T(1,128)} %get-tuple-element.246) | copy-start | bytes 388 | tf_op jit(solution)/shard_map/cond
  63.8 16.6 %copy-start.30 = (s32[1,32]{1,0:T(1,128)S(1)}, s32[1,32]{1,0:T(1,128)}, u32[]{:S(2)}) copy-start(s32[1,32]{1,0:T(1,128)} %get-tuple-element.247) | copy-start | bytes 388 | tf_op jit(solution)/shard_map/cond
  67.4 27.8 %copy-start.32 = (s32[2]{0:T(128)S(1)}, s32[2]{0:T(128)}, u32[]{:S(2)}) copy-start(s32[2]{0:T(128)} %copy-done.31) | copy-start | bytes 28 | tf_op jit(solution)/shard_map/cond
  67.4 27.9 %copy-start.33 = (f32[2]{0:T(128)S(1)}, f32[2]{0:T(128)}, u32[]{:S(2)}) copy-start(f32[2]{0:T(128)} %broadcast_select_fusion.3) | copy-start | bytes 28 | tf_op jit(solution)/shard_map/cond
  67.4 27.9 %copy-start.37 = (pred[8,32]{1,0:T(8,128)(4,1)S(1)}, pred[8,32]{1,0:T(8,128)(4,1)}, u32[]{:S(2)}) copy-start(pred[8,32]{1,0:T(8,128)(4,1)} %iota_compare_fusion.5) | copy-start | bytes 772 | tf_op jit(solution)/shard_map/cond
  67.4 27.9 %copy-start.38 = (pred[8,32]{1,0:T(8,128)(4,1)S(1)}, pred[8,32]{1,0:T(8,128)(4,1)}, u32[]{:S(2)}) copy-start(pred[8,32]{1,0:T(8,128)(4,1)} %iota_compare_fusion.6) | copy-start | bytes 772 | tf_op jit(solution)/shard_map/cond
  68.1 20.0 %collective-permute-start.8 = (bf16[12,8,32,128]{3,2,1,0:T(8,128)(2,1)}, bf16[12,8,32,128]{3,2,1,0:T(8,128)(2,1)S(1)}, u32[]{:S(2)}, u32[]{:S(2)}) collective-permute-start(bf16[12,8,32,128]{3,2,1,0:T(8,128)(2,1)} %get-tuple-element.86), channel_id=1, source_target_pairs={{0,32},{8,40},{16,48},{24,56},{32,64},{40,72},{48,80},{56,88},{64,... | collective-permute-start | bytes 2359304 | tf_op jit(solution)/shard_map/cond/branch_0_fun/ppermute | solution.py:172
  69.7 18.3 %collective-permute-start.9 = (bf16[12,8,32,128]{3,2,1,0:T(8,128)(2,1)}, bf16[12,8,32,128]{3,2,1,0:T(8,128)(2,1)S(1)}, u32[]{:S(2)}, u32[]{:S(2)}) collective-permute-start(bf16[12,8,32,128]{3,2,1,0:T(8,128)(2,1)} %get-tuple-element.87), channel_id=1, source_target_pairs={{0,96},{8,104},{16,112},{24,120},{32,0},{40,8},{48,16},{56,24},{64... | collective-permute-start | bytes 2359304 | tf_op jit(solution)/shard_map/cond/branch_0_fun/ppermute | solution.py:172
  74.9 18.8 %collective-permute-start.6 = (bf16[12,8,32,128]{3,2,1,0:T(8,128)(2,1)}, bf16[12,8,32,128]{3,2,1,0:T(8,128)(2,1)S(1)}, u32[]{:S(2)}, u32[]{:S(2)}) collective-permute-start(bf16[12,8,32,128]{3,2,1,0:T(8,128)(2,1)} %get-tuple-element.79), channel_id=1, source_target_pairs={{0,8},{8,16},{16,24},{24,0},{32,40},{40,48},{48,56},{56,32},{64,72... | collective-permute-start | bytes 2359304 | tf_op jit(solution)/shard_map/cond/branch_0_fun/ppermute | solution.py:172
  75.1 18.7 %collective-permute-start.7 = (bf16[12,8,32,128]{3,2,1,0:T(8,128)(2,1)}, bf16[12,8,32,128]{3,2,1,0:T(8,128)(2,1)}, u32[]{:S(2)}, u32[]{:S(2)}) collective-permute-start(bf16[12,8,32,128]{3,2,1,0:T(8,128)(2,1)} %get-tuple-element.80), channel_id=1, source_target_pairs={{0,24},{8,0},{16,8},{24,16},{32,56},{40,32},{48,40},{56,48},{64,88... | collective-permute-start | bytes 2359304 | tf_op jit(solution)/shard_map/cond/branch_0_fun/ppermute | solution.py:172
  88.0 17.4 %copy-start.18 = (bf16[12,8,32,128]{3,2,1,0:T(8,128)(2,1)}, bf16[12,8,32,128]{3,2,1,0:T(8,128)(2,1)S(1)}, u32[]{:S(2)}) copy-start(bf16[12,8,32,128]{3,2,1,0:T(8,128)(2,1)S(1)} %collective-permute-done.8.refs_5_) | copy-start | bytes 2359300 | tf_op jit(solution)/shard_map/cond
  88.0 17.4 %copy-start.19 = (bf16[12,8,32,128]{3,2,1,0:T(8,128)(2,1)}, bf16[12,8,32,128]{3,2,1,0:T(8,128)(2,1)S(1)}, u32[]{:S(2)}) copy-start(bf16[12,8,32,128]{3,2,1,0:T(8,128)(2,1)S(1)} %collective-permute-done.9.refs_7_) | copy-start | bytes 2359300 | tf_op jit(solution)/shard_map/cond
  88.0 18.7 %collective-permute-start.11 = (bf16[12,8,32,128]{3,2,1,0:T(8,128)(2,1)}, bf16[12,8,32,128]{3,2,1,0:T(8,128)(2,1)S(1)}, u32[]{:S(2)}, u32[]{:S(2)}) collective-permute-start(bf16[12,8,32,128]{3,2,1,0:T(8,128)(2,1)} %get-tuple-element.88), channel_id=1, source_target_pairs={{0,64},{8,72},{16,80},{24,88},{32,96},{40,104},{48,112},{56,120},{... | collective-permute-start | bytes 2359304 | tf_op jit(solution)/shard_map/cond/branch_0_fun/ppermute | solution.py:172
  93.7 11.7 %copy-start.20 = (bf16[12,8,32,128]{3,2,1,0:T(8,128)(2,1)}, bf16[12,8,32,128]{3,2,1,0:T(8,128)(2,1)S(1)}, u32[]{:S(2)}) copy-start(bf16[12,8,32,128]{3,2,1,0:T(8,128)(2,1)S(1)} %collective-permute-done.6.refs_1_) | copy-start | bytes 2359300 | tf_op jit(solution)/shard_map/cond
  93.7 18.1 %collective-permute-start.10 = (bf16[12,8,32,128]{3,2,1,0:T(8,128)(2,1)}, bf16[12,8,32,128]{3,2,1,0:T(8,128)(2,1)S(1)}, u32[]{:S(2)}, u32[]{:S(2)}) collective-permute-start(bf16[12,8,32,128]{3,2,1,0:T(8,128)(2,1)} %get-tuple-element.89), channel_id=1, source_target_pairs={{0,16},{8,24},{16,0},{24,8},{32,48},{40,56},{48,32},{56,40},{64,80... | collective-permute-start | bytes 2359304 | tf_op jit(solution)/shard_map/cond/branch_0_fun/ppermute | solution.py:172
  106.7 5.1 %copy-start.21 = (bf16[12,8,32,128]{3,2,1,0:T(8,128)(2,1)}, bf16[12,8,32,128]{3,2,1,0:T(8,128)(2,1)S(1)}, u32[]{:S(2)}) copy-start(bf16[12,8,32,128]{3,2,1,0:T(8,128)(2,1)S(1)} %collective-permute-done.11.refs_6_) | copy-start | bytes 2359300 | tf_op jit(solution)/shard_map/cond
  111.8 0.9 copy-start.22
  126.8 5.9 %collective-permute-start.12 = (f32[16,32,512]{2,1,0:T(8,128)S(1)}, f32[16,32,512]{2,1,0:T(8,128)S(1)}, u32[]{:S(2)}, u32[]{:S(2)}) collective-permute-start(f32[16,32,512]{2,1,0:T(8,128)S(1)} %get-tuple-element.94), channel_id=1, source_target_pairs={{0,1},{1,0},{2,3},{3,2},{4,5},{5,4},{6,7},{7,6},{8,9},{9,8},{10,11... | collective-permute-start | bytes 3145736 | tf_op jit(solution)/shard_map/cond/branch_0_fun/ppermute | solution.py:568

commit v5 on v4

--- a/solution.py
+++ b/solution.py
@@ -115,7 +115,7 @@
 
 
 def regroup_kernel(count, rels, tab_ref, *refs):
-    got, outs, (buf_ref, sems, out_sems) = refs[:4], refs[4:6], refs[6:]
+    got, outs, (buf_ref, sems, out_sems) = refs[:4], refs[4:-3], refs[-3:]
 
     def copy(n, away, at):
         src = got[away].at[(tab_ref[2, n] + rels[at]) & 3, tab_ref[1, n]]
@@ -129,13 +129,13 @@
 
             @pl.when(tab_ref[0, n] == away)
             def _():
-                for at in range(2):
+                for at in range(len(rels)):
                     copy(n, away, at).start()
 
         return carry
 
     lax.fori_loop(0, count, start, 0)
-    for at in range(2):
+    for at in range(len(rels)):
 
         def arrive(n, carry):
             copy(n, 0, at).wait()
@@ -143,7 +143,7 @@
 
         lax.fori_loop(0, count, arrive, 0)
         ship(at).start()
-    for at in range(2):
+    for at in range(len(rels)):
         ship(at).wait()
 
 
@@ -153,12 +153,12 @@
     return pl.pallas_call(
         functools.partial(regroup_kernel, count, rels),
         in_specs=[pl.BlockSpec(memory_space=pltpu.SMEM)] + [hbm] * 4,
-        out_specs=[hbm] * 2,
-        out_shape=[pltpu.HBM((count, QP, OJ, 128), BF16)] * 2,
+        out_specs=[hbm] * len(rels),
+        out_shape=[pltpu.HBM((count, QP, OJ, 128), BF16)] * len(rels),
         scratch_shapes=[
-            pltpu.VMEM((2, count, QP, OJ, 128), BF16),
-            pltpu.SemaphoreType.DMA((2, count)),
-            pltpu.SemaphoreType.DMA((2,)),
+            pltpu.VMEM((len(rels), count, QP, OJ, 128), BF16),
+            pltpu.SemaphoreType.DMA((len(rels), count)),
+            pltpu.SemaphoreType.DMA((len(rels),)),
         ],
         compiler_params=pltpu.CompilerParams(vmem_limit_bytes=VMEM),
         cost_estimate=cost(0, 8 * count * 2**15),
@@ -540,23 +540,21 @@
     cyc = cycle_term(ovov_ints.reshape(OI * SA, 4 * NV), amp_t, want, sym_lanes)
     (gate,) = after([gtab], cyc)
     early = arrange_ints(0, 1, gate, ints, pltpu.HBM)
-    (tab1,) = after([tabs[1]], early, pick)
+    (tab1,) = after([tabs[1]], early, pick, *tail)
     lines1 = [sent[1][0], second[1], second[2], second[3]]
     sides1 = regroup(tab1, lines1, 1, 3)
     (tab0,) = after([tabs[0]], sides1)
     lines0 = [sent[0][0], first[1], first[2], first[3]]
-    sides0 = regroup(tab0, lines0, 1, 3)
-    arrived0 = {n: move(x, n, False) for n, x in zip((1, 3), sides0)}
+    sides0 = regroup(tab0, lines0, 1, 3, 2)
+    arrived0 = {n: move(x, n, False) for n, x in zip((1, 3, 2), sides0)}
     sides1 = after(sides1, first[1], first[2], first[3])
     arrived1 = {n: move(x, n, True) for n, x in zip((1, 3), sides1)}
     rest1, rest0 = after([tab1, tab0], sides0)
     across1, arrived1[0] = regroup(rest1, lines1, 2, 0)
-    across0, arrived0[0] = regroup(rest0, lines0, 2, 0)
+    (arrived0[0],) = regroup(rest0, lines0, 0)
     (across1,) = after([across1], arrived1[1], arrived1[3])
-    (across0,) = after([across0], arrived0[1], arrived0[3], across1)
-    (gate,) = after([gtab], across0, *tail)
+    (gate,) = after([gtab], across1, arrived0[0], *tail)
     arrived1[2] = move(across1, 2, True)
-    arrived0[2] = move(across0, 2, False)
     late = arrange_ints(1, 1, gate, ints, pltpu.HBM)
     keep, give = ladder(
         jnp.concatenate(where),

time: 169 us -> 167 us (0.988)
  waiting for transfers between devices: 13.6 us -> 17 us
  other arithmetic: 10.1 us -> 6.77 us
    ppermute x12, waiting for transfers between devices: 11.3 us -> 14.7 us  [move(): return lax.ppermute(x, 'row', pairs)]
  transfers between devices with their start and end apart: 13 -> 13, of which waited for: 7 -> 6; matrix products, arithmetic and copies ran while one was open for 14% -> 11% of each run, Pallas kernels for 28% -> 28%
where the time goes in v5:
time: 167 us; the launch traced here: 166 us
  Pallas kernels  69.5 us (42%)
  blocking collectives  31.8 us (19%)
  starting transfers between devices  25.7 us (15%)
  waiting for transfers between devices  17 us (10%)
  local copies, waits for them, and re-layouts  14.1 us (8%)
  other arithmetic  6.77 us (4%)
    ppermute x12, starting transfers between devices, move(): return lax.ppermute(x, 'row', pairs)  21.2 us
    all_to_all x1, blocking collectives, body(): lax.all_to_all(keep + got, 'row', split_axis=0, concat_axis=0, tiled=True)  20.2 us
    pallas_call x2, Pallas kernels, arrange_ints(): pl.pallas_call(ints_kernel, grid_spec=pltpu.PrefetchScalarGridSpec(num_sc...  20 us
    ppermute x12, waiting for transfers between devices, move(): return lax.ppermute(x, 'row', pairs)  14.7 us
    pallas_call x4, Pallas kernels, regroup(): pl.pallas_call(functools.partial(regroup_kernel, count, rels), in_specs=[...  14.1 us
    pallas_call x1, Pallas kernels, ladder(): pl.pallas_call(ladder_kernel, in_specs=[smem] * 2 + [hbm] * 13, out_specs...  14.1 us
    pallas_call x2, Pallas kernels, pack(): pl.pallas_call(functools.partial(pack_kernel, piece, slots), in_specs=[pl...  12.3 us
    all_to_all x1, blocking collectives, body(): lax.all_to_all(by_run(ltab, both, spread), 'col', split_axis=0, concat_ax...  11.6 us
  transfers between devices with their start and end apart: 13, of which 6 were waited for; matrix products, arithmetic and copies ran while one was open for 11% of the time, Pallas kernels for 28%

profile of v5, /device:TPU:1, one launch (start us, length us, event | category | flops | bytes accessed | tf_op | source)
XLA Modules:
  0.0 166.1 jit_solution(6774155792141758947)
XLA Ops:
  0.0 0.7 fusion.38
  0.8 0.6 reduce_max.9
  2.1 163.9 %conditional.1 = (f32[2,32,8,64]{3,2,1,0:T(8,128)}) conditional(s32[]{:T(128)} %convert_element_type.35, (s32[32]{0:T(128)}, s32[32]{0:T(128)}, s32[64]{0:T(128)}, f32[64]{0:T(128)}, s32[512]{0:T(512)}, /*index=5*/s32[8]{0:T(128)}, bf16[32,8,4,512]{3,2,1,0:T(4,128)(2,1)}, bf16[4,32,512,64]{2,3,1,0:T(8,128)(2,1)}, ...), branch_computations={%region_2.19_spmd, %region_13.30_spmd} | conditional | flops 901215 | bytes 95621288 | solution.py:575
  2.3 6.1 %pack.4 = (bf16[4,4,8,32,128]{4,3,2,1,0:T(8,128)(2,1)}, bf16[4,4,8,32,128]{4,3,2,1,0:T(8,128)(2,1)}, bf16[4,4,8,32,128]{4,3,2,1,0:T(8,128)(2,1)}, bf16[4,4,8,32,128]{4,3,2,1,0:T(8,128)(2,1)}) custom-call(s32[6]{0:T(128)S(1)} %pad_add_fusion.1.tab_ref, bf16[4,32,64,512]{3,2,1,0:T(8,128)(2,1)} %bitcast.96), custom_call_target="tpu_custom_call" | custom-call | bytes 1024 | tf_op jit(solution)/shard_map/cond/branch_0_fun/pack/pallas_call | solution.py:98
  8.4 2.5 %collective-permute-start = (bf16[4,4,8,32,128]{4,3,2,1,0:T(8,128)(2,1)}, bf16[4,4,8,32,128]{4,3,2,1,0:T(8,128)(2,1)}, u32[]{:S(2)}, u32[]{:S(2)}) collective-permute-start(bf16[4,4,8,32,128]{4,3,2,1,0:T(8,128)(2,1)} %get-tuple-element.62), channel_id=1, source_target_pairs={{0,8},{8,16},{16,24},{24,0},{32,40},{40,48},{48,56},{56,32},{64,72... | collective-permute-start | bytes 3145736 | tf_op jit(solution)/shard_map/cond/branch_0_fun/ppermute | solution.py:172
  11.0 2.2 %collective-permute-start.1 = (bf16[4,4,8,32,128]{4,3,2,1,0:T(8,128)(2,1)}, bf16[4,4,8,32,128]{4,3,2,1,0:T(8,128)(2,1)}, u32[]{:S(2)}, u32[]{:S(2)}) collective-permute-start(bf16[4,4,8,32,128]{4,3,2,1,0:T(8,128)(2,1)} %get-tuple-element.63), channel_id=1, source_target_pairs={{0,24},{8,0},{16,8},{24,16},{32,56},{40,32},{48,40},{56,48},{64,88... | collective-permute-start | bytes 3145736 | tf_op jit(solution)/shard_map/cond/branch_0_fun/ppermute | solution.py:172
  13.2 6.2 %pack.5 = (bf16[4,4,8,32,128]{4,3,2,1,0:T(8,128)(2,1)}, bf16[4,4,8,32,128]{4,3,2,1,0:T(8,128)(2,1)}, bf16[4,4,8,32,128]{4,3,2,1,0:T(8,128)(2,1)}, bf16[4,4,8,32,128]{4,3,2,1,0:T(8,128)(2,1)}) custom-call(s32[6]{0:T(128)S(1)} %pad_add_fusion.1.tab_ref, bf16[4,32,64,512]{3,2,1,0:T(8,128)(2,1)} %bitcast.97), custom_call_target="tpu_custom_call" | custom-call | bytes 1024 | tf_op jit(solution)/shard_map/cond/branch_0_fun/pack/pallas_call | solution.py:98
  19.4 1.3 collective-permute-start.3
  20.6 2.4 %collective-permute-start.4 = (bf16[4,4,8,32,128]{4,3,2,1,0:T(8,128)(2,1)}, bf16[4,4,8,32,128]{4,3,2,1,0:T(8,128)(2,1)}, u32[]{:S(2)}, u32[]{:S(2)}) collective-permute-start(bf16[4,4,8,32,128]{4,3,2,1,0:T(8,128)(2,1)} %get-tuple-element.78), channel_id=1, source_target_pairs={{0,64},{8,72},{16,80},{24,88},{32,96},{40,104},{48,112},{56,120},{... | collective-permute-start | bytes 3145736 | tf_op jit(solution)/shard_map/cond/branch_0_fun/ppermute | solution.py:172
  23.1 1.2 collective-permute-start.5
  24.8 0.6 gather_fusion.6
  25.4 0.7 gather_fusion.4
  26.2 0.6 gather_fusion.2
  26.8 0.6 gather_fusion
  27.5 0.7 gather_fusion.5
  28.2 1.2 gather_fusion.3
  29.4 0.7 gather_fusion.1
  31.1 0.6 broadcast_xor_fusion.3
  33.1 0.7 and.324
  33.8 1.3 and.325
  35.6 1.3 copy.55
  37.8 0.6 broadcast_select_fusion.2
  38.7 1.3 collective-permute-start.2
  40.4 0.8 xor_xor_fusion.want_ref
  41.1 0.9 and_convert_fusion
  42.1 6.7 %cycle_term.2.refs_12_ = f32[32,32,512]{2,1,0:T(8,128)S(1)} custom-call(bf16[256,2048]{1,0:T(8,128)(2,1)} %bitcast.106, bf16[4,32,64,512]{3,2,1,0:T(8,128)(2,1)} %bitcast.98, s32[32,32,1]{2,1,0:T(8,128)S(1)} %xor_xor_fusion.want_ref, s32[8,512]{1,0:T(8,128)S(1)} %broadcast_in_dim.169.sym_ref), custom_call_target="tpu_custom_call" | custom-call | bytes 1024 | tf_op jit(solution)/shard_map/cond/branch_0_fun/cycle_term/pallas_call | solution.py:366
  48.8 10.1 %arrange_ints.4.refs_8_ = bf16[1,8,1024,512]{3,2,1,0:T(8,128)(2,1)} custom-call(s32[8,8]{1,0:T(8,128)S(1)} %get-tuple-element.90.gtab_ref, bf16[32,512,512]{2,1,0:T(8,128)(2,1)} %bitcast.102), custom_call_target="tpu_custom_call" | custom-call | bytes 1024 | tf_op jit(solution)/shard_map/cond/branch_0_fun/arrange_ints/pallas_call | solution.py:196
  58.9 4.5 %collective-permute-done.2.refs_2_ = bf16[4,4,8,32,128]{4,3,2,1,0:T(8,128)(2,1)S(1)} collective-permute-done((bf16[4,4,8,32,128]{4,3,2,1,0:T(8,128)(2,1)}, bf16[4,4,8,32,128]{4,3,2,1,0:T(8,128)(2,1)S(1)}, u32[]{:S(2)}, u32[]{:S(2)}) %collective-permute-start.2) | collective-permute-done | bytes 1048608 | tf_op jit(solution)/shard_map/cond/branch_0_fun/ppermute | solution.py:172
  63.5 1.0 copy-done.14
  64.4 3.6 %regroup.8 = (bf16[12,8,32,128]{3,2,1,0:T(8,128)(2,1)}, bf16[12,8,32,128]{3,2,1,0:T(8,128)(2,1)}) custom-call(s32[3,12]{1,0:T(4,128)S(1)} %add_add_fusion.tab_ref, bf16[4,4,8,32,128]{4,3,2,1,0:T(8,128)(2,1)} %get-tuple-element.69.refs_0_, bf16[4,4,8,32,128]{4,3,2,1,0:T(8,128)(2,1)} %collective-permute-done.refs_1_, bf16[4,4,8,32,128]{4,3,2,1,0:T(8,128)(2,1)} %copy-done.14, ...), custom_call_target="tpu_custom_call" | custom-call | bytes 1024 | tf_op jit(solution)/shard_map/cond/branch_0_fun/regroup/pallas_call | solution.py:153
  68.1 1.7 %collective-permute-start.9 = (bf16[12,8,32,128]{3,2,1,0:T(8,128)(2,1)}, bf16[12,8,32,128]{3,2,1,0:T(8,128)(2,1)S(1)}, u32[]{:S(2)}, u32[]{:S(2)}) collective-permute-start(bf16[12,8,32,128]{3,2,1,0:T(8,128)(2,1)} %get-tuple-element.86), channel_id=1, source_target_pairs={{0,32},{8,40},{16,48},{24,56},{32,64},{40,72},{48,80},{56,88},{64,... | collective-permute-start | bytes 2359304 | tf_op jit(solution)/shard_map/cond/branch_0_fun/ppermute | solution.py:172
  69.8 1.7 %collective-permute-start.10 = (bf16[12,8,32,128]{3,2,1,0:T(8,128)(2,1)}, bf16[12,8,32,128]{3,2,1,0:T(8,128)(2,1)S(1)}, u32[]{:S(2)}, u32[]{:S(2)}) collective-permute-start(bf16[12,8,32,128]{3,2,1,0:T(8,128)(2,1)} %get-tuple-element.88), channel_id=1, source_target_pairs={{0,96},{8,104},{16,112},{24,120},{32,0},{40,8},{48,16},{56,24},{64... | collective-permute-start | bytes 2359304 | tf_op jit(solution)/shard_map/cond/branch_0_fun/ppermute | solution.py:172
  71.6 4.2 %regroup.9 = (bf16[12,8,32,128]{3,2,1,0:T(8,128)(2,1)}, bf16[12,8,32,128]{3,2,1,0:T(8,128)(2,1)}, bf16[12,8,32,128]{3,2,1,0:T(8,128)(2,1)}) custom-call(s32[3,12]{1,0:T(4,128)S(1)} %add_add_fusion.1.tab_ref, bf16[4,4,8,32,128]{4,3,2,1,0:T(8,128)(2,1)} %get-tuple-element.76.refs_0_, bf16[4,4,8,32,128]{4,3,2,1,0:T(8,128)(2,1)} %copy-done.13, ...), custom_call_target="tpu_custom_call" | custom-call | bytes 1024 | tf_op jit(solution)/shard_map/cond/branch_0_fun/regroup/pallas_call | solution.py:153
  76.1 2.7 %collective-permute-start.8 = (bf16[12,8,32,128]{3,2,1,0:T(8,128)(2,1)}, bf16[12,8,32,128]{3,2,1,0:T(8,128)(2,1)}, u32[]{:S(2)}, u32[]{:S(2)}) collective-permute-start(bf16[12,8,32,128]{3,2,1,0:T(8,128)(2,1)} %get-tuple-element.81), channel_id=1, source_target_pairs={{0,24},{8,0},{16,8},{24,16},{32,56},{40,32},{48,40},{56,48},{64,88... | collective-permute-start | bytes 2359304 | tf_op jit(solution)/shard_map/cond/branch_0_fun/ppermute | solution.py:172
  79.1 3.5 %regroup.11 = (bf16[12,8,32,128]{3,2,1,0:T(8,128)(2,1)}, bf16[12,8,32,128]{3,2,1,0:T(8,128)(2,1)}) custom-call(s32[3,12]{1,0:T(4,128)S(1)} %add_add_fusion.tab_ref, bf16[4,4,8,32,128]{4,3,2,1,0:T(8,128)(2,1)} %get-tuple-element.69.refs_0_, bf16[4,4,8,32,128]{4,3,2,1,0:T(8,128)(2,1)} %collective-permute-done.refs_1_, bf16[4,4,8,32,128]{4,3,2,1,0:T(8,128)(2,1)} %copy-done.14, ...), custom_call_target="tpu_custom_call" | custom-call | bytes 1024 | tf_op jit(solution)/shard_map/cond/branch_0_fun/regroup/pallas_call | solution.py:153
  82.7 4.6 %collective-permute-done.9.refs_5_ = bf16[12,8,32,128]{3,2,1,0:T(8,128)(2,1)S(1)} collective-permute-done((bf16[12,8,32,128]{3,2,1,0:T(8,128)(2,1)}, bf16[12,8,32,128]{3,2,1,0:T(8,128)(2,1)S(1)}, u32[]{:S(2)}, u32[]{:S(2)}) %collective-permute-start.9) | collective-permute-done | bytes 786464 | tf_op jit(solution)/shard_map/cond/branch_0_fun/ppermute | solution.py:172
  87.6 3.6 %collective-permute-start.11 = (bf16[12,8,32,128]{3,2,1,0:T(8,128)(2,1)}, bf16[12,8,32,128]{3,2,1,0:T(8,128)(2,1)}, u32[]{:S(2)}, u32[]{:S(2)}) collective-permute-start(bf16[12,8,32,128]{3,2,1,0:T(8,128)(2,1)} %get-tuple-element.89), channel_id=1, source_target_pairs={{0,64},{8,72},{16,80},{24,88},{32,96},{40,104},{48,112},{56,120},{... | collective-permute-start | bytes 2359304 | tf_op jit(solution)/shard_map/cond/branch_0_fun/ppermute | solution.py:172
  91.4 1.0 copy.49.refs_10_
  92.8 2.8 %regroup.10.refs_0_ = bf16[12,8,32,128]{3,2,1,0:T(8,128)(2,1)} custom-call(s32[3,12]{1,0:T(4,128)S(1)} %add_add_fusion.1.tab_ref, bf16[4,4,8,32,128]{4,3,2,1,0:T(8,128)(2,1)} %get-tuple-element.76.refs_0_, bf16[4,4,8,32,128]{4,3,2,1,0:T(8,128)(2,1)} %copy-done.13, bf16[4,4,8,32,128]{4,3,2,1,0:T(8,128)(2,1)} %collective-permute-done.4.refs_2_, ...), custom_call_target="tpu_custom_call" | custom-call | bytes 1024 | tf_op jit(solution)/shard_map/cond/branch_0_fun/regroup/pallas_call | solution.py:153
  95.6 10.0 %arrange_ints.5.refs_9_ = bf16[1,8,1024,512]{3,2,1,0:T(8,128)(2,1)} custom-call(s32[8,8]{1,0:T(8,128)S(1)} %get-tuple-element.90.gtab_ref, bf16[32,512,512]{2,1,0:T(8,128)(2,1)} %bitcast.103), custom_call_target="tpu_custom_call" | custom-call | bytes 1024 | tf_op jit(solution)/shard_map/cond/branch_0_fun/arrange_ints/pallas_call | solution.py:196
  105.6 5.2 %collective-permute-done.7.refs_2_ = bf16[12,8,32,128]{3,2,1,0:T(8,128)(2,1)} collective-permute-done((bf16[12,8,32,128]{3,2,1,0:T(8,128)(2,1)}, bf16[12,8,32,128]{3,2,1,0:T(8,128)(2,1)}, u32[]{:S(2)}, u32[]{:S(2)}) %collective-permute-start.7) | collective-permute-done | bytes 786464 | tf_op jit(solution)/shard_map/cond/branch_0_fun/ppermute | solution.py:172
  110.8 14.1 %ladder.2 = (f32[16,32,512]{2,1,0:T(8,128)S(1)}, f32[16,32,512]{2,1,0:T(8,128)S(1)}) custom-call(s32[4,32]{1,0:T(4,128)S(1)} %pad_add_fusion.where_ref, s32[1]{0:T(128)} %bitcast.7.core_ref, bf16[12,8,32,128]{3,2,1,0:T(8,128)(2,1)} %regroup.10.refs_0_, bf16[12,8,32,128]{3,2,1,0:T(8,128)(2,1)} %copy-done.20, ...), custom_call_target="tpu_custom_call" | custom-call | bytes 1024 | tf_op jit(solution)/shard_map/cond/branch_0_fun/ladder/pallas_call | solution.py:313
  124.9 4.5 %collective-permute-start.12 = (f32[16,32,512]{2,1,0:T(8,128)S(1)}, f32[16,32,512]{2,1,0:T(8,128)S(1)}, u32[]{:S(2)}, u32[]{:S(2)}) collective-permute-start(f32[16,32,512]{2,1,0:T(8,128)S(1)} %get-tuple-element.92), channel_id=1, source_target_pairs={{0,1},{1,0},{2,3},{3,2},{4,5},{5,4},{6,7},{7,6},{8,9},{9,8},{10,11... | collective-permute-start | bytes 3145736 | tf_op jit(solution)/shard_map/cond/branch_0_fun/ppermute | solution.py:566
  129.4 2.3 %collective-permute-done.12 = f32[16,32,512]{2,1,0:T(8,128)S(1)} collective-permute-done((f32[16,32,512]{2,1,0:T(8,128)S(1)}, f32[16,32,512]{2,1,0:T(8,128)S(1)}, u32[]{:S(2)}, u32[]{:S(2)}) %collective-permute-start.12) | collective-permute-done | bytes 1048608 | tf_op jit(solution)/shard_map/cond/branch_0_fun/ppermute | solution.py:566
  131.9 20.2 %all_to_all.16.x_ref = f32[16,32,512]{2,1,0:T(8,128)S(1)} all-to-all(f32[16,32,512]{2,1,0:T(8,128)S(1)} %add.137), channel_id=1, replica_groups=mesh['row'=16,'col'=8] {'row'}, dimensions={0} | all-to-all | bytes 2097152 | tf_op jit(solution)/shard_map/cond/branch_0_fun/all_to_all | solution.py:567
  152.1 0.8 by_run.2
  153.0 11.6 %all_to_all.17.x_ref = f32[8,8,512]{2,1,0:T(8,128)S(1)} all-to-all(f32[8,8,512]{2,1,0:T(8,128)S(1)} %by_run.2), channel_id=1, replica_groups=mesh['row'=16,'col'=8] {'col'}, dimensions={0} | all-to-all | bytes 262144 | tf_op jit(solution)/shard_map/cond/branch_0_fun/all_to_all | solution.py:568
  164.6 1.5 finish.2
  (112 shorter events, 7.2 us)
Async XLA Ops:
  2.3 22.0 %copy-start.21 = (s32[32]{0:T(128)S(1)}, s32[32]{0:T(128)}, u32[]{:S(2)}) copy-start(s32[32]{0:T(128)} %get-tuple-element.42) | copy-start | bytes 388 | tf_op jit(solution)/shard_map/cond
  2.3 22.4 %copy-start.8 = (f32[512]{0:T(512)S(1)}, f32[512]{0:T(512)}, u32[]{:S(2)}) copy-start(f32[512]{0:T(512)} %get-tuple-element.67) | copy-start | bytes 6148 | tf_op jit(solution)/shard_map/cond
  2.3 22.4 %copy-start.6 = (s32[512]{0:T(512)S(1)}, s32[512]{0:T(512)}, u32[]{:S(2)}) copy-start(s32[512]{0:T(512)} %get-tuple-element.56) | copy-start | bytes 6148 | tf_op jit(solution)/shard_map/cond
  2.3 22.5 %copy-start.25 = (s32[8]{0:T(128)S(1)}, s32[8]{0:T(128)}, u32[]{:S(2)}) copy-start(s32[8]{0:T(128)} %get-tuple-element.58) | copy-start | bytes 100 | tf_op jit(solution)/shard_map/cond
  2.3 23.9 %copy-start.4 = (f32[64]{0:T(128)S(1)}, f32[64]{0:T(128)}, u32[]{:S(2)}) copy-start(f32[64]{0:T(128)} %get-tuple-element.44) | copy-start | bytes 772 | tf_op jit(solution)/shard_map/cond
  2.3 24.5 %copy-start.2 = (s32[64]{0:T(128)S(1)}, s32[64]{0:T(128)}, u32[]{:S(2)}) copy-start(s32[64]{0:T(128)} %get-tuple-element.40) | copy-start | bytes 772 | tf_op jit(solution)/shard_map/cond
  2.3 25.9 %copy-start.23 = (s32[32]{0:T(128)S(1)}, s32[32]{0:T(128)}, u32[]{:S(2)}) copy-start(s32[32]{0:T(128)} %get-tuple-element.22) | copy-start | bytes 388 | tf_op jit(solution)/shard_map/cond
  8.4 27.2 %copy-start.10 = (bf16[32,8,4,512]{3,2,1,0:T(4,128)(2,1)S(1)}, bf16[32,8,4,512]{3,2,1,0:T(4,128)(2,1)}, u32[]{:S(2)}) copy-start(bf16[32,8,4,512]{3,2,1,0:T(4,128)(2,1)} %get-tuple-element.199) | copy-start | bytes 3145732 | tf_op jit(solution)/shard_map/cond
  8.4 30.3 %collective-permute-start = (bf16[4,4,8,32,128]{4,3,2,1,0:T(8,128)(2,1)}, bf16[4,4,8,32,128]{4,3,2,1,0:T(8,128)(2,1)}, u32[]{:S(2)}, u32[]{:S(2)}) collective-permute-start(bf16[4,4,8,32,128]{4,3,2,1,0:T(8,128)(2,1)} %get-tuple-element.62), channel_id=1, source_target_pairs={{0,8},{8,16},{16,24},{24,0},{32,40},{40,48},{48,56},{56,32},{64,72... | collective-permute-start | bytes 3145736 | tf_op jit(solution)/shard_map/cond/branch_0_fun/ppermute | solution.py:172
  11.0 27.7 %collective-permute-start.1 = (bf16[4,4,8,32,128]{4,3,2,1,0:T(8,128)(2,1)}, bf16[4,4,8,32,128]{4,3,2,1,0:T(8,128)(2,1)}, u32[]{:S(2)}, u32[]{:S(2)}) collective-permute-start(bf16[4,4,8,32,128]{4,3,2,1,0:T(8,128)(2,1)} %get-tuple-element.63), channel_id=1, source_target_pairs={{0,24},{8,0},{16,8},{24,16},{32,56},{40,32},{48,40},{56,48},{64,88... | collective-permute-start | bytes 3145736 | tf_op jit(solution)/shard_map/cond/branch_0_fun/ppermute | solution.py:172
  19.4 48.7 %collective-permute-start.3 = (bf16[4,4,8,32,128]{4,3,2,1,0:T(8,128)(2,1)}, bf16[4,4,8,32,128]{4,3,2,1,0:T(8,128)(2,1)S(1)}, u32[]{:S(2)}, u32[]{:S(2)}) collective-permute-start(bf16[4,4,8,32,128]{4,3,2,1,0:T(8,128)(2,1)} %get-tuple-element.77), channel_id=1, source_target_pairs={{0,32},{8,40},{16,48},{24,56},{32,64},{40,72},{48,80},{56,88},{64,... | collective-permute-start | bytes 3145736 | tf_op jit(solution)/shard_map/cond/branch_0_fun/ppermute | solution.py:172
  20.6 47.5 %collective-permute-start.4 = (bf16[4,4,8,32,128]{4,3,2,1,0:T(8,128)(2,1)}, bf16[4,4,8,32,128]{4,3,2,1,0:T(8,128)(2,1)}, u32[]{:S(2)}, u32[]{:S(2)}) collective-permute-start(bf16[4,4,8,32,128]{4,3,2,1,0:T(8,128)(2,1)} %get-tuple-element.78), channel_id=1, source_target_pairs={{0,64},{8,72},{16,80},{24,88},{32,96},{40,104},{48,112},{56,120},{... | collective-permute-start | bytes 3145736 | tf_op jit(solution)/shard_map/cond/branch_0_fun/ppermute | solution.py:172
  23.1 45.0 %collective-permute-start.5 = (bf16[4,4,8,32,128]{4,3,2,1,0:T(8,128)(2,1)}, bf16[4,4,8,32,128]{4,3,2,1,0:T(8,128)(2,1)}, u32[]{:S(2)}, u32[]{:S(2)}) collective-permute-start(bf16[4,4,8,32,128]{4,3,2,1,0:T(8,128)(2,1)} %get-tuple-element.79), channel_id=1, source_target_pairs={{0,96},{8,104},{16,112},{24,120},{32,0},{40,8},{48,16},{56,24},{64... | collective-permute-start | bytes 3145736 | tf_op jit(solution)/shard_map/cond/branch_0_fun/ppermute | solution.py:172
  38.7 24.8 %collective-permute-start.2 = (bf16[4,4,8,32,128]{4,3,2,1,0:T(8,128)(2,1)}, bf16[4,4,8,32,128]{4,3,2,1,0:T(8,128)(2,1)S(1)}, u32[]{:S(2)}, u32[]{:S(2)}) collective-permute-start(bf16[4,4,8,32,128]{4,3,2,1,0:T(8,128)(2,1)} %get-tuple-element.71), channel_id=1, source_target_pairs={{0,16},{8,24},{16,0},{24,8},{32,48},{40,56},{48,32},{56,40},{64,80... | collective-permute-start | bytes 3145736 | tf_op jit(solution)/shard_map/cond/branch_0_fun/ppermute | solution.py:172
  48.8 10.1 %copy-start = (f32[32,32,512]{2,1,0:T(8,128)}, f32[32,32,512]{2,1,0:T(8,128)S(1)}, u32[]{:S(2)}) copy-start(f32[32,32,512]{2,1,0:T(8,128)S(1)} %cycle_term.2.refs_12_) | copy-start | bytes 6291460 | tf_op jit(solution)/shard_map/cond
  63.4 1.0 copy-start.14
  68.0 3.6 %copy-start.13 = (bf16[4,4,8,32,128]{4,3,2,1,0:T(8,128)(2,1)}, bf16[4,4,8,32,128]{4,3,2,1,0:T(8,128)(2,1)S(1)}, u32[]{:S(2)}) copy-start(bf16[4,4,8,32,128]{4,3,2,1,0:T(8,128)(2,1)S(1)} %collective-permute-done.3.refs_1_) | copy-start | bytes 3145732 | tf_op jit(solution)/shard_map/cond
  68.1 19.2 %collective-permute-start.9 = (bf16[12,8,32,128]{3,2,1,0:T(8,128)(2,1)}, bf16[12,8,32,128]{3,2,1,0:T(8,128)(2,1)S(1)}, u32[]{:S(2)}, u32[]{:S(2)}) collective-permute-start(bf16[12,8,32,128]{3,2,1,0:T(8,128)(2,1)} %get-tuple-element.86), channel_id=1, source_target_pairs={{0,32},{8,40},{16,48},{24,56},{32,64},{40,72},{48,80},{56,88},{64,... | collective-permute-start | bytes 2359304 | tf_op jit(solution)/shard_map/cond/branch_0_fun/ppermute | solution.py:172
  69.8 17.8 %collective-permute-start.10 = (bf16[12,8,32,128]{3,2,1,0:T(8,128)(2,1)}, bf16[12,8,32,128]{3,2,1,0:T(8,128)(2,1)S(1)}, u32[]{:S(2)}, u32[]{:S(2)}) collective-permute-start(bf16[12,8,32,128]{3,2,1,0:T(8,128)(2,1)} %get-tuple-element.88), channel_id=1, source_target_pairs={{0,96},{8,104},{16,112},{24,120},{32,0},{40,8},{48,16},{56,24},{64... | collective-permute-start | bytes 2359304 | tf_op jit(solution)/shard_map/cond/branch_0_fun/ppermute | solution.py:172
  75.8 29.8 %collective-permute-start.6 = (bf16[12,8,32,128]{3,2,1,0:T(8,128)(2,1)}, bf16[12,8,32,128]{3,2,1,0:T(8,128)(2,1)S(1)}, u32[]{:S(2)}, u32[]{:S(2)}) collective-permute-start(bf16[12,8,32,128]{3,2,1,0:T(8,128)(2,1)} %get-tuple-element.80), channel_id=1, source_target_pairs={{0,8},{8,16},{16,24},{24,0},{32,40},{40,48},{48,56},{56,32},{64,72... | collective-permute-start | bytes 2359304 | tf_op jit(solution)/shard_map/cond/branch_0_fun/ppermute | solution.py:172
  76.1 29.5 %collective-permute-start.8 = (bf16[12,8,32,128]{3,2,1,0:T(8,128)(2,1)}, bf16[12,8,32,128]{3,2,1,0:T(8,128)(2,1)}, u32[]{:S(2)}, u32[]{:S(2)}) collective-permute-start(bf16[12,8,32,128]{3,2,1,0:T(8,128)(2,1)} %get-tuple-element.81), channel_id=1, source_target_pairs={{0,24},{8,0},{16,8},{24,16},{32,56},{40,32},{48,40},{56,48},{64,88... | collective-permute-start | bytes 2359304 | tf_op jit(solution)/shard_map/cond/branch_0_fun/ppermute | solution.py:172
  78.7 32.0 %collective-permute-start.7 = (bf16[12,8,32,128]{3,2,1,0:T(8,128)(2,1)}, bf16[12,8,32,128]{3,2,1,0:T(8,128)(2,1)}, u32[]{:S(2)}, u32[]{:S(2)}) collective-permute-start(bf16[12,8,32,128]{3,2,1,0:T(8,128)(2,1)} %get-tuple-element.82), channel_id=1, source_target_pairs={{0,16},{8,24},{16,0},{24,8},{32,48},{40,56},{48,32},{56,40},{64,80... | collective-permute-start | bytes 2359304 | tf_op jit(solution)/shard_map/cond/branch_0_fun/ppermute | solution.py:172
  87.3 18.3 %copy-start.18 = (bf16[12,8,32,128]{3,2,1,0:T(8,128)(2,1)}, bf16[12,8,32,128]{3,2,1,0:T(8,128)(2,1)S(1)}, u32[]{:S(2)}) copy-start(bf16[12,8,32,128]{3,2,1,0:T(8,128)(2,1)S(1)} %collective-permute-done.9.refs_5_) | copy-start | bytes 2359300 | tf_op jit(solution)/shard_map/cond
  87.6 18.0 %copy-start.19 = (bf16[12,8,32,128]{3,2,1,0:T(8,128)(2,1)}, bf16[12,8,32,128]{3,2,1,0:T(8,128)(2,1)S(1)}, u32[]{:S(2)}) copy-start(bf16[12,8,32,128]{3,2,1,0:T(8,128)(2,1)S(1)} %collective-permute-done.10.refs_7_) | copy-start | bytes 2359300 | tf_op jit(solution)/shard_map/cond
  87.6 23.1 %collective-permute-start.11 = (bf16[12,8,32,128]{3,2,1,0:T(8,128)(2,1)}, bf16[12,8,32,128]{3,2,1,0:T(8,128)(2,1)}, u32[]{:S(2)}, u32[]{:S(2)}) collective-permute-start(bf16[12,8,32,128]{3,2,1,0:T(8,128)(2,1)} %get-tuple-element.89), channel_id=1, source_target_pairs={{0,64},{8,72},{16,80},{24,88},{32,96},{40,104},{48,112},{56,120},{... | collective-permute-start | bytes 2359304 | tf_op jit(solution)/shard_map/cond/branch_0_fun/ppermute | solution.py:172
  105.6 5.2 %copy-start.20 = (bf16[12,8,32,128]{3,2,1,0:T(8,128)(2,1)}, bf16[12,8,32,128]{3,2,1,0:T(8,128)(2,1)S(1)}, u32[]{:S(2)}) copy-start(bf16[12,8,32,128]{3,2,1,0:T(8,128)(2,1)S(1)} %collective-permute-done.6.refs_1_) | copy-start | bytes 2359300 | tf_op jit(solution)/shard_map/cond
  124.9 6.8 %collective-permute-start.12 = (f32[16,32,512]{2,1,0:T(8,128)S(1)}, f32[16,32,512]{2,1,0:T(8,128)S(1)}, u32[]{:S(2)}, u32[]{:S(2)}) collective-permute-start(f32[16,32,512]{2,1,0:T(8,128)S(1)} %get-tuple-element.92), channel_id=1, source_target_pairs={{0,1},{1,0},{2,3},{3,2},{4,5},{5,4},{6,7},{7,6},{8,9},{9,8},{10,11... | collective-permute-start | bytes 3145736 | tf_op jit(solution)/shard_map/cond/branch_0_fun/ppermute | solution.py:566
